TPU v7x, 32 devices: a whole 2x2x4 slice. The times are simulated.
32 devices in a mesh: row: 4 (over z), col: 4 (over x, core), depth: 2 (over y).
Axes of the slice: x: 2, y: 2, z: 4, core: 2. Of those that a mesh axis runs over, the one named last changes fastest.
Arguments:
- x_matrix: bfloat16 [576, 576], P(('row', 'depth'), 'col'), may hold values from -0.25 to 0.25
- tangent: bfloat16 [576, 576], P(('row', 'depth'), 'col'), may hold values from -6 to 6
- fill_x: int32 [5, 5], replicated, may hold values from 0 to 1, as said below
- fill_t: int32 [5, 5], replicated, may hold values from 0 to 1, as said below
Outputs:
- tangent_next: float32 [576, 576], P(('row', 'depth'), 'col')
Inputs may be any that keep to these rules, and one draw needn't show every extreme that they name: `fill_x`: 1 where the block of X is filled, else 0; every diagonal block is filled. `fill_t`: 1 where the block of X' is filled, else 0; every diagonal block is filled.
All inputs are finite; a program needn't handle non-finite values.
Results may differ from a plain program's by a relative error of at most 0.00098.
Values may be sent and summed in bfloat16 or wider, within the bound.
No kernel may reach another device: no remote copies, remote signals or barrier semaphores. Data moves between devices by JAX's collectives and lax.ppermute only.
A program may use at most 64 MiB of HBM per device.

v0:
```python
import jax
import jax.numpy as jnp
from jax import lax
from jax.sharding import PartitionSpec as P

BLOCK = 128


def block_mask(fill, row_start, col_start, rows, cols):
    count = fill.shape[0]
    blocks = lax.iota(jnp.int32, count)
    row_ids = (row_start + lax.iota(jnp.int32, rows)) // BLOCK
    col_ids = (col_start + lax.iota(jnp.int32, cols)) // BLOCK
    row_hot = (row_ids[:, None] == blocks[None, :]).astype(jnp.float32)
    col_hot = (blocks[:, None] == col_ids[None, :]).astype(jnp.float32)
    inner = jnp.dot(row_hot, fill.astype(jnp.float32), precision=lax.Precision.HIGHEST)
    return jnp.dot(inner, col_hot, precision=lax.Precision.HIGHEST)


def left_panels(stacked):
    count, rows, width = stacked.shape
    layers = lax.axis_size("depth")
    columns = lax.axis_size("col")
    tiled = jnp.tile(stacked, (1, 1, columns))
    received = lax.all_to_all(tiled, ("col", "depth"), split_axis=2, concat_axis=1, tiled=True)
    return received.reshape(count, columns, layers, rows, rows)


def right_panels(stacked):
    count, rows, width = stacked.shape
    grid_rows = lax.axis_size("row")
    received = lax.all_gather(stacked, "row", axis=1, tiled=True)
    return received.reshape(count, grid_rows, rows, width)


def partial_rows(left, right, count):
    out = jnp.einsum("cdij,cjk->dik", left, right, preferred_element_type=jnp.float32)
    return out.reshape(count, right.shape[2])


def layer_sum(term_fn, rows):
    return lax.psum_scatter(
        term_fn(jnp.int32(0), lax.axis_size("depth") * rows),
        "depth",
        scatter_dimension=0,
        tiled=True,
    )


def body(x_matrix, tangent, fill_x, fill_t):
    rows, width = x_matrix.shape
    layers = lax.axis_size("depth")
    row_start = (lax.axis_index("row") * layers + lax.axis_index("depth")) * rows
    col_start = lax.axis_index("col") * width
    masked_x = (
        x_matrix.astype(jnp.float32) * block_mask(fill_x, row_start, col_start, rows, width)
    ).astype(jnp.bfloat16)
    masked_t = (
        tangent.astype(jnp.float32) * block_mask(fill_t, row_start, col_start, rows, width)
    ).astype(jnp.bfloat16)
    paired = jnp.stack([masked_x, masked_t])
    lefts = left_panels(paired)
    rights = right_panels(paired)
    left_x = lefts[0]
    left_t = lefts[1]
    right_x = rights[0]
    right_t = rights[1]

    def first_terms(start, count):
        square_term = partial_rows(left_x, right_x, count)
        cross_term = partial_rows(left_t, right_x, count)
        return jnp.concatenate([square_term, cross_term], axis=1)

    firsts = layer_sum(first_terms, rows).astype(jnp.bfloat16)
    square = firsts[:, :width]
    cross = firsts[:, width:]
    left_square = left_panels(square[None])[0]
    seconds = right_panels(jnp.stack([square, cross]))
    right_square = seconds[0]
    right_cross = seconds[1]

    def last_terms(start, count):
        total = partial_rows(left_t, right_square, count)
        total = total + partial_rows(left_x, right_cross, count)
        return total + partial_rows(left_square, right_t, count)

    summed = layer_sum(last_terms, rows)
    return 1.5 * masked_t.astype(jnp.float32) - 0.5 * summed


def solution(mesh):
    placed = (P(("row", "depth"), "col"), P(("row", "depth"), "col"), P(), P())
    return jax.shard_map(
        body, mesh=mesh, in_specs=placed, out_specs=P(("row", "depth"), "col"), check_vma=False
    )
```

profile of v0, /device:TPU:0, one launch (start us, length us, event | category | flops | bytes accessed | tf_op | source)
XLA Modules:
  0.0 89.9 jit_solution(8510044799648045284)
XLA Ops:
  6.6 0.7 copy-done.2
  7.4 0.5 copy-done.3
  8.1 0.6 copy-done
  8.7 0.2 fusion.2
  8.9 0.5 copy-done.1
  9.4 0.2 fusion.4
  9.8 0.9 tile.8
  10.7 5.2 %all-to-all-start = ((bf16[2,72,576]{1,0,2:T(2,128)(2,1)}), bf16[2,72,576]{1,0,2:T(2,128)(2,1)S(1)}, u32[]{:S(2)}, u32[]{:S(2)}) async-start(bf16[2,72,576]{1,0,2:T(2,128)(2,1)} %bitcast.2), calls=%async_computation | async-start | bytes 589824 | tf_op jit(solution)/shard_map/all_to_all | solution.py:25
  15.9 14.4 %all_gather.6 = bf16[2,288,144]{2,1,0:T(8,128)(2,1)S(1)} all-gather(bf16[2,72,144]{2,1,0:T(8,128)(2,1)S(1)} %pad_maximum_fusion.1), channel_id=1, replica_groups=mesh['row'=4,'col'=4,'depth'=2] {'row'}, dimensions={1}, use_global_device_ids=true | all-gather | bytes 207360 | tf_op jit(solution)/shard_map/all_gather | solution.py:32
  30.7 0.2 convolution_bitcast_fusion.3
  30.9 0.2 convolution_bitcast_fusion.4
  31.2 0.8 pad_maximum_fusion
  32.0 13.3 %reduce-scatter.7.cloned.1.call-done = f32[72,288]{1,0:T(8,128)} async-done(((f32[144,288]{1,0:T(8,128)}), f32[72,288]{1,0:T(8,128)}) %reduce-scatter.7.cloned.1.call-update) | async-done | bytes 82960
  45.3 0.9 %convert_element_type.35 = bf16[72,288]{1,0:T(8,128)(2,1)S(1)} convert(f32[72,288]{1,0:T(8,128)} %reduce-scatter.7.cloned.1.call-done) | non-fusion elementwise | flops 20736 | bytes 124416 | tf_op jit(solution)/shard_map/convert_element_type | solution.py:74
  46.7 0.5 broadcast.83
  47.2 1.6 %reduce = bf16[576,72]{1,0:T(8,128)(2,1)S(1)} reduce(bf16[576,1,72]{2,1,0:T(2,128)(2,1)S(1)} %bitcast.65, bf16[]{:T(256)} %broadcast.83), dimensions={1}, to_apply=%bitcast.43.reduce_sub_computation | reduce | bytes 165890
  48.8 0.9 reshape.81
  49.7 3.4 %all-to-all-start.1 = ((bf16[8,2,2592]{2,1,0:T(2,128)(2,1)}), bf16[8,2,2592]{2,1,0:T(2,128)(2,1)S(1)}, u32[]{:S(2)}, u32[]{:S(2)}) async-start(bf16[8,2,2592]{2,1,0:T(2,128)(2,1)} %reshape.81), calls=%async_computation.1 | async-start | bytes 172032 | tf_op jit(solution)/shard_map/all_to_all | solution.py:25
  53.1 14.2 %all_gather.7 = bf16[2,288,144]{2,1,0:T(8,128)(2,1)S(1)} all-gather(bf16[2,72,144]{2,1,0:T(8,128)(2,1)S(1)} %pad_maximum_fusion.2), channel_id=1, replica_groups=mesh['row'=4,'col'=4,'depth'=2] {'row'}, dimensions={1}, use_global_device_ids=true | all-gather | bytes 207360 | tf_op jit(solution)/shard_map/all_gather | solution.py:32
  67.3 0.2 convolution_bitcast_fusion.1
  68.2 0.2 convolution_bitcast_fusion
  68.5 0.9 fusion.1
  69.4 12.2 %reduce-scatter.5.cloned.1.call-done = f32[72,144]{1,0:T(8,128)} async-done(((f32[144,144]{1,0:T(8,128)}), f32[72,144]{1,0:T(8,128)}) %reduce-scatter.5.cloned.1.call-update) | async-done | bytes 41488 | tf_op jit(solution)/shard_map/reduce_scatter | solution.py:42
  81.6 1.5 %multiply_subtract_fusion = f32[72,144]{1,0:T(8,128)} fusion(f32[72,144]{1,0:T(8,128)} %reduce-scatter.5.cloned.1.call-done, bf16[72,144]{1,0:T(8,128)(2,1)S(1)} %fusion.2), kind=kLoop, calls=%fused_computation.15 | loop fusion | flops 41472 | bytes 103680 | tf_op jit(solution)/shard_map/sub | solution.py:88
  (31 shorter events, 2.1 us)
Async XLA Ops:
  6.5 0.7 copy-start.2
  7.2 0.7 copy-start.3
  7.9 0.8 copy-start
  8.7 0.8 copy-start.1
  10.7 19.6 %all-to-all-start = ((bf16[2,72,576]{1,0,2:T(2,128)(2,1)}), bf16[2,72,576]{1,0,2:T(2,128)(2,1)S(1)}, u32[]{:S(2)}, u32[]{:S(2)}) async-start(bf16[2,72,576]{1,0,2:T(2,128)(2,1)} %bitcast.2), calls=%async_computation | async-start | bytes 589824 | tf_op jit(solution)/shard_map/all_to_all | solution.py:25
  15.9 29.4 %reduce-scatter.7.cloned.1.call-start = ((), (), s32[]{:S(2)}) async-start(), calls=%async_computation.5 | async-start | bytes 331776
  49.7 17.9 %all-to-all-start.1 = ((bf16[8,2,2592]{2,1,0:T(2,128)(2,1)}), bf16[8,2,2592]{2,1,0:T(2,128)(2,1)S(1)}, u32[]{:S(2)}, u32[]{:S(2)}) async-start(bf16[8,2,2592]{2,1,0:T(2,128)(2,1)} %reshape.81), calls=%async_computation.1 | async-start | bytes 172032 | tf_op jit(solution)/shard_map/all_to_all | solution.py:25
  53.0 28.5 %reduce-scatter.5.cloned.1.call-start = ((), (), s32[]{:S(2)}) async-start(), calls=%async_computation.4 | async-start | bytes 221184 | tf_op jit(solution)/shard_map/reduce_scatter | solution.py:42
Sparse Core Ops, SparseCore 0:
  32.1 13.1 reduce-scatter.6
  69.5 12.0 reduce-scatter.4
where the time goes:
time: 90.5 us; the launch traced here: 89.9 us
  blocking collectives  28.6 us (32%)
  waiting for transfers between devices  25.5 us (28%)
  between operations  13.6 us (15%)
  starting transfers between devices  8.61 us (10%)
  local copies, waits for them, and re-layouts  6.02 us (7%)
  other arithmetic  4.89 us (5%)
  matrix products  2.69 us (3%)
    all_gather x2, blocking collectives, right_panels(): received = lax.all_gather(stacked, 'row', axis=1, tiled=True)  28.6 us
    unnamed x3, waiting for transfers between devices  13.3 us
    reduce_scatter x1, waiting for transfers between devices, layer_sum(): lax.psum_scatter(term_fn(jnp.int32(0), lax.axis_size('depth') * rows), 'd...  12.2 us
    all_to_all x2, starting transfers between devices, left_panels(): lax.all_to_all(tiled, ('col', 'depth'), split_axis=2, concat_axis=1, tile...  8.53 us
    unnamed x11, local copies, waits for them, and re-layouts  3.87 us
    dot_general x5, matrix products, partial_rows(): jnp.einsum('cdij,cjk->dik', left, right, preferred_element_type=jnp.float32)  1.85 us
  transfers between devices with their start and end apart: 4, of which 2 were waited for; matrix products, arithmetic and copies ran while one was open for 0% of the time, Pallas kernels for 0%

commit v1 on v0

v1 whole, which is shorter than its diff:
```python
import functools

import jax
import jax.numpy as jnp
from jax import lax
from jax.experimental import pallas as pl
from jax.experimental.pallas import tpu as pltpu
from jax.sharding import PartitionSpec as P

BLOCK = 128
LANES = 128
VMEM = pl.BlockSpec(memory_space=pltpu.VMEM)
SMEM = pl.BlockSpec(memory_space=pltpu.SMEM)
LIMIT = 48 * 1024 * 1024


def aligned(rows):
    return -(-rows // 16) * 16


def swap(value, axis, offset):
    size = lax.axis_size(axis)
    return lax.ppermute(value, axis, [(i, i ^ offset) for i in range(size)])


def block_fill(fill_ref, row_start, col_start, rows, width):
    count = fill_ref.shape[0]
    row_ids = row_start + lax.broadcasted_iota(jnp.int32, (rows, width), 0)
    col_ids = col_start + lax.broadcasted_iota(jnp.int32, (rows, width), 1)
    first_row, first_col = row_start // BLOCK, col_start // BLOCK
    mask = jnp.zeros((rows, width), jnp.float32)
    for i in range((rows - 2) // BLOCK + 2):
        row_at = first_row + i
        in_row = (row_ids >= row_at * BLOCK) & (row_ids < (row_at + 1) * BLOCK)
        for j in range((width - 2) // BLOCK + 2):
            col_at = first_col + j
            here = in_row & (col_ids >= col_at * BLOCK) & (col_ids < (col_at + 1) * BLOCK)
            flag = fill_ref[jnp.minimum(row_at, count - 1), jnp.minimum(col_at, count - 1)]
            mask = jnp.where(here, flag.astype(jnp.float32), mask)
    return mask


def pack_kernel(x_ref, t_ref, fill_x_ref, fill_t_ref, out_ref):
    rows, width = x_ref.shape
    row_at = lax.axis_index("row") * lax.axis_size("depth") + lax.axis_index("depth")
    row_start, col_start = row_at * rows, lax.axis_index("col") * width
    main = width - width % LANES
    rem = width - main
    for k, (ref, fill_ref) in enumerate(((x_ref, fill_x_ref), (t_ref, fill_t_ref))):
        mask = block_fill(fill_ref, row_start, col_start, rows, width)
        masked = (ref[...].astype(jnp.float32) * mask).astype(out_ref.dtype)
        out_ref[0, :, k * main : (k + 1) * main] = masked[:, :main]
        if rem:
            out_ref[0, :, 2 * main + k * rem : 2 * main + (k + 1) * rem] = masked[:, main:]


def pick(value, which, total, width):
    main = width - width % LANES
    rem = width - main
    parts = [value[:, which * main : (which + 1) * main]]
    if rem:
        parts.append(value[:, total * main + which * rem : total * main + (which + 1) * rem])
    return jnp.concatenate(parts, axis=1) if rem else parts[0]


def place(bits, position):
    offset = 0
    for at, weight in bits:
        offset = offset + ((position >> at) & 1) * weight
    return offset


def walk(refs, step, carry):
    base = 0
    for ref in refs:
        count = ref.shape[0]
        if count <= 4:
            for i in range(count):
                carry = step(base + i, ref[i], carry)
        else:
            carry = lax.fori_loop(
                0, count, lambda i, c, ref=ref, base=base: step(base + i, ref[i], c), carry
            )
        base += count
    return carry


def first_kernel(counts, bits, width, *refs):
    n_rows, n_cols = counts
    left, right = refs[:n_rows], refs[n_rows : n_rows + n_cols]
    out_ref, lhs = refs[n_rows + n_cols :]
    row_bits, depth_bits, col_bits = bits
    rows = right[0].shape[1]
    parts = width // rows
    top = aligned(rows)
    main = width - width % LANES
    rem = width - main
    my_row, my_depth, my_col = (lax.axis_index(a) for a in ("row", "depth", "col"))
    layers = lax.axis_size("depth")

    def fill(position, block, carry):
        col = my_col ^ place(col_bits, position)
        for k in range(2):
            whole = pick(block, k, 2, width)
            for h in range(parts):
                lhs[col * parts + h, k * top : k * top + rows, :] = whole[:, h * rows : (h + 1) * rows]
        return carry

    walk(left, fill, 0)

    def multiply(position, block, carry):
        row = my_row ^ place(row_bits, position)
        depth = my_depth ^ place(depth_bits, position)
        return carry + jnp.dot(
            lhs[row * layers + depth], block, preferred_element_type=jnp.float32
        )

    acc = walk(right, multiply, jnp.zeros((lhs.shape[1], right[0].shape[2]), jnp.float32))
    for at, size, base in ((0, main, 0), (2 * main, rem, 3 * main)):
        if not size:
            continue
        square = acc[:rows, at : at + size]
        cross = acc[top : top + rows, at : at + size] + acc[:rows, at + size : at + 2 * size]
        high = cross.astype(jnp.bfloat16)
        low = (cross - high.astype(jnp.float32)).astype(jnp.bfloat16)
        for k, value in enumerate((high, low, square.astype(jnp.bfloat16))):
            out_ref[0, :, base + k * size : base + (k + 1) * size] = value


def last_kernel(counts, bits, width, *refs):
    n_rows, n_cols = counts
    left, right = refs[:n_rows], refs[n_rows : n_rows + n_cols]
    own_ref, out_ref, lhs = refs[n_rows + n_cols :]
    row_bits, depth_bits, col_bits = bits
    rows = right[0].shape[1]
    parts = width // rows
    top = aligned(rows)
    main = width - width % LANES
    rem = width - main
    my_row, my_depth, my_col = (lax.axis_index(a) for a in ("row", "depth", "col"))
    layers = lax.axis_size("depth")

    def fill(position, block, carry):
        col = my_col ^ place(col_bits, position)
        for k in range(3):
            whole = pick(block, k, 3, width)
            for h in range(parts):
                lhs[col * parts + h, k * top : k * top + rows, :] = whole[:, h * rows : (h + 1) * rows]
        return carry

    walk(left, fill, 0)

    def multiply(position, block, carry):
        row = my_row ^ place(row_bits, position)
        depth = my_depth ^ place(depth_bits, position)
        return carry + jnp.dot(
            lhs[row * layers + depth], block, preferred_element_type=jnp.float32
        )

    acc = walk(right, multiply, jnp.zeros((lhs.shape[1], right[0].shape[2]), jnp.float32))
    for at, size, base in ((0, main, 0), (2 * main, rem, main)):
        if not size:
            continue
        total = (
            acc[:rows, at : at + size]
            + acc[top : top + rows, at : at + size]
            + acc[2 * top : 2 * top + rows, at + size : at + 2 * size]
        )
        own = own_ref[0, :, at + size : at + 2 * size].astype(jnp.float32)
        out_ref[:, base : base + size] = 1.5 * own - 0.5 * total


def gather_columns(block):
    rows, layers = lax.axis_size("row"), lax.axis_size("depth")
    far = swap(block, "row", 3)
    near = swap(block, "row", 1)
    side = swap(block, "depth", 1)
    pair = jnp.concatenate([near, far], axis=0)
    opposite = swap(far, "row", 1)
    side_opposite = swap(side, "row", 2)
    side_pair = swap(pair, "depth", 1)
    row_bits, depth_bits = [(0, 1), (1, 2)], [(2, 1)]
    gathered = [block, near, opposite, far, side, side_pair[:1], side_opposite, side_pair[1:]]
    if rows == 4 and layers == 2:
        return gathered, row_bits, depth_bits
    held = jnp.concatenate(gathered, axis=0)
    at = 3
    for axis, offset, bits in [("row", 1 << k, row_bits) for k in range(2, rows.bit_length() - 1)] + [
        ("depth", 1 << k, depth_bits) for k in range(1, layers.bit_length() - 1)
    ]:
        held = jnp.concatenate([held, swap(held, axis, offset)], axis=0)
        bits.append((at, offset))
        at += 1
    return [held], row_bits, depth_bits


def gather_rows(block):
    size = lax.axis_size("col")
    bits, at, held = [], 0, block
    for k in range(1, size.bit_length() - 1):
        held = jnp.concatenate([held, swap(held, "col", 1 << k)], axis=0)
        bits.append((at, 1 << k))
        at += 1
    bits.append((at, 1))
    return [held, swap(held, "col", 1)], bits


def body(x_matrix, tangent, fill_x, fill_t):
    rows, width = x_matrix.shape
    main = width - width % LANES
    blocks = lax.axis_size("row") * lax.axis_size("depth")
    params = pltpu.CompilerParams(vmem_limit_bytes=LIMIT)
    packed = pl.pallas_call(
        pack_kernel,
        out_shape=jax.ShapeDtypeStruct((1, rows, 2 * width), jnp.bfloat16),
        in_specs=[VMEM, VMEM, SMEM, SMEM],
        out_specs=VMEM,
        compiler_params=params,
        name="pack",
    )(x_matrix, tangent, fill_x, fill_t)
    right, row_bits, depth_bits = gather_columns(packed)
    left, col_bits = gather_rows(packed)
    bits = (tuple(row_bits), tuple(depth_bits), tuple(col_bits))
    top = aligned(rows)
    firsts = pl.pallas_call(
        functools.partial(first_kernel, (len(left), len(right)), bits, width),
        out_shape=jax.ShapeDtypeStruct((1, rows, 3 * width), jnp.bfloat16),
        in_specs=[VMEM] * (len(left) + len(right)),
        out_specs=VMEM,
        scratch_shapes=[pltpu.VMEM((blocks, 2 * top, rows), jnp.bfloat16)],
        compiler_params=params,
        name="firsts",
    )(*left, *right)
    left, col_bits = gather_rows(firsts)
    return pl.pallas_call(
        functools.partial(last_kernel, (len(left), len(right)), bits, width),
        out_shape=jax.ShapeDtypeStruct((rows, width), jnp.float32),
        in_specs=[VMEM] * (len(left) + len(right) + 1),
        out_specs=VMEM,
        scratch_shapes=[pltpu.VMEM((blocks, 3 * top, rows), jnp.bfloat16)],
        compiler_params=params,
        name="lasts",
    )(*left, *right, packed)


def solution(mesh):
    placed = (P(("row", "depth"), "col"), P(("row", "depth"), "col"), P(), P())
    return jax.shard_map(
        body, mesh=mesh, in_specs=placed, out_specs=P(("row", "depth"), "col"), check_vma=False
    )
```

time: 90.5 us -> 31.1 us (0.34)
  blocking collectives: 28.6 us -> 0 us
  waiting for transfers between devices: 25.5 us -> 10.6 us
  between operations: 13.6 us -> 0.05 us
  starting transfers between devices: 8.61 us -> 13.8 us
  other arithmetic: 4.89 us -> 0.07 us
  Pallas kernels: 0 us -> 3.32 us
  local copies, waits for them, and re-layouts: 6.02 us -> 2.92 us
  matrix products: 2.69 us -> 0 us
    all_gather x2 -> x0, blocking collectives: 28.6 us -> none  [right_panels(): received = lax.all_gather(stacked, 'row', axis=1, tiled=True)]
    ppermute x0 -> x10, starting transfers between devices: none -> 13.8 us  [swap(): return lax.ppermute(value, axis, [(i, i ^ offset) for i in range(size)])]
    unnamed x3 -> x0, waiting for transfers between devices: 13.3 us -> none
    reduce_scatter x1 -> x0, waiting for transfers between devices: 12.2 us -> none  [layer_sum(): lax.psum_scatter(term_fn(jnp.int32(0), lax.axis_size('depth') * rows), 'd...]
    ppermute x0 -> x10, waiting for transfers between devices: none -> 10.6 us  [swap(): return lax.ppermute(value, axis, [(i, i ^ offset) for i in range(size)])]
    all_to_all x2 -> x0, starting transfers between devices: 8.53 us -> none  [left_panels(): lax.all_to_all(tiled, ('col', 'depth'), split_axis=2, concat_axis=1, tile...]
    pallas_call x0 -> x3, Pallas kernels: none -> 3.32 us  [the longest x1 1.73 us: body(): pl.pallas_call(functools.partial(last_kernel, (len(left), len(right)), bi...]
    dot_general x9 -> x0, matrix products: 2.69 us -> none  [the longest x5 1.85 us: partial_rows(): jnp.einsum('cdij,cjk->dik', left, right, preferred_element_type=jnp.float32)]
  transfers between devices with their start and end apart: 4 -> 10, of which waited for: 2 -> 5; matrix products, arithmetic and copies ran while one was open for 0% -> 0% of each run, Pallas kernels for 0% -> 0%
where the time goes in v1:
time: 31.1 us; the launch traced here: 30.8 us
  starting transfers between devices  13.8 us (44%)
  waiting for transfers between devices  10.6 us (34%)
  Pallas kernels  3.32 us (11%)
  local copies, waits for them, and re-layouts  2.92 us (9%)
    ppermute x10, starting transfers between devices, swap(): return lax.ppermute(value, axis, [(i, i ^ offset) for i in range(size)])  13.8 us
    ppermute x10, waiting for transfers between devices, swap(): return lax.ppermute(value, axis, [(i, i ^ offset) for i in range(size)])  10.6 us
    unnamed x8, local copies, waits for them, and re-layouts  2.91 us
    pallas_call x1, Pallas kernels, body(): pl.pallas_call(functools.partial(last_kernel, (len(left), len(right)), bi...  1.73 us
    pallas_call x1, Pallas kernels, body(): pl.pallas_call(pack_kernel, out_shape=jax.ShapeDtypeStruct((1, rows, 2 *...  0.89 us
    pallas_call x1, Pallas kernels, body(): pl.pallas_call(functools.partial(first_kernel, (len(left), len(right)), b...  0.7 us
  transfers between devices with their start and end apart: 10, of which 5 were waited for; matrix products, arithmetic and copies ran while one was open for 0% of the time, Pallas kernels for 0%

profile of v1, /device:TPU:0, one launch (start us, length us, event | category | flops | bytes accessed | tf_op | source)
XLA Modules:
  0.0 30.8 jit_solution(968423365819062615)
XLA Ops:
  0.0 0.8 %copy-done = bf16[72,144]{1,0:T(8,128)(2,1)S(1)} copy-done((bf16[72,144]{1,0:T(8,128)(2,1)S(1)}, bf16[72,144]{1,0:T(8,128)(2,1)}, u32[]{:S(2)}) %copy-start) | copy-done | bytes 20760
  0.8 0.8 %copy-done.1 = bf16[72,144]{1,0:T(8,128)(2,1)S(1)} copy-done((bf16[72,144]{1,0:T(8,128)(2,1)S(1)}, bf16[72,144]{1,0:T(8,128)(2,1)}, u32[]{:S(2)}) %copy-start.1) | copy-done | bytes 20760
  1.5 0.7 %copy-done.2 = s32[5,5]{1,0:T(8,128)S(1)} copy-done((s32[5,5]{1,0:T(8,128)S(1)}, s32[5,5]{1,0:T(8,128)}, u32[]{:S(2)}) %copy-start.2) | copy-done | bytes 124
  2.2 0.7 %copy-done.3 = s32[5,5]{1,0:T(8,128)S(1)} copy-done((s32[5,5]{1,0:T(8,128)S(1)}, s32[5,5]{1,0:T(8,128)}, u32[]{:S(2)}) %copy-start.3) | copy-done | bytes 124
  2.9 0.9 %pack.1.refs_2_.refs_10_ = bf16[1,72,288]{2,1,0:T(8,128)(2,1)S(1)} custom-call(bf16[72,144]{1,0:T(8,128)(2,1)S(1)} %copy-done, bf16[72,144]{1,0:T(8,128)(2,1)S(1)} %copy-done.1, s32[5,5]{1,0:T(8,128)S(1)} %copy-done.2, s32[5,5]{1,0:T(8,128)S(1)} %copy-done.3), custom_call_target="tpu_custom_call" | custom-call | tf_op jit(solution)/shard_map/pack/pallas_call | solution.py:213
  3.8 5.1 %collective-permute-start.3 = (bf16[1,72,288]{2,1,0:T(8,128)(2,1)S(1)}, bf16[1,72,288]{2,1,0:T(8,128)(2,1)S(1)}, u32[]{:S(2)}, u32[]{:S(2)}) collective-permute-start(bf16[1,72,288]{2,1,0:T(8,128)(2,1)S(1)} %pack.1.refs_2_.refs_10_), channel_id=1, source_target_pairs={{0,24},{8,16},{16,8},{24,0},{1,25},{9,17},{17,9},{25,1},{2,26},{10... | collective-permute-start | bytes 124424 | tf_op jit(solution)/shard_map/ppermute | solution.py:23
  8.9 0.0 collective-permute-start.2
  8.9 1.5 %collective-permute-start.5 = (bf16[1,72,288]{2,1,0:T(8,128)(2,1)S(1)}, bf16[1,72,288]{2,1,0:T(8,128)(2,1)S(1)}, u32[]{:S(2)}, u32[]{:S(2)}) collective-permute-start(bf16[1,72,288]{2,1,0:T(8,128)(2,1)S(1)} %pack.1.refs_2_.refs_10_), channel_id=1, source_target_pairs={{0,1},{1,0},{2,3},{3,2},{4,5},{5,4},{6,7},{7,6},{8,9},{9,8},{10,11... | collective-permute-start | bytes 124424 | tf_op jit(solution)/shard_map/ppermute | solution.py:23
  10.4 1.5 %collective-permute-start = (bf16[1,72,288]{2,1,0:T(8,128)(2,1)S(1)}, bf16[1,72,288]{2,1,0:T(8,128)(2,1)S(1)}, u32[]{:S(2)}, u32[]{:S(2)}) collective-permute-start(bf16[1,72,288]{2,1,0:T(8,128)(2,1)S(1)} %pack.1.refs_2_.refs_10_), channel_id=1, source_target_pairs={{0,4},{2,6},{4,0},{6,2},{1,5},{3,7},{5,1},{7,3},{8,12},{10,14},{12... | collective-permute-start | bytes 124424 | tf_op jit(solution)/shard_map/ppermute | solution.py:23
  11.9 0.0 collective-permute-done.3.refs_5_
  11.9 1.1 %collective-permute-done.2.refs_3_ = bf16[1,72,288]{2,1,0:T(8,128)(2,1)S(1)} collective-permute-done((bf16[1,72,288]{2,1,0:T(8,128)(2,1)S(1)}, bf16[1,72,288]{2,1,0:T(8,128)(2,1)S(1)}, u32[]{:S(2)}, u32[]{:S(2)}) %collective-permute-start.2) | collective-permute-done | bytes 41504 | tf_op jit(solution)/shard_map/ppermute | solution.py:23
  13.0 1.6 %collective-permute-start.6 = (bf16[2,72,288]{2,1,0:T(8,128)(2,1)S(1)}, bf16[2,72,288]{2,1,0:T(8,128)(2,1)S(1)}, u32[]{:S(2)}, u32[]{:S(2)}) collective-permute-start(bf16[2,72,288]{2,1,0:T(8,128)(2,1)S(1)} %pad_maximum_fusion.2), channel_id=1, source_target_pairs={{0,1},{1,0},{2,3},{3,2},{4,5},{5,4},{6,7},{7,6},{8,9},{9,8},{10,11... | collective-permute-start | bytes 248840 | tf_op jit(solution)/shard_map/ppermute | solution.py:23
  14.7 0.1 collective-permute-start.1
  14.7 2.0 %collective-permute-start.4 = (bf16[1,72,288]{2,1,0:T(8,128)(2,1)S(1)}, bf16[1,72,288]{2,1,0:T(8,128)(2,1)S(1)}, u32[]{:S(2)}, u32[]{:S(2)}) collective-permute-start(bf16[1,72,288]{2,1,0:T(8,128)(2,1)S(1)} %collective-permute-done.3.refs_5_), channel_id=1, source_target_pairs={{0,8},{8,0},{16,24},{24,16},{1,9},{9,1},{17,25},{25,17},{2,10},{10... | collective-permute-start | bytes 124424 | tf_op jit(solution)/shard_map/ppermute | solution.py:23
  16.7 0.0 collective-permute-done.5.refs_6_
  16.7 0.5 %collective-permute-start.7 = (bf16[1,72,288]{2,1,0:T(8,128)(2,1)S(1)}, bf16[1,72,288]{2,1,0:T(8,128)(2,1)S(1)}, u32[]{:S(2)}, u32[]{:S(2)}) collective-permute-start(bf16[1,72,288]{2,1,0:T(8,128)(2,1)S(1)} %collective-permute-done.5.refs_6_), channel_id=1, source_target_pairs={{0,16},{8,24},{16,0},{24,8},{1,17},{9,25},{17,1},{25,9},{2,18},{10... | collective-permute-start | bytes 124424 | tf_op jit(solution)/shard_map/ppermute | solution.py:23
  17.2 0.6 %collective-permute-done.6 = bf16[2,72,288]{2,1,0:T(8,128)(2,1)S(1)} collective-permute-done((bf16[2,72,288]{2,1,0:T(8,128)(2,1)S(1)}, bf16[2,72,288]{2,1,0:T(8,128)(2,1)S(1)}, u32[]{:S(2)}, u32[]{:S(2)}) %collective-permute-start.6) | collective-permute-done | bytes 82976 | tf_op jit(solution)/shard_map/ppermute | solution.py:23
  17.9 4.6 %collective-permute-done.7.refs_8_ = bf16[1,72,288]{2,1,0:T(8,128)(2,1)S(1)} collective-permute-done((bf16[1,72,288]{2,1,0:T(8,128)(2,1)S(1)}, bf16[1,72,288]{2,1,0:T(8,128)(2,1)S(1)}, u32[]{:S(2)}, u32[]{:S(2)}) %collective-permute-start.7) | collective-permute-done | bytes 41504 | tf_op jit(solution)/shard_map/ppermute | solution.py:23
  22.5 0.7 %firsts.1 = bf16[1,72,432]{2,1,0:T(8,128)(2,1)S(1)} custom-call(bf16[2,72,288]{2,1,0:T(8,128)(2,1)S(1)} %pad_maximum_fusion.1.refs_0_, bf16[2,72,288]{2,1,0:T(8,128)(2,1)S(1)} %collective-permute-done.1.refs_1_, bf16[1,72,288]{2,1,0:T(8,128)(2,1)S(1)} %pack.1.refs_2_.refs_10_, bf16[1,72,288]{2,1,0:T(8,128)(2,1)S(1)} %collective-permute-done.2.refs_3_, ...), custom_call_target="tpu_custom_call" | custom-call | tf_op jit(solution)/shard_map/firsts/pallas_call | solution.py:225
  23.2 1.6 %collective-permute-start.8 = (bf16[1,72,432]{2,1,0:T(8,128)(2,1)S(1)}, bf16[1,72,432]{2,1,0:T(8,128)(2,1)S(1)}, u32[]{:S(2)}, u32[]{:S(2)}) collective-permute-start(bf16[1,72,432]{2,1,0:T(8,128)(2,1)S(1)} %firsts.1), channel_id=1, source_target_pairs={{0,4},{2,6},{4,0},{6,2},{1,5},{3,7},{5,1},{7,3},{8,12},{10,14},{12... | collective-permute-start | bytes 186632 | tf_op jit(solution)/shard_map/ppermute | solution.py:23
  24.7 2.9 %collective-permute-done.8 = bf16[1,72,432]{2,1,0:T(8,128)(2,1)S(1)} collective-permute-done((bf16[1,72,432]{2,1,0:T(8,128)(2,1)S(1)}, bf16[1,72,432]{2,1,0:T(8,128)(2,1)S(1)}, u32[]{:S(2)}, u32[]{:S(2)}) %collective-permute-start.8) | collective-permute-done | bytes 62240 | tf_op jit(solution)/shard_map/ppermute | solution.py:23
  27.6 0.1 collective-permute-start.9
  27.7 1.4 %collective-permute-done.9.refs_1_ = bf16[2,72,432]{2,1,0:T(8,128)(2,1)S(1)} collective-permute-done((bf16[2,72,432]{2,1,0:T(8,128)(2,1)S(1)}, bf16[2,72,432]{2,1,0:T(8,128)(2,1)S(1)}, u32[]{:S(2)}, u32[]{:S(2)}) %collective-permute-start.9) | collective-permute-done | bytes 124448 | tf_op jit(solution)/shard_map/ppermute | solution.py:23
  29.1 1.7 %lasts.1 = f32[72,144]{1,0:T(8,128)} custom-call(bf16[2,72,432]{2,1,0:T(8,128)(2,1)S(1)} %pad_maximum_fusion.refs_0_, bf16[2,72,432]{2,1,0:T(8,128)(2,1)S(1)} %collective-permute-done.9.refs_1_, bf16[1,72,288]{2,1,0:T(8,128)(2,1)S(1)} %pack.1.refs_2_.refs_10_, bf16[1,72,288]{2,1,0:T(8,128)(2,1)S(1)} %collective-permute-done.2.refs_3_, ...), custom_call_target="tpu_custom_call" | custom-call | tf_op jit(solution)/shard_map/lasts/pallas_call | solution.py:235
  (11 shorter events, 0.1 us)
Async XLA Ops:
  0.0 0.8 %copy-start = (bf16[72,144]{1,0:T(8,128)(2,1)S(1)}, bf16[72,144]{1,0:T(8,128)(2,1)}, u32[]{:S(2)}) copy-start(bf16[72,144]{1,0:T(8,128)(2,1)} %x_ref.1) | copy-start | bytes 62212
  0.8 0.8 %copy-start.1 = (bf16[72,144]{1,0:T(8,128)(2,1)S(1)}, bf16[72,144]{1,0:T(8,128)(2,1)}, u32[]{:S(2)}) copy-start(bf16[72,144]{1,0:T(8,128)(2,1)} %t_ref.1) | copy-start | bytes 62212
  1.5 0.7 %copy-start.2 = (s32[5,5]{1,0:T(8,128)S(1)}, s32[5,5]{1,0:T(8,128)}, u32[]{:S(2)}) copy-start(s32[5,5]{1,0:T(8,128)} %fill_x_ref.1) | copy-start | bytes 304
  2.2 0.7 %copy-start.3 = (s32[5,5]{1,0:T(8,128)S(1)}, s32[5,5]{1,0:T(8,128)}, u32[]{:S(2)}) copy-start(s32[5,5]{1,0:T(8,128)} %fill_t_ref.1) | copy-start | bytes 304
  3.8 8.1 %collective-permute-start.3 = (bf16[1,72,288]{2,1,0:T(8,128)(2,1)S(1)}, bf16[1,72,288]{2,1,0:T(8,128)(2,1)S(1)}, u32[]{:S(2)}, u32[]{:S(2)}) collective-permute-start(bf16[1,72,288]{2,1,0:T(8,128)(2,1)S(1)} %pack.1.refs_2_.refs_10_), channel_id=1, source_target_pairs={{0,24},{8,16},{16,8},{24,0},{1,25},{9,17},{17,9},{25,1},{2,26},{10... | collective-permute-start | bytes 124424 | tf_op jit(solution)/shard_map/ppermute | solution.py:23
  8.9 4.2 %collective-permute-start.2 = (bf16[1,72,288]{2,1,0:T(8,128)(2,1)S(1)}, bf16[1,72,288]{2,1,0:T(8,128)(2,1)S(1)}, u32[]{:S(2)}, u32[]{:S(2)}) collective-permute-start(bf16[1,72,288]{2,1,0:T(8,128)(2,1)S(1)} %pack.1.refs_2_.refs_10_), channel_id=1, source_target_pairs={{0,8},{8,0},{16,24},{24,16},{1,9},{9,1},{17,25},{25,17},{2,10},{10... | collective-permute-start | bytes 124424 | tf_op jit(solution)/shard_map/ppermute | solution.py:23
  8.9 7.9 %collective-permute-start.5 = (bf16[1,72,288]{2,1,0:T(8,128)(2,1)S(1)}, bf16[1,72,288]{2,1,0:T(8,128)(2,1)S(1)}, u32[]{:S(2)}, u32[]{:S(2)}) collective-permute-start(bf16[1,72,288]{2,1,0:T(8,128)(2,1)S(1)} %pack.1.refs_2_.refs_10_), channel_id=1, source_target_pairs={{0,1},{1,0},{2,3},{3,2},{4,5},{5,4},{6,7},{7,6},{8,9},{9,8},{10,11... | collective-permute-start | bytes 124424 | tf_op jit(solution)/shard_map/ppermute | solution.py:23
  10.4 4.3 %collective-permute-start = (bf16[1,72,288]{2,1,0:T(8,128)(2,1)S(1)}, bf16[1,72,288]{2,1,0:T(8,128)(2,1)S(1)}, u32[]{:S(2)}, u32[]{:S(2)}) collective-permute-start(bf16[1,72,288]{2,1,0:T(8,128)(2,1)S(1)} %pack.1.refs_2_.refs_10_), channel_id=1, source_target_pairs={{0,4},{2,6},{4,0},{6,2},{1,5},{3,7},{5,1},{7,3},{8,12},{10,14},{12... | collective-permute-start | bytes 124424 | tf_op jit(solution)/shard_map/ppermute | solution.py:23
  13.0 4.8 %collective-permute-start.6 = (bf16[2,72,288]{2,1,0:T(8,128)(2,1)S(1)}, bf16[2,72,288]{2,1,0:T(8,128)(2,1)S(1)}, u32[]{:S(2)}, u32[]{:S(2)}) collective-permute-start(bf16[2,72,288]{2,1,0:T(8,128)(2,1)S(1)} %pad_maximum_fusion.2), channel_id=1, source_target_pairs={{0,1},{1,0},{2,3},{3,2},{4,5},{5,4},{6,7},{7,6},{8,9},{9,8},{10,11... | collective-permute-start | bytes 248840 | tf_op jit(solution)/shard_map/ppermute | solution.py:23
  14.7 7.8 %collective-permute-start.1 = (bf16[2,72,288]{2,1,0:T(8,128)(2,1)S(1)}, bf16[2,72,288]{2,1,0:T(8,128)(2,1)S(1)}, u32[]{:S(2)}, u32[]{:S(2)}) collective-permute-start(bf16[2,72,288]{2,1,0:T(8,128)(2,1)S(1)} %pad_maximum_fusion.1.refs_0_), channel_id=1, source_target_pairs={{0,2},{2,0},{4,6},{6,4},{1,3},{3,1},{5,7},{7,5},{8,10},{10,8},{12,... | collective-permute-start | bytes 248840 | tf_op jit(solution)/shard_map/ppermute | solution.py:23
  14.7 7.7 %collective-permute-start.4 = (bf16[1,72,288]{2,1,0:T(8,128)(2,1)S(1)}, bf16[1,72,288]{2,1,0:T(8,128)(2,1)S(1)}, u32[]{:S(2)}, u32[]{:S(2)}) collective-permute-start(bf16[1,72,288]{2,1,0:T(8,128)(2,1)S(1)} %collective-permute-done.3.refs_5_), channel_id=1, source_target_pairs={{0,8},{8,0},{16,24},{24,16},{1,9},{9,1},{17,25},{25,17},{2,10},{10... | collective-permute-start | bytes 124424 | tf_op jit(solution)/shard_map/ppermute | solution.py:23
  16.7 5.7 %collective-permute-start.7 = (bf16[1,72,288]{2,1,0:T(8,128)(2,1)S(1)}, bf16[1,72,288]{2,1,0:T(8,128)(2,1)S(1)}, u32[]{:S(2)}, u32[]{:S(2)}) collective-permute-start(bf16[1,72,288]{2,1,0:T(8,128)(2,1)S(1)} %collective-permute-done.5.refs_6_), channel_id=1, source_target_pairs={{0,16},{8,24},{16,0},{24,8},{1,17},{9,25},{17,1},{25,9},{2,18},{10... | collective-permute-start | bytes 124424 | tf_op jit(solution)/shard_map/ppermute | solution.py:23
  23.2 4.4 %collective-permute-start.8 = (bf16[1,72,432]{2,1,0:T(8,128)(2,1)S(1)}, bf16[1,72,432]{2,1,0:T(8,128)(2,1)S(1)}, u32[]{:S(2)}, u32[]{:S(2)}) collective-permute-start(bf16[1,72,432]{2,1,0:T(8,128)(2,1)S(1)} %firsts.1), channel_id=1, source_target_pairs={{0,4},{2,6},{4,0},{6,2},{1,5},{3,7},{5,1},{7,3},{8,12},{10,14},{12... | collective-permute-start | bytes 186632 | tf_op jit(solution)/shard_map/ppermute | solution.py:23
  27.6 1.4 %collective-permute-start.9 = (bf16[2,72,432]{2,1,0:T(8,128)(2,1)S(1)}, bf16[2,72,432]{2,1,0:T(8,128)(2,1)S(1)}, u32[]{:S(2)}, u32[]{:S(2)}) collective-permute-start(bf16[2,72,432]{2,1,0:T(8,128)(2,1)S(1)} %pad_maximum_fusion.refs_0_), channel_id=1, source_target_pairs={{0,2},{2,0},{4,6},{6,4},{1,3},{3,1},{5,7},{7,5},{8,10},{10,8},{12,... | collective-permute-start | bytes 373256 | tf_op jit(solution)/shard_map/ppermute | solution.py:23

commit v2 on v1

v2 whole, which is shorter than its diff:
```python
import functools

import jax
import jax.numpy as jnp
from jax import lax
from jax.experimental import pallas as pl
from jax.experimental.pallas import tpu as pltpu
from jax.sharding import PartitionSpec as P

BLOCK = 128
LANES = 128
FOLD = 16
HBM = pl.BlockSpec(memory_space=pltpu.HBM)
VMEM = pl.BlockSpec(memory_space=pltpu.VMEM)
PARAMS = pltpu.CompilerParams(vmem_limit_bytes=48 * 1024 * 1024)


def aligned(rows):
    return -(-rows // 16) * 16


def split(width):
    rem = width % LANES
    return width - rem, rem, FOLD if rem else 0


def swap(value, axis, offset):
    size = lax.axis_size(axis)
    return lax.ppermute(value, axis, [(i, i ^ offset) for i in range(size)])


def block_fill(fill_ref, row_start, col_start, rows, width):
    count = fill_ref.shape[0]
    row_ids = row_start + lax.broadcasted_iota(jnp.int32, (rows, width), 0)
    col_ids = col_start + lax.broadcasted_iota(jnp.int32, (rows, width), 1)
    first_row, first_col = row_start // BLOCK, col_start // BLOCK
    mask = jnp.zeros((rows, width), jnp.float32)
    for i in range((rows - 2) // BLOCK + 2):
        row_at = first_row + i
        in_row = (row_ids >= row_at * BLOCK) & (row_ids < (row_at + 1) * BLOCK)
        for j in range((width - 2) // BLOCK + 2):
            col_at = first_col + j
            here = in_row & (col_ids >= col_at * BLOCK) & (col_ids < (col_at + 1) * BLOCK)
            flag = fill_ref[jnp.minimum(row_at, count - 1), jnp.minimum(col_at, count - 1)]
            mask = jnp.where(here, flag.astype(jnp.float32), mask)
    return mask


def fold(value):
    rows, lanes = value.shape
    spare = -rows % FOLD
    if spare:
        value = jnp.concatenate([value, jnp.zeros((spare, lanes), value.dtype)], axis=0)
    return jnp.concatenate([value[at : at + FOLD] for at in range(0, rows, FOLD)], axis=1)


def unfold(value, rows, lanes):
    groups = [value[:, k * lanes : (k + 1) * lanes] for k in range(-(-rows // FOLD))]
    return jnp.concatenate(groups, axis=0)[:rows]


def pack_kernel(
    x_hbm, t_hbm, fill_x_hbm, fill_t_hbm, out_ref, x_ref, t_ref, fill_x_ref, fill_t_ref, sems
):
    rows, width = x_ref.shape
    main, rem, lead = split(width)
    pairs = ((fill_x_hbm, fill_x_ref), (fill_t_hbm, fill_t_ref), (x_hbm, x_ref), (t_hbm, t_ref))
    copies = [pltpu.make_async_copy(src, dst, sems.at[k]) for k, (src, dst) in enumerate(pairs)]
    for copy in copies:
        copy.start()
    row_at = lax.axis_index("row") * lax.axis_size("depth") + lax.axis_index("depth")
    row_start, col_start = row_at * rows, lax.axis_index("col") * width
    copies[0].wait()
    copies[1].wait()
    masks = [block_fill(ref, row_start, col_start, rows, width) for ref in (fill_x_ref, fill_t_ref)]
    copies[2].wait()
    copies[3].wait()
    masked = [x_ref[...].astype(jnp.float32) * masks[0], t_ref[...].astype(jnp.float32) * masks[1]]
    for k, value in enumerate(masked):
        out_ref[0, lead:, k * main : (k + 1) * main] = value[:, :main].astype(out_ref.dtype)
    if rem:
        folded = fold(jnp.concatenate([value[:, main:] for value in masked], axis=1))
        out_ref[0, :FOLD, : folded.shape[1]] = folded.astype(out_ref.dtype)


def mains_and_rems(block, rows, rem, lead, total):
    mains = block[lead:]
    return mains, (unfold(block[:lead], rows, total * rem) if rem else None)


def place(bits, position):
    if isinstance(bits[0], int):
        return bits[position]
    offset = 0
    for at, weight in bits:
        offset = offset ^ (((position >> at) & 1) * weight)
    return offset


def walk(refs, step, carry):
    base = 0
    for ref in refs:
        count = ref.shape[0]
        if count <= 4:
            for i in range(count):
                carry = step(base + i, ref[i], carry)
        else:
            carry = lax.fori_loop(
                0, count, lambda i, c, ref=ref, base=base: step(base + i, ref[i], c), carry
            )
        base += count
    return carry


def panel_product(left, right, lhs, total, width, rows, places):
    row_bits, depth_bits, col_bits = places
    main, rem, lead = split(width)
    parts, top = width // rows, aligned(rows)
    my_row, my_depth, my_col = (lax.axis_index(a) for a in ("row", "depth", "col"))
    layers = lax.axis_size("depth")

    def fill(position, block, carry):
        col = my_col ^ place(col_bits, position)
        mains, rems = mains_and_rems(block, rows, rem, lead, total)
        for k in range(total):
            whole = mains[:, k * main : (k + 1) * main]
            if rem:
                whole = jnp.concatenate([whole, rems[:, k * rem : (k + 1) * rem]], axis=1)
            for h in range(parts):
                lhs[col * parts + h, k * top : k * top + rows, :] = whole[:, h * rows : (h + 1) * rows]
        return carry

    walk(left, fill, 0)

    def multiply(position, block, carry):
        row = my_row ^ place(row_bits, position)
        depth = my_depth ^ place(depth_bits, position)
        factor = lhs[row * layers + depth]
        operands = mains_and_rems(block, rows, rem, lead, 2)
        return tuple(
            c + jnp.dot(factor, o, preferred_element_type=jnp.float32)
            for c, o in zip(carry, operands[: len(carry)], strict=True)
        )

    sizes = (2 * main, 2 * rem) if rem else (2 * main,)
    zeros = tuple(jnp.zeros((lhs.shape[1], size), jnp.float32) for size in sizes)
    return walk(right, multiply, zeros)


def first_kernel(counts, places, width, *refs):
    n_left, n_right = counts
    left, right = refs[:n_left], refs[n_left : n_left + n_right]
    out_ref, lhs = refs[n_left + n_right :]
    main, rem, lead = split(width)
    rows = out_ref.shape[1] - lead
    top = aligned(rows)
    sums = panel_product(left, right, lhs, 2, width, rows, places)
    results = []
    for acc in sums:
        size = acc.shape[1] // 2
        square = acc[:rows, :size]
        cross = acc[top : top + rows, :size] + acc[:rows, size:]
        high = cross.astype(jnp.bfloat16).astype(jnp.float32)
        results.append((high, cross - high, square))
    for k, value in enumerate(results[0]):
        out_ref[0, lead:, k * main : (k + 1) * main] = value.astype(out_ref.dtype)
    if rem:
        folded = fold(jnp.concatenate(results[1], axis=1))
        out_ref[0, :FOLD, : folded.shape[1]] = folded.astype(out_ref.dtype)


def last_kernel(counts, places, width, *refs):
    n_left, n_right = counts
    left, right = refs[:n_left], refs[n_left : n_left + n_right]
    own_ref, out_ref, lhs = refs[n_left + n_right :]
    main, rem, lead = split(width)
    rows = out_ref.shape[0]
    top = aligned(rows)
    sums = panel_product(left, right, lhs, 3, width, rows, places)
    owns = mains_and_rems(own_ref[0], rows, rem, lead, 2)
    for acc, own, base in zip(sums, owns, (0, main)):
        size = acc.shape[1] // 2
        total = acc[:rows, :size] + acc[top : top + rows, :size] + acc[2 * top : 2 * top + rows, size:]
        out_ref[:, base : base + size] = 1.5 * own[:, size:].astype(jnp.float32) - 0.5 * total


def gather_columns(block):
    rows, layers = lax.axis_size("row"), lax.axis_size("depth")
    zs = [swap(block, "row", k) for k in (1, 2, 3)]
    line = jnp.concatenate([block] + zs, axis=0)
    gathered = [line, swap(line, "depth", 1)]
    row_bits, depth_bits = (0, 1, 2, 3, 0, 1, 2, 3), (0, 0, 0, 0, 1, 1, 1, 1)

    if rows == 4 and layers == 2:
        return gathered, row_bits, depth_bits
    places = list(zip(row_bits, depth_bits, strict=True))
    blocks = jnp.concatenate(gathered, axis=0)
    held = jnp.stack([blocks[places.index((k & 3, k >> 2))] for k in range(8)])
    row_bits, depth_bits, at = [(0, 1), (1, 2)], [(2, 1)], 3
    for axis, offset, bits in [("row", 1 << k, row_bits) for k in range(2, rows.bit_length() - 1)] + [
        ("depth", 1 << k, depth_bits) for k in range(1, layers.bit_length() - 1)
    ]:
        held = jnp.concatenate([held, swap(held, axis, offset)], axis=0)
        bits.append((at, offset))
        at += 1
    return [held], row_bits, depth_bits


def gather_rows(block):
    size = lax.axis_size("col")
    bits, at, held = [], 0, block
    for k in range(1, size.bit_length() - 1):
        held = jnp.concatenate([held, swap(held, "col", 1 << k)], axis=0)
        bits.append((at, 1 << k))
        at += 1
    bits.append((at, 1))
    return [held, swap(held, "col", 1)], bits


def body(x_matrix, tangent, fill_x, fill_t):
    rows, width = x_matrix.shape
    _, _, lead = split(width)
    blocks = lax.axis_size("row") * lax.axis_size("depth")
    packed = pl.pallas_call(
        pack_kernel,
        out_shape=jax.ShapeDtypeStruct((1, lead + rows, 2 * split(width)[0]), jnp.bfloat16),
        in_specs=[HBM] * 4,
        out_specs=VMEM,
        scratch_shapes=[
            pltpu.VMEM((rows, width), jnp.bfloat16),
            pltpu.VMEM((rows, width), jnp.bfloat16),
            pltpu.SMEM(fill_x.shape, jnp.int32),
            pltpu.SMEM(fill_t.shape, jnp.int32),
            pltpu.SemaphoreType.DMA((4,)),
        ],
        compiler_params=PARAMS,
        name="pack",
    )(*(pltpu.with_memory_space_constraint(a, pltpu.HBM) for a in (x_matrix, tangent, fill_x, fill_t)))
    right, row_bits, depth_bits = gather_columns(packed)
    left, col_bits = gather_rows(packed)
    places = (row_bits, depth_bits, col_bits)
    top = aligned(rows)
    firsts = pl.pallas_call(
        functools.partial(first_kernel, (len(left), len(right)), places, width),
        out_shape=jax.ShapeDtypeStruct((1, lead + rows, 3 * split(width)[0]), jnp.bfloat16),
        in_specs=[VMEM] * (len(left) + len(right)),
        out_specs=VMEM,
        scratch_shapes=[pltpu.VMEM((blocks, 2 * top, rows), jnp.bfloat16)],
        compiler_params=PARAMS,
        name="firsts",
    )(*left, *right)
    left, col_bits = gather_rows(firsts)
    return pl.pallas_call(
        functools.partial(last_kernel, (len(left), len(right)), places, width),
        out_shape=jax.ShapeDtypeStruct((rows, width), jnp.float32),
        in_specs=[VMEM] * (len(left) + len(right) + 1),
        out_specs=VMEM,
        scratch_shapes=[pltpu.VMEM((blocks, 3 * top, rows), jnp.bfloat16)],
        compiler_params=PARAMS,
        name="lasts",
    )(*left, *right, packed)


def solution(mesh):
    placed = (P(("row", "depth"), "col"), P(("row", "depth"), "col"), P(), P())
    return jax.shard_map(
        body, mesh=mesh, in_specs=placed, out_specs=P(("row", "depth"), "col"), check_vma=False
    )
```

time: 31.1 us -> 25.3 us (0.81)
  starting transfers between devices: 13.8 us -> 10.6 us
  local copies, waits for them, and re-layouts: 2.92 us -> 0 us
  Pallas kernels: 3.32 us -> 3.71 us
    ppermute x10 -> x8, starting transfers between devices: 13.8 us -> 10.6 us  [swap(): return lax.ppermute(value, axis, [(i, i ^ offset) for i in range(size)])]
    unnamed x8 -> x0, local copies, waits for them, and re-layouts: 2.91 us -> none
    pallas_call x3, Pallas kernels: 3.32 us -> 3.71 us  [the longest x1 1.81 us: body(): pl.pallas_call(functools.partial(last_kernel, (len(left), len(right)), pl...]
    ppermute x10 -> x8, waiting for transfers between devices: 10.6 us -> 10.7 us  [swap(): return lax.ppermute(value, axis, [(i, i ^ offset) for i in range(size)])]
  transfers between devices with their start and end apart: 10 -> 8, of which waited for: 5 -> 5; matrix products, arithmetic and copies ran while one was open for 0% -> 0% of each run, Pallas kernels for 0% -> 0%
where the time goes in v2:
time: 25.3 us; the launch traced here: 25.1 us
  waiting for transfers between devices  10.7 us (42%)
  starting transfers between devices  10.6 us (42%)
  Pallas kernels  3.71 us (15%)
    ppermute x8, waiting for transfers between devices, swap(): return lax.ppermute(value, axis, [(i, i ^ offset) for i in range(size)])  10.7 us
    ppermute x8, starting transfers between devices, swap(): return lax.ppermute(value, axis, [(i, i ^ offset) for i in range(size)])  10.6 us
    pallas_call x1, Pallas kernels, body(): pl.pallas_call(functools.partial(last_kernel, (len(left), len(right)), pl...  1.81 us
    pallas_call x1, Pallas kernels, body(): pl.pallas_call(pack_kernel, out_shape=jax.ShapeDtypeStruct((1, lead + row...  1.07 us
    pallas_call x1, Pallas kernels, body(): pl.pallas_call(functools.partial(first_kernel, (len(left), len(right)), p...  0.83 us
  transfers between devices with their start and end apart: 8, of which 5 were waited for; matrix products, arithmetic and copies ran while one was open for 0% of the time, Pallas kernels for 0%

profile of v2, /device:TPU:0, one launch (start us, length us, event | category | flops | bytes accessed | tf_op | source)
XLA Modules:
  0.0 25.1 jit_solution(15536968588412630421)
XLA Ops:
  0.0 1.1 %pack.1.refs_4_ = bf16[1,88,256]{2,1,0:T(8,128)(2,1)S(1)} custom-call(bf16[72,144]{1,0:T(8,128)(2,1)} %x_hbm.1, bf16[72,144]{1,0:T(8,128)(2,1)} %t_hbm.1, s32[5,5]{1,0:T(8,128)} %fill_x_hbm.1, s32[5,5]{1,0:T(8,128)} %fill_t_hbm.1), custom_call_target="tpu_custom_call" | custom-call | tf_op jit(solution)/shard_map/pack/pallas_call | solution.py:224
  1.1 5.1 %collective-permute-start.4 = (bf16[1,88,256]{2,1,0:T(8,128)(2,1)S(1)}, bf16[1,88,256]{2,1,0:T(8,128)(2,1)S(1)}, u32[]{:S(2)}, u32[]{:S(2)}) collective-permute-start(bf16[1,88,256]{2,1,0:T(8,128)(2,1)S(1)} %pack.1.refs_4_), channel_id=1, source_target_pairs={{0,24},{8,16},{16,8},{24,0},{1,25},{9,17},{17,9},{25,1},{2,26},{10... | collective-permute-start | bytes 135176 | tf_op jit(solution)/shard_map/ppermute | solution.py:29
  6.2 0.0 collective-permute-start.3
  6.2 0.6 %collective-permute-start.2 = (bf16[1,88,256]{2,1,0:T(8,128)(2,1)S(1)}, bf16[1,88,256]{2,1,0:T(8,128)(2,1)S(1)}, u32[]{:S(2)}, u32[]{:S(2)}) collective-permute-start(bf16[1,88,256]{2,1,0:T(8,128)(2,1)S(1)} %pack.1.refs_4_), channel_id=1, source_target_pairs={{0,8},{8,0},{16,24},{24,16},{1,9},{9,1},{17,25},{25,17},{2,10},{10... | collective-permute-start | bytes 135176 | tf_op jit(solution)/shard_map/ppermute | solution.py:29
  6.8 1.6 %collective-permute-start = (bf16[1,88,256]{2,1,0:T(8,128)(2,1)S(1)}, bf16[1,88,256]{2,1,0:T(8,128)(2,1)S(1)}, u32[]{:S(2)}, u32[]{:S(2)}) collective-permute-start(bf16[1,88,256]{2,1,0:T(8,128)(2,1)S(1)} %pack.1.refs_4_), channel_id=1, source_target_pairs={{0,4},{2,6},{4,0},{6,2},{1,5},{3,7},{5,1},{7,3},{8,12},{10,14},{12... | collective-permute-start | bytes 135176 | tf_op jit(solution)/shard_map/ppermute | solution.py:29
  8.5 0.0 collective-permute-done.4
  8.5 2.7 %collective-permute-done.3 = bf16[1,88,256]{2,1,0:T(8,128)(2,1)S(1)} collective-permute-done((bf16[1,88,256]{2,1,0:T(8,128)(2,1)S(1)}, bf16[1,88,256]{2,1,0:T(8,128)(2,1)S(1)}, u32[]{:S(2)}, u32[]{:S(2)}) %collective-permute-start.3) | collective-permute-done | bytes 45088 | tf_op jit(solution)/shard_map/ppermute | solution.py:29
  11.1 0.0 collective-permute-done.2
  11.2 1.6 %collective-permute-start.5 = (bf16[4,88,256]{2,1,0:T(8,128)(2,1)S(1)}, bf16[4,88,256]{2,1,0:T(8,128)(2,1)S(1)}, u32[]{:S(2)}, u32[]{:S(2)}) collective-permute-start(bf16[4,88,256]{2,1,0:T(8,128)(2,1)S(1)} %pad_maximum_fusion.refs_2_), channel_id=1, source_target_pairs={{0,1},{1,0},{2,3},{3,2},{4,5},{5,4},{6,7},{7,6},{8,9},{9,8},{10,11... | collective-permute-start | bytes 540680 | tf_op jit(solution)/shard_map/ppermute | solution.py:29
  12.8 0.0 collective-permute-done
  12.8 0.1 collective-permute-start.1
  12.9 1.3 %collective-permute-done.1.refs_1_ = bf16[2,88,256]{2,1,0:T(8,128)(2,1)S(1)} collective-permute-done((bf16[2,88,256]{2,1,0:T(8,128)(2,1)S(1)}, bf16[2,88,256]{2,1,0:T(8,128)(2,1)S(1)}, u32[]{:S(2)}, u32[]{:S(2)}) %collective-permute-start.1) | collective-permute-done | bytes 90144 | tf_op jit(solution)/shard_map/ppermute | solution.py:29
  14.1 2.6 %collective-permute-done.5.refs_3_ = bf16[4,88,256]{2,1,0:T(8,128)(2,1)S(1)} collective-permute-done((bf16[4,88,256]{2,1,0:T(8,128)(2,1)S(1)}, bf16[4,88,256]{2,1,0:T(8,128)(2,1)S(1)}, u32[]{:S(2)}, u32[]{:S(2)}) %collective-permute-start.5) | collective-permute-done | bytes 180256 | tf_op jit(solution)/shard_map/ppermute | solution.py:29
  16.7 0.8 %firsts.1 = bf16[1,88,384]{2,1,0:T(8,128)(2,1)S(1)} custom-call(bf16[2,88,256]{2,1,0:T(8,128)(2,1)S(1)} %pad_maximum_fusion.2.refs_0_, bf16[2,88,256]{2,1,0:T(8,128)(2,1)S(1)} %collective-permute-done.1.refs_1_, bf16[4,88,256]{2,1,0:T(8,128)(2,1)S(1)} %pad_maximum_fusion.refs_2_, bf16[4,88,256]{2,1,0:T(8,128)(2,1)S(1)} %collective-permute-done.5.refs_3_), custom_call_target="tpu_custom_call" | custom-call | tf_op jit(solution)/shard_map/firsts/pallas_call | solution.py:243
  17.6 1.5 %collective-permute-start.6 = (bf16[1,88,384]{2,1,0:T(8,128)(2,1)S(1)}, bf16[1,88,384]{2,1,0:T(8,128)(2,1)S(1)}, u32[]{:S(2)}, u32[]{:S(2)}) collective-permute-start(bf16[1,88,384]{2,1,0:T(8,128)(2,1)S(1)} %firsts.1), channel_id=1, source_target_pairs={{0,4},{2,6},{4,0},{6,2},{1,5},{3,7},{5,1},{7,3},{8,12},{10,14},{12... | collective-permute-start | bytes 202760 | tf_op jit(solution)/shard_map/ppermute | solution.py:29
  19.1 2.8 %collective-permute-done.6 = bf16[1,88,384]{2,1,0:T(8,128)(2,1)S(1)} collective-permute-done((bf16[1,88,384]{2,1,0:T(8,128)(2,1)S(1)}, bf16[1,88,384]{2,1,0:T(8,128)(2,1)S(1)}, u32[]{:S(2)}, u32[]{:S(2)}) %collective-permute-start.6) | collective-permute-done | bytes 67616 | tf_op jit(solution)/shard_map/ppermute | solution.py:29
  21.9 0.1 collective-permute-start.7
  22.0 1.3 %collective-permute-done.7.refs_1_ = bf16[2,88,384]{2,1,0:T(8,128)(2,1)S(1)} collective-permute-done((bf16[2,88,384]{2,1,0:T(8,128)(2,1)S(1)}, bf16[2,88,384]{2,1,0:T(8,128)(2,1)S(1)}, u32[]{:S(2)}, u32[]{:S(2)}) %collective-permute-start.7) | collective-permute-done | bytes 135200 | tf_op jit(solution)/shard_map/ppermute | solution.py:29
  23.3 1.8 %lasts.1 = f32[72,144]{1,0:T(8,128)} custom-call(bf16[2,88,384]{2,1,0:T(8,128)(2,1)S(1)} %pad_maximum_fusion.1.refs_0_, bf16[2,88,384]{2,1,0:T(8,128)(2,1)S(1)} %collective-permute-done.7.refs_1_, bf16[4,88,256]{2,1,0:T(8,128)(2,1)S(1)} %pad_maximum_fusion.refs_2_, bf16[4,88,256]{2,1,0:T(8,128)(2,1)S(1)} %collective-permute-done.5.refs_3_, ...), custom_call_target="tpu_custom_call" | custom-call | tf_op jit(solution)/shard_map/lasts/pallas_call | solution.py:253
  (3 shorter events, 0.1 us)
Async XLA Ops:
  1.1 7.4 %collective-permute-start.4 = (bf16[1,88,256]{2,1,0:T(8,128)(2,1)S(1)}, bf16[1,88,256]{2,1,0:T(8,128)(2,1)S(1)}, u32[]{:S(2)}, u32[]{:S(2)}) collective-permute-start(bf16[1,88,256]{2,1,0:T(8,128)(2,1)S(1)} %pack.1.refs_4_), channel_id=1, source_target_pairs={{0,24},{8,16},{16,8},{24,0},{1,25},{9,17},{17,9},{25,1},{2,26},{10... | collective-permute-start | bytes 135176 | tf_op jit(solution)/shard_map/ppermute | solution.py:29
  6.2 4.9 %collective-permute-start.3 = (bf16[1,88,256]{2,1,0:T(8,128)(2,1)S(1)}, bf16[1,88,256]{2,1,0:T(8,128)(2,1)S(1)}, u32[]{:S(2)}, u32[]{:S(2)}) collective-permute-start(bf16[1,88,256]{2,1,0:T(8,128)(2,1)S(1)} %pack.1.refs_4_), channel_id=1, source_target_pairs={{0,16},{8,24},{16,0},{24,8},{1,17},{9,25},{17,1},{25,9},{2,18},{10... | collective-permute-start | bytes 135176 | tf_op jit(solution)/shard_map/ppermute | solution.py:29
  6.2 4.9 %collective-permute-start.2 = (bf16[1,88,256]{2,1,0:T(8,128)(2,1)S(1)}, bf16[1,88,256]{2,1,0:T(8,128)(2,1)S(1)}, u32[]{:S(2)}, u32[]{:S(2)}) collective-permute-start(bf16[1,88,256]{2,1,0:T(8,128)(2,1)S(1)} %pack.1.refs_4_), channel_id=1, source_target_pairs={{0,8},{8,0},{16,24},{24,16},{1,9},{9,1},{17,25},{25,17},{2,10},{10... | collective-permute-start | bytes 135176 | tf_op jit(solution)/shard_map/ppermute | solution.py:29
  6.8 5.9 %collective-permute-start = (bf16[1,88,256]{2,1,0:T(8,128)(2,1)S(1)}, bf16[1,88,256]{2,1,0:T(8,128)(2,1)S(1)}, u32[]{:S(2)}, u32[]{:S(2)}) collective-permute-start(bf16[1,88,256]{2,1,0:T(8,128)(2,1)S(1)} %pack.1.refs_4_), channel_id=1, source_target_pairs={{0,4},{2,6},{4,0},{6,2},{1,5},{3,7},{5,1},{7,3},{8,12},{10,14},{12... | collective-permute-start | bytes 135176 | tf_op jit(solution)/shard_map/ppermute | solution.py:29
  11.2 5.6 %collective-permute-start.5 = (bf16[4,88,256]{2,1,0:T(8,128)(2,1)S(1)}, bf16[4,88,256]{2,1,0:T(8,128)(2,1)S(1)}, u32[]{:S(2)}, u32[]{:S(2)}) collective-permute-start(bf16[4,88,256]{2,1,0:T(8,128)(2,1)S(1)} %pad_maximum_fusion.refs_2_), channel_id=1, source_target_pairs={{0,1},{1,0},{2,3},{3,2},{4,5},{5,4},{6,7},{7,6},{8,9},{9,8},{10,11... | collective-permute-start | bytes 540680 | tf_op jit(solution)/shard_map/ppermute | solution.py:29
  12.8 1.4 %collective-permute-start.1 = (bf16[2,88,256]{2,1,0:T(8,128)(2,1)S(1)}, bf16[2,88,256]{2,1,0:T(8,128)(2,1)S(1)}, u32[]{:S(2)}, u32[]{:S(2)}) collective-permute-start(bf16[2,88,256]{2,1,0:T(8,128)(2,1)S(1)} %pad_maximum_fusion.2.refs_0_), channel_id=1, source_target_pairs={{0,2},{2,0},{4,6},{6,4},{1,3},{3,1},{5,7},{7,5},{8,10},{10,8},{12,... | collective-permute-start | bytes 270344 | tf_op jit(solution)/shard_map/ppermute | solution.py:29
  17.6 4.3 %collective-permute-start.6 = (bf16[1,88,384]{2,1,0:T(8,128)(2,1)S(1)}, bf16[1,88,384]{2,1,0:T(8,128)(2,1)S(1)}, u32[]{:S(2)}, u32[]{:S(2)}) collective-permute-start(bf16[1,88,384]{2,1,0:T(8,128)(2,1)S(1)} %firsts.1), channel_id=1, source_target_pairs={{0,4},{2,6},{4,0},{6,2},{1,5},{3,7},{5,1},{7,3},{8,12},{10,14},{12... | collective-permute-start | bytes 202760 | tf_op jit(solution)/shard_map/ppermute | solution.py:29
  21.9 1.4 %collective-permute-start.7 = (bf16[2,88,384]{2,1,0:T(8,128)(2,1)S(1)}, bf16[2,88,384]{2,1,0:T(8,128)(2,1)S(1)}, u32[]{:S(2)}, u32[]{:S(2)}) collective-permute-start(bf16[2,88,384]{2,1,0:T(8,128)(2,1)S(1)} %pad_maximum_fusion.1.refs_0_), channel_id=1, source_target_pairs={{0,2},{2,0},{4,6},{6,4},{1,3},{3,1},{5,7},{7,5},{8,10},{10,8},{12,... | collective-permute-start | bytes 405512 | tf_op jit(solution)/shard_map/ppermute | solution.py:29

commit v3 on v2

--- a/solution.py
+++ b/solution.py
@@ -27,6 +27,11 @@
 def swap(value, axis, offset):
     size = lax.axis_size(axis)
     return lax.ppermute(value, axis, [(i, i ^ offset) for i in range(size)])
+
+
+def turn(value, axis, offset):
+    size = lax.axis_size(axis)
+    return lax.ppermute(value, axis, [((i + offset) % size, i) for i in range(size)])
 
 
 def block_fill(fill_ref, row_start, col_start, rows, width):
@@ -63,7 +68,6 @@
     x_hbm, t_hbm, fill_x_hbm, fill_t_hbm, out_ref, x_ref, t_ref, fill_x_ref, fill_t_ref, sems
 ):
     rows, width = x_ref.shape
-    main, rem, lead = split(width)
     pairs = ((fill_x_hbm, fill_x_ref), (fill_t_hbm, fill_t_ref), (x_hbm, x_ref), (t_hbm, t_ref))
     copies = [pltpu.make_async_copy(src, dst, sems.at[k]) for k, (src, dst) in enumerate(pairs)]
     for copy in copies:
@@ -76,11 +80,28 @@
     copies[2].wait()
     copies[3].wait()
     masked = [x_ref[...].astype(jnp.float32) * masks[0], t_ref[...].astype(jnp.float32) * masks[1]]
-    for k, value in enumerate(masked):
+    pack(out_ref, masked, width)
+
+
+def natural(block, rows, width, total):
+    main, rem, lead = split(width)
+    parts = [block[lead : lead + rows, k * main : (k + 1) * main] for k in range(total)]
+    if rem:
+        rems = unfold(block[:lead], rows, total * rem)
+        parts = [
+            jnp.concatenate([part, rems[:, k * rem : (k + 1) * rem]], axis=1)
+            for k, part in enumerate(parts)
+        ]
+    return parts
+
+
+def pack(out_ref, values, width):
+    main, rem, lead = split(width)
+    for k, value in enumerate(values):
         out_ref[0, lead:, k * main : (k + 1) * main] = value[:, :main].astype(out_ref.dtype)
     if rem:
-        folded = fold(jnp.concatenate([value[:, main:] for value in masked], axis=1))
-        out_ref[0, :FOLD, : folded.shape[1]] = folded.astype(out_ref.dtype)
+        folded = fold(jnp.concatenate([value[:, main:] for value in values], axis=1))
+        out_ref[0, :lead, : folded.shape[1]] = folded.astype(out_ref.dtype)
 
 
 def mains_and_rems(block, rows, rem, lead, total):
@@ -89,8 +110,6 @@
 
 
 def place(bits, position):
-    if isinstance(bits[0], int):
-        return bits[position]
     offset = 0
     for at, weight in bits:
         offset = offset ^ (((position >> at) & 1) * weight)
@@ -184,46 +203,162 @@
         out_ref[:, base : base + size] = 1.5 * own[:, size:].astype(jnp.float32) - 0.5 * total
 
 
-def gather_columns(block):
-    rows, layers = lax.axis_size("row"), lax.axis_size("depth")
-    zs = [swap(block, "row", k) for k in (1, 2, 3)]
-    line = jnp.concatenate([block] + zs, axis=0)
-    gathered = [line, swap(line, "depth", 1)]
-    row_bits, depth_bits = (0, 1, 2, 3, 0, 1, 2, 3), (0, 0, 0, 0, 1, 1, 1, 1)
-
-    if rows == 4 and layers == 2:
-        return gathered, row_bits, depth_bits
-    places = list(zip(row_bits, depth_bits, strict=True))
-    blocks = jnp.concatenate(gathered, axis=0)
-    held = jnp.stack([blocks[places.index((k & 3, k >> 2))] for k in range(8)])
-    row_bits, depth_bits, at = [(0, 1), (1, 2)], [(2, 1)], 3
-    for axis, offset, bits in [("row", 1 << k, row_bits) for k in range(2, rows.bit_length() - 1)] + [
-        ("depth", 1 << k, depth_bits) for k in range(1, layers.bit_length() - 1)
-    ]:
-        held = jnp.concatenate([held, swap(held, axis, offset)], axis=0)
-        bits.append((at, offset))
-        at += 1
-    return [held], row_bits, depth_bits
-
-
-def gather_rows(block):
-    size = lax.axis_size("col")
-    bits, at, held = [], 0, block
-    for k in range(1, size.bit_length() - 1):
-        held = jnp.concatenate([held, swap(held, "col", 1 << k)], axis=0)
-        bits.append((at, 1 << k))
-        at += 1
-    bits.append((at, 1))
-    return [held, swap(held, "col", 1)], bits
+def times(left, right):
+    return jnp.dot(left, right, preferred_element_type=jnp.float32)
+
+
+def add_panels(offsets, mine, others, lhs, rhs, width, rows):
+    my_row, my_depth = lax.axis_index("row"), lax.axis_index("depth")
+    top = aligned(rows)
+    square = cross = jnp.zeros((rows, width), jnp.float32)
+    for k, offset in enumerate(offsets):
+        row = lax.rem(my_row + offset, lax.axis_size("row"))
+        panels = []
+        for a, b in zip(
+            natural(mine[k], rows, width, 2), natural(others[k], rows, width, 2), strict=True
+        ):
+            a, b = a.astype(jnp.float32), b.astype(jnp.float32)
+            halves = [jnp.where(my_depth == 0, a, b), jnp.where(my_depth == 0, b, a)]
+            panels.append(jnp.concatenate(halves, axis=0).astype(jnp.bfloat16))
+        for which, panel in enumerate(panels):
+            rhs[row, which] = panel
+        both = times(lhs[row], panels[0])
+        square += both[:rows]
+        cross += both[top : top + rows] + times(lhs[row, :rows], panels[1])
+    return square, cross
+
+
+def firsts_kernel(offsets, width, own, beside, *refs):
+    mine, others = refs[: len(offsets)], refs[len(offsets) : 2 * len(offsets)]
+    out_ref, low_ref, rhs, lhs = refs[2 * len(offsets) :]
+    rows = own.shape[1] - split(width)[2]
+    top = aligned(rows)
+    my_col = lax.axis_index("col")
+    for ref, across in ((own, 0), (beside, 1)):
+        for k in range(2):
+            col = my_col ^ across ^ (3 * k)
+            for which, part in enumerate(natural(ref[k], rows, width, 2)):
+                lhs[col, which * top : which * top + rows, :] = part
+    square = cross = jnp.zeros((rows, width), jnp.float32)
+    for row_offsets, left, right in zip(offsets, mine, others, strict=True):
+        terms = add_panels(row_offsets, left, right, lhs, rhs, width, rows)
+        square, cross = square + terms[0], cross + terms[1]
+    high = cross.astype(jnp.bfloat16).astype(jnp.float32)
+    pack(out_ref, (high, square), width)
+    low_ref[...] = jnp.zeros_like(low_ref)
+    pack(low_ref, (cross - high,), width)
+
+
+def panel_terms(col, block, low, rhs, width, rows):
+    high, square = natural(block, rows, width, 2)
+    total = times(high, rhs[col, 0]) + times(square, rhs[col, 1])
+    if low is not None:
+        total += times(natural(low, rows, width, 1)[0], rhs[col, 0])
+    return total
+
+
+def early_lasts_kernel(width, held, rhs, out_ref):
+    rows = out_ref.shape[0]
+    my_col = lax.axis_index("col")
+    out_ref[...] = panel_terms(my_col, held[0], held[2], rhs, width, rows) + panel_terms(
+        my_col ^ 3, held[1], None, rhs, width, rows
+    )
+
+
+def late_lasts_kernel(width, other, rhs, early, own_ref, out_ref):
+    rows = out_ref.shape[0]
+    my_col = lax.axis_index("col")
+    total = early[...] + panel_terms(my_col ^ 1, other[0], other[2], rhs, width, rows)
+    total += panel_terms(my_col ^ 2, other[1], None, rhs, width, rows)
+    own = natural(own_ref[0], rows, width, 2)[1].astype(jnp.float32)
+    out_ref[...] = 1.5 * own - 0.5 * total
+
+
+def call(kernel, name, out_shape, operands, scratch=(), **kwargs):
+    return pl.pallas_call(
+        kernel,
+        out_shape=out_shape,
+        in_specs=[VMEM] * len(operands),
+        out_specs=jax.tree.map(lambda _: VMEM, out_shape),
+        scratch_shapes=list(scratch),
+        compiler_params=PARAMS,
+        name=name,
+        **kwargs,
+    )(*operands)
+
+
+def fast_body(block, rows, width):
+    grid, top = lax.axis_size("row"), aligned(rows)
+    shape = jax.ShapeDtypeStruct
+    opposite = turn(block, "row", 2)
+    line = jnp.concatenate([turn(block, "row", 1), turn(block, "row", 3), block], axis=0)
+    side_line = swap(line, "depth", 1)
+    side_opposite = swap(opposite, "depth", 1)
+    held = jnp.concatenate([block, swap(block, "col", 3)], axis=0)
+    beside = swap(held, "col", 1)
+    panels = shape((grid, 2, width, width), jnp.bfloat16)
+    firsts, low, rhs = call(
+        functools.partial(firsts_kernel, ((1, 3, 0), (2,)), width),
+        "firsts",
+        (shape(block.shape, block.dtype), shape(block.shape, block.dtype), panels),
+        (held, beside, line, opposite, side_line, side_opposite),
+        [pltpu.VMEM((grid, 2 * top, width), jnp.bfloat16)],
+    )
+    held = jnp.concatenate([firsts, swap(firsts, "col", 3), low], axis=0)
+    other = swap(held, "col", 1)
+    out = shape((rows, width), jnp.float32)
+    early = call(
+        functools.partial(early_lasts_kernel, width), "early_lasts", out, (held, rhs)
+    )
+    return call(
+        functools.partial(late_lasts_kernel, width), "late_lasts", out, (other, rhs, early, block)
+    )
+
+
+def gather(block, axes):
+    held, at, bits = block, 0, []
+    for axis, steps in axes:
+        meaning = []
+        for step in steps:
+            held = jnp.concatenate([held, swap(held, axis, step)], axis=0)
+            meaning.append((at, step))
+            at += 1
+        bits.append(meaning)
+    return [held], bits
+
+
+def general_body(block, rows, width):
+    def steps(axis):
+        return [1 << k for k in range(lax.axis_size(axis).bit_length() - 1)]
+
+    right, (row_bits, depth_bits) = gather(block, [(a, steps(a)) for a in ("row", "depth")])
+    left, (col_bits,) = gather(block, [("col", steps("col")[::-1])])
+    places = (row_bits, depth_bits, col_bits)
+    blocks, top = right[0].shape[0], aligned(rows)
+    _, _, lead = split(width)
+    firsts = call(
+        functools.partial(first_kernel, (1, 1), places, width),
+        "firsts",
+        jax.ShapeDtypeStruct((1, lead + rows, 3 * split(width)[0]), jnp.bfloat16),
+        (*left, *right),
+        [pltpu.VMEM((blocks, 2 * top, rows), jnp.bfloat16)],
+    )
+    left, (col_bits,) = gather(firsts, [("col", steps("col")[::-1])])
+    return call(
+        functools.partial(last_kernel, (1, 1), places, width),
+        "lasts",
+        jax.ShapeDtypeStruct((rows, width), jnp.float32),
+        (*left, *right, block),
+        [pltpu.VMEM((blocks, 3 * top, rows), jnp.bfloat16)],
+    )
 
 
 def body(x_matrix, tangent, fill_x, fill_t):
     rows, width = x_matrix.shape
-    _, _, lead = split(width)
-    blocks = lax.axis_size("row") * lax.axis_size("depth")
-    packed = pl.pallas_call(
+    main, _, lead = split(width)
+    block = pl.pallas_call(
         pack_kernel,
-        out_shape=jax.ShapeDtypeStruct((1, lead + rows, 2 * split(width)[0]), jnp.bfloat16),
+        out_shape=jax.ShapeDtypeStruct((1, lead + rows, 2 * main), jnp.bfloat16),
         in_specs=[HBM] * 4,
         out_specs=VMEM,
         scratch_shapes=[
@@ -236,29 +371,8 @@
         compiler_params=PARAMS,
         name="pack",
     )(*(pltpu.with_memory_space_constraint(a, pltpu.HBM) for a in (x_matrix, tangent, fill_x, fill_t)))
-    right, row_bits, depth_bits = gather_columns(packed)
-    left, col_bits = gather_rows(packed)
-    places = (row_bits, depth_bits, col_bits)
-    top = aligned(rows)
-    firsts = pl.pallas_call(
-        functools.partial(first_kernel, (len(left), len(right)), places, width),
-        out_shape=jax.ShapeDtypeStruct((1, lead + rows, 3 * split(width)[0]), jnp.bfloat16),
-        in_specs=[VMEM] * (len(left) + len(right)),
-        out_specs=VMEM,
-        scratch_shapes=[pltpu.VMEM((blocks, 2 * top, rows), jnp.bfloat16)],
-        compiler_params=PARAMS,
-        name="firsts",
-    )(*left, *right)
-    left, col_bits = gather_rows(firsts)
-    return pl.pallas_call(
-        functools.partial(last_kernel, (len(left), len(right)), places, width),
-        out_shape=jax.ShapeDtypeStruct((rows, width), jnp.float32),
-        in_specs=[VMEM] * (len(left) + len(right) + 1),
-        out_specs=VMEM,
-        scratch_shapes=[pltpu.VMEM((blocks, 3 * top, rows), jnp.bfloat16)],
-        compiler_params=PARAMS,
-        name="lasts",
-    )(*left, *right, packed)
+    sizes = tuple(lax.axis_size(a) for a in ("row", "col", "depth"))
+    return (fast_body if sizes == (4, 4, 2) else general_body)(block, rows, width)
 
 
 def solution(mesh):

time: 25.3 us -> 22.5 us (0.89)
  waiting for transfers between devices: 10.7 us -> 9.56 us
  Pallas kernels: 3.71 us -> 2.88 us
  starting transfers between devices: 10.6 us -> 9.79 us
    ppermute x8 -> x6, starting transfers between devices: 10.6 us -> 3.67 us  [swap(): return lax.ppermute(value, axis, [(i, i ^ offset) for i in range(size)])]
    ppermute x0 -> x3, starting transfers between devices: none -> 6.11 us  [turn(): lax.ppermute(value, axis, [((i + offset) % size, i) for i in range(size)])]
    ppermute x8 -> x6, waiting for transfers between devices: 10.7 us -> 8.16 us  [swap(): return lax.ppermute(value, axis, [(i, i ^ offset) for i in range(size)])]
    ppermute x0 -> x3, waiting for transfers between devices: none -> 1.4 us  [turn(): lax.ppermute(value, axis, [((i + offset) % size, i) for i in range(size)])]
    pallas_call x2 -> x3, Pallas kernels: 2.64 us -> 1.81 us  [call(): pl.pallas_call(kernel, out_shape=out_shape, in_specs=[VMEM] * len(operand...]
  transfers between devices with their start and end apart: 8 -> 9, of which waited for: 5 -> 6; matrix products, arithmetic and copies ran while one was open for 0% -> 0% of each run, Pallas kernels for 0% -> 1%
where the time goes in v3:
time: 22.5 us; the launch traced here: 22.3 us
  starting transfers between devices  9.79 us (44%)
  waiting for transfers between devices  9.56 us (42%)
  Pallas kernels  2.88 us (13%)
    ppermute x6, waiting for transfers between devices, swap(): return lax.ppermute(value, axis, [(i, i ^ offset) for i in range(size)])  8.16 us
    ppermute x3, starting transfers between devices, turn(): lax.ppermute(value, axis, [((i + offset) % size, i) for i in range(size)])  6.11 us
    ppermute x6, starting transfers between devices, swap(): return lax.ppermute(value, axis, [(i, i ^ offset) for i in range(size)])  3.67 us
    pallas_call x3, Pallas kernels, call(): pl.pallas_call(kernel, out_shape=out_shape, in_specs=[VMEM] * len(operand...  1.81 us
    ppermute x3, waiting for transfers between devices, turn(): lax.ppermute(value, axis, [((i + offset) % size, i) for i in range(size)])  1.4 us
    pallas_call x1, Pallas kernels, body(): pl.pallas_call(pack_kernel, out_shape=jax.ShapeDtypeStruct((1, lead + row...  1.07 us
  transfers between devices with their start and end apart: 9, of which 6 were waited for; matrix products, arithmetic and copies ran while one was open for 0% of the time, Pallas kernels for 1%

profile of v3, /device:TPU:0, one launch (start us, length us, event | category | flops | bytes accessed | tf_op | source)
XLA Modules:
  0.0 22.3 jit_solution(10292584071590229572)
XLA Ops:
  0.0 1.1 %pack.1.own_ref = bf16[1,88,256]{2,1,0:T(8,128)(2,1)S(1)} custom-call(bf16[72,144]{1,0:T(8,128)(2,1)} %x_hbm.1, bf16[72,144]{1,0:T(8,128)(2,1)} %t_hbm.1, s32[5,5]{1,0:T(8,128)} %fill_x_hbm.1, s32[5,5]{1,0:T(8,128)} %fill_t_hbm.1), custom_call_target="tpu_custom_call" | custom-call | tf_op jit(solution)/shard_map/pack/pallas_call | solution.py:359
  1.1 3.1 %collective-permute-start.3 = (bf16[1,88,256]{2,1,0:T(8,128)(2,1)S(1)}, bf16[1,88,256]{2,1,0:T(8,128)(2,1)S(1)}, u32[]{:S(2)}, u32[]{:S(2)}) collective-permute-start(bf16[1,88,256]{2,1,0:T(8,128)(2,1)S(1)} %pack.1.own_ref), channel_id=1, source_target_pairs={{24,0},{0,8},{8,16},{16,24},{25,1},{1,9},{9,17},{17,25},{26,2},{2,... | collective-permute-start | bytes 135176 | tf_op jit(solution)/shard_map/ppermute | solution.py:34
  4.2 2.1 %collective-permute-start.2 = (bf16[1,88,256]{2,1,0:T(8,128)(2,1)S(1)}, bf16[1,88,256]{2,1,0:T(8,128)(2,1)S(1)}, u32[]{:S(2)}, u32[]{:S(2)}) collective-permute-start(bf16[1,88,256]{2,1,0:T(8,128)(2,1)S(1)} %pack.1.own_ref), channel_id=1, source_target_pairs={{8,0},{16,8},{24,16},{0,24},{9,1},{17,9},{25,17},{1,25},{10,2},{18... | collective-permute-start | bytes 135176 | tf_op jit(solution)/shard_map/ppermute | solution.py:34
  6.2 0.9 %collective-permute-start.4 = (bf16[1,88,256]{2,1,0:T(8,128)(2,1)S(1)}, bf16[1,88,256]{2,1,0:T(8,128)(2,1)S(1)}, u32[]{:S(2)}, u32[]{:S(2)}) collective-permute-start(bf16[1,88,256]{2,1,0:T(8,128)(2,1)S(1)} %pack.1.own_ref), channel_id=1, source_target_pairs={{16,0},{24,8},{0,16},{8,24},{17,1},{25,9},{1,17},{9,25},{18,2},{26... | collective-permute-start | bytes 135176 | tf_op jit(solution)/shard_map/ppermute | solution.py:34
  7.2 0.1 collective-permute-start
  7.3 1.0 %collective-permute-done.3 = bf16[1,88,256]{2,1,0:T(8,128)(2,1)S(1)} collective-permute-done((bf16[1,88,256]{2,1,0:T(8,128)(2,1)S(1)}, bf16[1,88,256]{2,1,0:T(8,128)(2,1)S(1)}, u32[]{:S(2)}, u32[]{:S(2)}) %collective-permute-start.3) | collective-permute-done | bytes 45088 | tf_op jit(solution)/shard_map/ppermute | solution.py:34
  8.3 0.4 %collective-permute-done.2 = bf16[1,88,256]{2,1,0:T(8,128)(2,1)S(1)} collective-permute-done((bf16[1,88,256]{2,1,0:T(8,128)(2,1)S(1)}, bf16[1,88,256]{2,1,0:T(8,128)(2,1)S(1)}, u32[]{:S(2)}, u32[]{:S(2)}) %collective-permute-start.2) | collective-permute-done | bytes 45088 | tf_op jit(solution)/shard_map/ppermute | solution.py:34
  8.7 1.6 %collective-permute-start.5 = (bf16[3,88,256]{2,1,0:T(8,128)(2,1)S(1)}, bf16[3,88,256]{2,1,0:T(8,128)(2,1)S(1)}, u32[]{:S(2)}, u32[]{:S(2)}) collective-permute-start(bf16[3,88,256]{2,1,0:T(8,128)(2,1)S(1)} %pad_maximum_fusion.refs_0_), channel_id=1, source_target_pairs={{0,1},{1,0},{2,3},{3,2},{4,5},{5,4},{6,7},{7,6},{8,9},{9,8},{10,11... | collective-permute-start | bytes 405512 | tf_op jit(solution)/shard_map/ppermute | solution.py:29
  10.3 0.8 %collective-permute-done = bf16[1,88,256]{2,1,0:T(8,128)(2,1)S(1)} collective-permute-done((bf16[1,88,256]{2,1,0:T(8,128)(2,1)S(1)}, bf16[1,88,256]{2,1,0:T(8,128)(2,1)S(1)}, u32[]{:S(2)}, u32[]{:S(2)}) %collective-permute-start) | collective-permute-done | bytes 45088 | tf_op jit(solution)/shard_map/ppermute | solution.py:29
  11.1 0.2 %collective-permute-start.1 = (bf16[2,88,256]{2,1,0:T(8,128)(2,1)S(1)}, bf16[2,88,256]{2,1,0:T(8,128)(2,1)S(1)}, u32[]{:S(2)}, u32[]{:S(2)}) collective-permute-start(bf16[2,88,256]{2,1,0:T(8,128)(2,1)S(1)} %pad_maximum_fusion.1.own), channel_id=1, source_target_pairs={{0,2},{2,0},{4,6},{6,4},{1,3},{3,1},{5,7},{7,5},{8,10},{10,8},{12,... | collective-permute-start | bytes 270344 | tf_op jit(solution)/shard_map/ppermute | solution.py:29
  11.3 0.0 collective-permute-done.4.refs_1_
  11.3 1.5 %collective-permute-start.6 = (bf16[1,88,256]{2,1,0:T(8,128)(2,1)S(1)}, bf16[1,88,256]{2,1,0:T(8,128)(2,1)S(1)}, u32[]{:S(2)}, u32[]{:S(2)}) collective-permute-start(bf16[1,88,256]{2,1,0:T(8,128)(2,1)S(1)} %collective-permute-done.4.refs_1_), channel_id=1, source_target_pairs={{0,1},{1,0},{2,3},{3,2},{4,5},{5,4},{6,7},{7,6},{8,9},{9,8},{10,11... | collective-permute-start | bytes 135176 | tf_op jit(solution)/shard_map/ppermute | solution.py:29
  12.9 2.5 %collective-permute-done.6.refs_3_ = bf16[1,88,256]{2,1,0:T(8,128)(2,1)S(1)} collective-permute-done((bf16[1,88,256]{2,1,0:T(8,128)(2,1)S(1)}, bf16[1,88,256]{2,1,0:T(8,128)(2,1)S(1)}, u32[]{:S(2)}, u32[]{:S(2)}) %collective-permute-start.6) | collective-permute-done | bytes 45088 | tf_op jit(solution)/shard_map/ppermute | solution.py:29
  15.4 0.0 collective-permute-done.1.beside
  15.4 0.0 collective-permute-done.5.refs_2_
  15.4 0.6 %firsts.1 = (bf16[1,88,256]{2,1,0:T(8,128)(2,1)S(1)}, bf16[1,88,256]{2,1,0:T(8,128)(2,1)S(1)}, bf16[4,2,144,144]{3,2,1,0:T(8,128)(2,1)S(1)}) custom-call(bf16[2,88,256]{2,1,0:T(8,128)(2,1)S(1)} %pad_maximum_fusion.1.own, bf16[2,88,256]{2,1,0:T(8,128)(2,1)S(1)} %collective-permute-done.1.beside, bf16[3,88,256]{2,1,0:T(8,128)(2,1)S(1)} %pad_maximum_fusion.refs_0_, ...), custom_call_target="tpu_custom_call" | custom-call | tf_op jit(solution)/shard_map/firsts/pallas_call | solution.py:278
  16.0 0.1 collective-permute-start.7
  16.1 3.9 %collective-permute-done.7 = bf16[1,88,256]{2,1,0:T(8,128)(2,1)S(1)} collective-permute-done((bf16[1,88,256]{2,1,0:T(8,128)(2,1)S(1)}, bf16[1,88,256]{2,1,0:T(8,128)(2,1)S(1)}, u32[]{:S(2)}, u32[]{:S(2)}) %collective-permute-start.7) | collective-permute-done | bytes 45088 | tf_op jit(solution)/shard_map/ppermute | solution.py:29
  20.0 0.2 collective-permute-start.8
  20.1 0.3 %early_lasts.1.early = f32[72,144]{1,0:T(8,128)S(1)} custom-call(bf16[3,88,256]{2,1,0:T(8,128)(2,1)S(1)} %constant_dynamic-update-slice_fusion.held, bf16[4,2,144,144]{3,2,1,0:T(8,128)(2,1)S(1)} %get-tuple-element.10.rhs), custom_call_target="tpu_custom_call" | custom-call | tf_op jit(solution)/shard_map/early_lasts/pallas_call | solution.py:278
  20.4 0.9 %collective-permute-done.8.other = bf16[3,88,256]{2,1,0:T(8,128)(2,1)S(1)} collective-permute-done((bf16[3,88,256]{2,1,0:T(8,128)(2,1)S(1)}, bf16[3,88,256]{2,1,0:T(8,128)(2,1)S(1)}, u32[]{:S(2)}, u32[]{:S(2)}) %collective-permute-start.8) | collective-permute-done | bytes 135200 | tf_op jit(solution)/shard_map/ppermute | solution.py:29
  21.4 0.9 %late_lasts.1 = f32[72,144]{1,0:T(8,128)} custom-call(bf16[3,88,256]{2,1,0:T(8,128)(2,1)S(1)} %collective-permute-done.8.other, bf16[4,2,144,144]{3,2,1,0:T(8,128)(2,1)S(1)} %get-tuple-element.10.rhs, f32[72,144]{1,0:T(8,128)S(1)} %early_lasts.1.early, bf16[1,88,256]{2,1,0:T(8,128)(2,1)S(1)} %pack.1.own_ref), custom_call_target="tpu_custom_call" | custom-call | tf_op jit(solution)/shard_map/late_lasts/pallas_call | solution.py:278
  (5 shorter events, 0.0 us)
Async XLA Ops:
  1.1 7.2 %collective-permute-start.3 = (bf16[1,88,256]{2,1,0:T(8,128)(2,1)S(1)}, bf16[1,88,256]{2,1,0:T(8,128)(2,1)S(1)}, u32[]{:S(2)}, u32[]{:S(2)}) collective-permute-start(bf16[1,88,256]{2,1,0:T(8,128)(2,1)S(1)} %pack.1.own_ref), channel_id=1, source_target_pairs={{24,0},{0,8},{8,16},{16,24},{25,1},{1,9},{9,17},{17,25},{26,2},{2,... | collective-permute-start | bytes 135176 | tf_op jit(solution)/shard_map/ppermute | solution.py:34
  4.2 4.5 %collective-permute-start.2 = (bf16[1,88,256]{2,1,0:T(8,128)(2,1)S(1)}, bf16[1,88,256]{2,1,0:T(8,128)(2,1)S(1)}, u32[]{:S(2)}, u32[]{:S(2)}) collective-permute-start(bf16[1,88,256]{2,1,0:T(8,128)(2,1)S(1)} %pack.1.own_ref), channel_id=1, source_target_pairs={{8,0},{16,8},{24,16},{0,24},{9,1},{17,9},{25,17},{1,25},{10,2},{18... | collective-permute-start | bytes 135176 | tf_op jit(solution)/shard_map/ppermute | solution.py:34
  6.2 5.1 %collective-permute-start.4 = (bf16[1,88,256]{2,1,0:T(8,128)(2,1)S(1)}, bf16[1,88,256]{2,1,0:T(8,128)(2,1)S(1)}, u32[]{:S(2)}, u32[]{:S(2)}) collective-permute-start(bf16[1,88,256]{2,1,0:T(8,128)(2,1)S(1)} %pack.1.own_ref), channel_id=1, source_target_pairs={{16,0},{24,8},{0,16},{8,24},{17,1},{25,9},{1,17},{9,25},{18,2},{26... | collective-permute-start | bytes 135176 | tf_op jit(solution)/shard_map/ppermute | solution.py:34
  7.2 3.9 %collective-permute-start = (bf16[1,88,256]{2,1,0:T(8,128)(2,1)S(1)}, bf16[1,88,256]{2,1,0:T(8,128)(2,1)S(1)}, u32[]{:S(2)}, u32[]{:S(2)}) collective-permute-start(bf16[1,88,256]{2,1,0:T(8,128)(2,1)S(1)} %pack.1.own_ref), channel_id=1, source_target_pairs={{0,6},{2,4},{4,2},{6,0},{1,7},{3,5},{5,3},{7,1},{8,14},{10,12},{12... | collective-permute-start | bytes 135176 | tf_op jit(solution)/shard_map/ppermute | solution.py:29
  8.7 6.7 %collective-permute-start.5 = (bf16[3,88,256]{2,1,0:T(8,128)(2,1)S(1)}, bf16[3,88,256]{2,1,0:T(8,128)(2,1)S(1)}, u32[]{:S(2)}, u32[]{:S(2)}) collective-permute-start(bf16[3,88,256]{2,1,0:T(8,128)(2,1)S(1)} %pad_maximum_fusion.refs_0_), channel_id=1, source_target_pairs={{0,1},{1,0},{2,3},{3,2},{4,5},{5,4},{6,7},{7,6},{8,9},{9,8},{10,11... | collective-permute-start | bytes 405512 | tf_op jit(solution)/shard_map/ppermute | solution.py:29
  11.1 4.3 %collective-permute-start.1 = (bf16[2,88,256]{2,1,0:T(8,128)(2,1)S(1)}, bf16[2,88,256]{2,1,0:T(8,128)(2,1)S(1)}, u32[]{:S(2)}, u32[]{:S(2)}) collective-permute-start(bf16[2,88,256]{2,1,0:T(8,128)(2,1)S(1)} %pad_maximum_fusion.1.own), channel_id=1, source_target_pairs={{0,2},{2,0},{4,6},{6,4},{1,3},{3,1},{5,7},{7,5},{8,10},{10,8},{12,... | collective-permute-start | bytes 270344 | tf_op jit(solution)/shard_map/ppermute | solution.py:29
  11.3 4.0 %collective-permute-start.6 = (bf16[1,88,256]{2,1,0:T(8,128)(2,1)S(1)}, bf16[1,88,256]{2,1,0:T(8,128)(2,1)S(1)}, u32[]{:S(2)}, u32[]{:S(2)}) collective-permute-start(bf16[1,88,256]{2,1,0:T(8,128)(2,1)S(1)} %collective-permute-done.4.refs_1_), channel_id=1, source_target_pairs={{0,1},{1,0},{2,3},{3,2},{4,5},{5,4},{6,7},{7,6},{8,9},{9,8},{10,11... | collective-permute-start | bytes 135176 | tf_op jit(solution)/shard_map/ppermute | solution.py:29
  16.0 4.0 %collective-permute-start.7 = (bf16[1,88,256]{2,1,0:T(8,128)(2,1)S(1)}, bf16[1,88,256]{2,1,0:T(8,128)(2,1)S(1)}, u32[]{:S(2)}, u32[]{:S(2)}) collective-permute-start(bf16[1,88,256]{2,1,0:T(8,128)(2,1)S(1)} %get-tuple-element.8), channel_id=1, source_target_pairs={{0,6},{2,4},{4,2},{6,0},{1,7},{3,5},{5,3},{7,1},{8,14},{10,12},{12... | collective-permute-start | bytes 135176 | tf_op jit(solution)/shard_map/ppermute | solution.py:29
  20.0 1.4 %collective-permute-start.8 = (bf16[3,88,256]{2,1,0:T(8,128)(2,1)S(1)}, bf16[3,88,256]{2,1,0:T(8,128)(2,1)S(1)}, u32[]{:S(2)}, u32[]{:S(2)}) collective-permute-start(bf16[3,88,256]{2,1,0:T(8,128)(2,1)S(1)} %constant_dynamic-update-slice_fusion.held), channel_id=1, source_target_pairs={{0,2},{2,0},{4,6},{6,4},{1,3},{3,1},{5,7},{7,5},{8,10},{10,8},{12,... | collective-permute-start | bytes 405512 | tf_op jit(solution)/shard_map/ppermute | solution.py:29

commit v4 on v3

--- a/solution.py
+++ b/solution.py
@@ -37,17 +37,18 @@
 def block_fill(fill_ref, row_start, col_start, rows, width):
     count = fill_ref.shape[0]
     row_ids = row_start + lax.broadcasted_iota(jnp.int32, (rows, width), 0)
-    col_ids = col_start + lax.broadcasted_iota(jnp.int32, (rows, width), 1)
+    col_ids = col_start + lax.broadcasted_iota(jnp.int32, (1, width), 1)
     first_row, first_col = row_start // BLOCK, col_start // BLOCK
-    mask = jnp.zeros((rows, width), jnp.float32)
+    mask = None
     for i in range((rows - 2) // BLOCK + 2):
-        row_at = first_row + i
-        in_row = (row_ids >= row_at * BLOCK) & (row_ids < (row_at + 1) * BLOCK)
+        row_at = jnp.minimum(first_row + i, count - 1)
+        flags = None
         for j in range((width - 2) // BLOCK + 2):
-            col_at = first_col + j
-            here = in_row & (col_ids >= col_at * BLOCK) & (col_ids < (col_at + 1) * BLOCK)
-            flag = fill_ref[jnp.minimum(row_at, count - 1), jnp.minimum(col_at, count - 1)]
-            mask = jnp.where(here, flag.astype(jnp.float32), mask)
+            flag = fill_ref[row_at, jnp.minimum(first_col + j, count - 1)].astype(jnp.float32)
+            passed = col_ids >= (first_col + j) * BLOCK
+            flags = jnp.where(passed, flag, 0.0 if flags is None else flags)
+        flags = jnp.broadcast_to(flags, (rows, width))
+        mask = flags if mask is None else jnp.where(row_ids >= (first_row + i) * BLOCK, flags, mask)
     return mask
 
 
@@ -257,19 +258,24 @@
     return total
 
 
-def early_lasts_kernel(width, held, rhs, out_ref):
+def near_lasts_kernel(width, mine, other, rhs, out_ref):
     rows = out_ref.shape[0]
     my_col = lax.axis_index("col")
-    out_ref[...] = panel_terms(my_col, held[0], held[2], rhs, width, rows) + panel_terms(
-        my_col ^ 3, held[1], None, rhs, width, rows
-    )
-
-
-def late_lasts_kernel(width, other, rhs, early, own_ref, out_ref):
+    out_ref[...] = panel_terms(my_col, mine[0], mine[1], rhs, width, rows) + panel_terms(
+        my_col ^ 1, other[0], other[1], rhs, width, rows
+    )
+
+
+def far_lasts_kernel(width, across, rhs, early, out_ref):
     rows = out_ref.shape[0]
     my_col = lax.axis_index("col")
-    total = early[...] + panel_terms(my_col ^ 1, other[0], other[2], rhs, width, rows)
-    total += panel_terms(my_col ^ 2, other[1], None, rhs, width, rows)
+    out_ref[...] = early[...] + panel_terms(my_col ^ 3, across[0], None, rhs, width, rows)
+
+
+def late_lasts_kernel(width, across, rhs, early, own_ref, out_ref):
+    rows = out_ref.shape[0]
+    my_col = lax.axis_index("col")
+    total = early[...] + panel_terms(my_col ^ 2, across[0], None, rhs, width, rows)
     own = natural(own_ref[0], rows, width, 2)[1].astype(jnp.float32)
     out_ref[...] = 1.5 * own - 0.5 * total
 
@@ -304,14 +310,17 @@
         (held, beside, line, opposite, side_line, side_opposite),
         [pltpu.VMEM((grid, 2 * top, width), jnp.bfloat16)],
     )
-    held = jnp.concatenate([firsts, swap(firsts, "col", 3), low], axis=0)
-    other = swap(held, "col", 1)
+    across = swap(firsts, "col", 3)
     out = shape((rows, width), jnp.float32)
-    early = call(
-        functools.partial(early_lasts_kernel, width), "early_lasts", out, (held, rhs)
-    )
+    mine = jnp.concatenate([firsts, low], axis=0)
+    near = (mine, swap(mine, "col", 1))
+    total = call(functools.partial(near_lasts_kernel, width), "near_lasts", out, (*near, rhs))
+    total = call(functools.partial(far_lasts_kernel, width), "far_lasts", out, (across, rhs, total))
     return call(
-        functools.partial(late_lasts_kernel, width), "late_lasts", out, (other, rhs, early, block)
+        functools.partial(late_lasts_kernel, width),
+        "late_lasts",
+        out,
+        (swap(across, "col", 1), rhs, total, block),
     )
 
 

time: 22.5 us -> 21.9 us (0.973)
  waiting for transfers between devices: 9.56 us -> 6.95 us
  starting transfers between devices: 9.79 us -> 11.7 us
    ppermute x6 -> x7, waiting for transfers between devices: 8.16 us -> 5.55 us  [swap(): return lax.ppermute(value, axis, [(i, i ^ offset) for i in range(size)])]
    ppermute x6 -> x7, starting transfers between devices: 3.67 us -> 5.55 us  [swap(): return lax.ppermute(value, axis, [(i, i ^ offset) for i in range(size)])]
    pallas_call x3 -> x4, Pallas kernels: 1.81 us -> 2.06 us  [call(): pl.pallas_call(kernel, out_shape=out_shape, in_specs=[VMEM] * len(operand...]
  transfers between devices with their start and end apart: 9 -> 10, of which waited for: 6 -> 6; matrix products, arithmetic and copies ran while one was open for 0% -> 0% of each run, Pallas kernels for 1% -> 3%
where the time goes in v4:
time: 21.9 us; the launch traced here: 21.7 us
  starting transfers between devices  11.7 us (53%)
  waiting for transfers between devices  6.95 us (32%)
  Pallas kernels  3.03 us (14%)
    ppermute x3, starting transfers between devices, turn(): lax.ppermute(value, axis, [((i + offset) % size, i) for i in range(size)])  6.11 us
    ppermute x7, waiting for transfers between devices, swap(): return lax.ppermute(value, axis, [(i, i ^ offset) for i in range(size)])  5.55 us
    ppermute x7, starting transfers between devices, swap(): return lax.ppermute(value, axis, [(i, i ^ offset) for i in range(size)])  5.55 us
    pallas_call x4, Pallas kernels, call(): pl.pallas_call(kernel, out_shape=out_shape, in_specs=[VMEM] * len(operand...  2.06 us
    ppermute x3, waiting for transfers between devices, turn(): lax.ppermute(value, axis, [((i + offset) % size, i) for i in range(size)])  1.4 us
    pallas_call x1, Pallas kernels, body(): pl.pallas_call(pack_kernel, out_shape=jax.ShapeDtypeStruct((1, lead + row...  0.97 us
  transfers between devices with their start and end apart: 10, of which 6 were waited for; matrix products, arithmetic and copies ran while one was open for 0% of the time, Pallas kernels for 3%

profile of v4, /device:TPU:0, one launch (start us, length us, event | category | flops | bytes accessed | tf_op | source)
XLA Modules:
  0.0 21.7 jit_solution(14658346707499267335)
XLA Ops:
  0.0 1.0 %pack.1.own_ref = bf16[1,88,256]{2,1,0:T(8,128)(2,1)S(1)} custom-call(bf16[72,144]{1,0:T(8,128)(2,1)} %x_hbm.1, bf16[72,144]{1,0:T(8,128)(2,1)} %t_hbm.1, s32[5,5]{1,0:T(8,128)} %fill_x_hbm.1, s32[5,5]{1,0:T(8,128)} %fill_t_hbm.1), custom_call_target="tpu_custom_call" | custom-call | tf_op jit(solution)/shard_map/pack/pallas_call | solution.py:368
  1.0 3.1 %collective-permute-start.3 = (bf16[1,88,256]{2,1,0:T(8,128)(2,1)S(1)}, bf16[1,88,256]{2,1,0:T(8,128)(2,1)S(1)}, u32[]{:S(2)}, u32[]{:S(2)}) collective-permute-start(bf16[1,88,256]{2,1,0:T(8,128)(2,1)S(1)} %pack.1.own_ref), channel_id=1, source_target_pairs={{24,0},{0,8},{8,16},{16,24},{25,1},{1,9},{9,17},{17,25},{26,2},{2,... | collective-permute-start | bytes 135176 | tf_op jit(solution)/shard_map/ppermute | solution.py:34
  4.1 2.1 %collective-permute-start.2 = (bf16[1,88,256]{2,1,0:T(8,128)(2,1)S(1)}, bf16[1,88,256]{2,1,0:T(8,128)(2,1)S(1)}, u32[]{:S(2)}, u32[]{:S(2)}) collective-permute-start(bf16[1,88,256]{2,1,0:T(8,128)(2,1)S(1)} %pack.1.own_ref), channel_id=1, source_target_pairs={{8,0},{16,8},{24,16},{0,24},{9,1},{17,9},{25,17},{1,25},{10,2},{18... | collective-permute-start | bytes 135176 | tf_op jit(solution)/shard_map/ppermute | solution.py:34
  6.1 0.9 %collective-permute-start.4 = (bf16[1,88,256]{2,1,0:T(8,128)(2,1)S(1)}, bf16[1,88,256]{2,1,0:T(8,128)(2,1)S(1)}, u32[]{:S(2)}, u32[]{:S(2)}) collective-permute-start(bf16[1,88,256]{2,1,0:T(8,128)(2,1)S(1)} %pack.1.own_ref), channel_id=1, source_target_pairs={{16,0},{24,8},{0,16},{8,24},{17,1},{25,9},{1,17},{9,25},{18,2},{26... | collective-permute-start | bytes 135176 | tf_op jit(solution)/shard_map/ppermute | solution.py:34
  7.1 0.1 collective-permute-start
  7.2 1.0 %collective-permute-done.3 = bf16[1,88,256]{2,1,0:T(8,128)(2,1)S(1)} collective-permute-done((bf16[1,88,256]{2,1,0:T(8,128)(2,1)S(1)}, bf16[1,88,256]{2,1,0:T(8,128)(2,1)S(1)}, u32[]{:S(2)}, u32[]{:S(2)}) %collective-permute-start.3) | collective-permute-done | bytes 45088 | tf_op jit(solution)/shard_map/ppermute | solution.py:34
  8.2 0.4 %collective-permute-done.2 = bf16[1,88,256]{2,1,0:T(8,128)(2,1)S(1)} collective-permute-done((bf16[1,88,256]{2,1,0:T(8,128)(2,1)S(1)}, bf16[1,88,256]{2,1,0:T(8,128)(2,1)S(1)}, u32[]{:S(2)}, u32[]{:S(2)}) %collective-permute-start.2) | collective-permute-done | bytes 45088 | tf_op jit(solution)/shard_map/ppermute | solution.py:34
  8.6 1.6 %collective-permute-start.5 = (bf16[3,88,256]{2,1,0:T(8,128)(2,1)S(1)}, bf16[3,88,256]{2,1,0:T(8,128)(2,1)S(1)}, u32[]{:S(2)}, u32[]{:S(2)}) collective-permute-start(bf16[3,88,256]{2,1,0:T(8,128)(2,1)S(1)} %pad_maximum_fusion.refs_0_), channel_id=1, source_target_pairs={{0,1},{1,0},{2,3},{3,2},{4,5},{5,4},{6,7},{7,6},{8,9},{9,8},{10,11... | collective-permute-start | bytes 405512 | tf_op jit(solution)/shard_map/ppermute | solution.py:29
  10.2 0.8 %collective-permute-done = bf16[1,88,256]{2,1,0:T(8,128)(2,1)S(1)} collective-permute-done((bf16[1,88,256]{2,1,0:T(8,128)(2,1)S(1)}, bf16[1,88,256]{2,1,0:T(8,128)(2,1)S(1)}, u32[]{:S(2)}, u32[]{:S(2)}) %collective-permute-start) | collective-permute-done | bytes 45088 | tf_op jit(solution)/shard_map/ppermute | solution.py:29
  11.0 0.2 %collective-permute-start.1 = (bf16[2,88,256]{2,1,0:T(8,128)(2,1)S(1)}, bf16[2,88,256]{2,1,0:T(8,128)(2,1)S(1)}, u32[]{:S(2)}, u32[]{:S(2)}) collective-permute-start(bf16[2,88,256]{2,1,0:T(8,128)(2,1)S(1)} %pad_maximum_fusion.1.own), channel_id=1, source_target_pairs={{0,2},{2,0},{4,6},{6,4},{1,3},{3,1},{5,7},{7,5},{8,10},{10,8},{12,... | collective-permute-start | bytes 270344 | tf_op jit(solution)/shard_map/ppermute | solution.py:29
  11.2 0.0 collective-permute-done.4.refs_1_
  11.2 1.5 %collective-permute-start.6 = (bf16[1,88,256]{2,1,0:T(8,128)(2,1)S(1)}, bf16[1,88,256]{2,1,0:T(8,128)(2,1)S(1)}, u32[]{:S(2)}, u32[]{:S(2)}) collective-permute-start(bf16[1,88,256]{2,1,0:T(8,128)(2,1)S(1)} %collective-permute-done.4.refs_1_), channel_id=1, source_target_pairs={{0,1},{1,0},{2,3},{3,2},{4,5},{5,4},{6,7},{7,6},{8,9},{9,8},{10,11... | collective-permute-start | bytes 135176 | tf_op jit(solution)/shard_map/ppermute | solution.py:29
  12.8 2.5 %collective-permute-done.6.refs_3_ = bf16[1,88,256]{2,1,0:T(8,128)(2,1)S(1)} collective-permute-done((bf16[1,88,256]{2,1,0:T(8,128)(2,1)S(1)}, bf16[1,88,256]{2,1,0:T(8,128)(2,1)S(1)}, u32[]{:S(2)}, u32[]{:S(2)}) %collective-permute-start.6) | collective-permute-done | bytes 45088 | tf_op jit(solution)/shard_map/ppermute | solution.py:29
  15.3 0.0 collective-permute-done.1.beside
  15.3 0.6 %firsts.1 = (bf16[1,88,256]{2,1,0:T(8,128)(2,1)S(1)}, bf16[1,88,256]{2,1,0:T(8,128)(2,1)S(1)}, bf16[4,2,144,144]{3,2,1,0:T(8,128)(2,1)S(1)}) custom-call(bf16[2,88,256]{2,1,0:T(8,128)(2,1)S(1)} %pad_maximum_fusion.1.own, bf16[2,88,256]{2,1,0:T(8,128)(2,1)S(1)} %collective-permute-done.1.beside, bf16[3,88,256]{2,1,0:T(8,128)(2,1)S(1)} %pad_maximum_fusion.refs_0_, ...), custom_call_target="tpu_custom_call" | custom-call | tf_op jit(solution)/shard_map/firsts/pallas_call | solution.py:284
  15.9 0.1 collective-permute-start.9
  16.0 1.6 %collective-permute-start.7 = (bf16[1,88,256]{2,1,0:T(8,128)(2,1)S(1)}, bf16[1,88,256]{2,1,0:T(8,128)(2,1)S(1)}, u32[]{:S(2)}, u32[]{:S(2)}) collective-permute-start(bf16[1,88,256]{2,1,0:T(8,128)(2,1)S(1)} %get-tuple-element.8), channel_id=1, source_target_pairs={{0,6},{2,4},{4,2},{6,0},{1,7},{3,5},{5,3},{7,1},{8,14},{10,12},{12... | collective-permute-start | bytes 135176 | tf_op jit(solution)/shard_map/ppermute | solution.py:29
  17.6 1.9 %collective-permute-done.7.across = bf16[1,88,256]{2,1,0:T(8,128)(2,1)S(1)} collective-permute-done((bf16[1,88,256]{2,1,0:T(8,128)(2,1)S(1)}, bf16[1,88,256]{2,1,0:T(8,128)(2,1)S(1)}, u32[]{:S(2)}, u32[]{:S(2)}) %collective-permute-start.7) | collective-permute-done | bytes 45088 | tf_op jit(solution)/shard_map/ppermute | solution.py:29
  19.5 0.4 %collective-permute-start.8 = (bf16[1,88,256]{2,1,0:T(8,128)(2,1)S(1)}, bf16[1,88,256]{2,1,0:T(8,128)(2,1)S(1)}, u32[]{:S(2)}, u32[]{:S(2)}) collective-permute-start(bf16[1,88,256]{2,1,0:T(8,128)(2,1)S(1)} %collective-permute-done.7.across), channel_id=1, source_target_pairs={{0,2},{2,0},{4,6},{6,4},{1,3},{3,1},{5,7},{7,5},{8,10},{10,8},{12,... | collective-permute-start | bytes 135176 | tf_op jit(solution)/shard_map/ppermute | solution.py:29
  20.0 0.0 collective-permute-done.9.other
  20.0 0.3 %near_lasts.1.early = f32[72,144]{1,0:T(8,128)S(1)} custom-call(bf16[2,88,256]{2,1,0:T(8,128)(2,1)S(1)} %constant_dynamic-update-slice_fusion.mine, bf16[2,88,256]{2,1,0:T(8,128)(2,1)S(1)} %collective-permute-done.9.other, bf16[4,2,144,144]{3,2,1,0:T(8,128)(2,1)S(1)} %get-tuple-element.9.rhs), custom_call_target="tpu_custom_call" | custom-call | tf_op jit(solution)/shard_map/near_lasts/pallas_call | solution.py:284
  20.3 0.3 %far_lasts.1.early = f32[72,144]{1,0:T(8,128)S(1)} custom-call(bf16[1,88,256]{2,1,0:T(8,128)(2,1)S(1)} %collective-permute-done.7.across, bf16[4,2,144,144]{3,2,1,0:T(8,128)(2,1)S(1)} %get-tuple-element.9.rhs, f32[72,144]{1,0:T(8,128)S(1)} %near_lasts.1.early), custom_call_target="tpu_custom_call" | custom-call | tf_op jit(solution)/shard_map/far_lasts/pallas_call | solution.py:284
  20.6 0.3 %collective-permute-done.8.across = bf16[1,88,256]{2,1,0:T(8,128)(2,1)S(1)} collective-permute-done((bf16[1,88,256]{2,1,0:T(8,128)(2,1)S(1)}, bf16[1,88,256]{2,1,0:T(8,128)(2,1)S(1)}, u32[]{:S(2)}, u32[]{:S(2)}) %collective-permute-start.8) | collective-permute-done | bytes 45088 | tf_op jit(solution)/shard_map/ppermute | solution.py:29
  20.8 0.9 %late_lasts.1 = f32[72,144]{1,0:T(8,128)} custom-call(bf16[1,88,256]{2,1,0:T(8,128)(2,1)S(1)} %collective-permute-done.8.across, bf16[4,2,144,144]{3,2,1,0:T(8,128)(2,1)S(1)} %get-tuple-element.9.rhs, f32[72,144]{1,0:T(8,128)S(1)} %far_lasts.1.early, bf16[1,88,256]{2,1,0:T(8,128)(2,1)S(1)} %pack.1.own_ref), custom_call_target="tpu_custom_call" | custom-call | tf_op jit(solution)/shard_map/late_lasts/pallas_call | solution.py:284
  (5 shorter events, 0.0 us)
Async XLA Ops:
  1.0 7.2 %collective-permute-start.3 = (bf16[1,88,256]{2,1,0:T(8,128)(2,1)S(1)}, bf16[1,88,256]{2,1,0:T(8,128)(2,1)S(1)}, u32[]{:S(2)}, u32[]{:S(2)}) collective-permute-start(bf16[1,88,256]{2,1,0:T(8,128)(2,1)S(1)} %pack.1.own_ref), channel_id=1, source_target_pairs={{24,0},{0,8},{8,16},{16,24},{25,1},{1,9},{9,17},{17,25},{26,2},{2,... | collective-permute-start | bytes 135176 | tf_op jit(solution)/shard_map/ppermute | solution.py:34
  4.1 4.5 %collective-permute-start.2 = (bf16[1,88,256]{2,1,0:T(8,128)(2,1)S(1)}, bf16[1,88,256]{2,1,0:T(8,128)(2,1)S(1)}, u32[]{:S(2)}, u32[]{:S(2)}) collective-permute-start(bf16[1,88,256]{2,1,0:T(8,128)(2,1)S(1)} %pack.1.own_ref), channel_id=1, source_target_pairs={{8,0},{16,8},{24,16},{0,24},{9,1},{17,9},{25,17},{1,25},{10,2},{18... | collective-permute-start | bytes 135176 | tf_op jit(solution)/shard_map/ppermute | solution.py:34
  6.1 5.1 %collective-permute-start.4 = (bf16[1,88,256]{2,1,0:T(8,128)(2,1)S(1)}, bf16[1,88,256]{2,1,0:T(8,128)(2,1)S(1)}, u32[]{:S(2)}, u32[]{:S(2)}) collective-permute-start(bf16[1,88,256]{2,1,0:T(8,128)(2,1)S(1)} %pack.1.own_ref), channel_id=1, source_target_pairs={{16,0},{24,8},{0,16},{8,24},{17,1},{25,9},{1,17},{9,25},{18,2},{26... | collective-permute-start | bytes 135176 | tf_op jit(solution)/shard_map/ppermute | solution.py:34
  7.1 3.9 %collective-permute-start = (bf16[1,88,256]{2,1,0:T(8,128)(2,1)S(1)}, bf16[1,88,256]{2,1,0:T(8,128)(2,1)S(1)}, u32[]{:S(2)}, u32[]{:S(2)}) collective-permute-start(bf16[1,88,256]{2,1,0:T(8,128)(2,1)S(1)} %pack.1.own_ref), channel_id=1, source_target_pairs={{0,6},{2,4},{4,2},{6,0},{1,7},{3,5},{5,3},{7,1},{8,14},{10,12},{12... | collective-permute-start | bytes 135176 | tf_op jit(solution)/shard_map/ppermute | solution.py:29
  8.6 6.7 %collective-permute-start.5 = (bf16[3,88,256]{2,1,0:T(8,128)(2,1)S(1)}, bf16[3,88,256]{2,1,0:T(8,128)(2,1)S(1)}, u32[]{:S(2)}, u32[]{:S(2)}) collective-permute-start(bf16[3,88,256]{2,1,0:T(8,128)(2,1)S(1)} %pad_maximum_fusion.refs_0_), channel_id=1, source_target_pairs={{0,1},{1,0},{2,3},{3,2},{4,5},{5,4},{6,7},{7,6},{8,9},{9,8},{10,11... | collective-permute-start | bytes 405512 | tf_op jit(solution)/shard_map/ppermute | solution.py:29
  11.0 4.3 %collective-permute-start.1 = (bf16[2,88,256]{2,1,0:T(8,128)(2,1)S(1)}, bf16[2,88,256]{2,1,0:T(8,128)(2,1)S(1)}, u32[]{:S(2)}, u32[]{:S(2)}) collective-permute-start(bf16[2,88,256]{2,1,0:T(8,128)(2,1)S(1)} %pad_maximum_fusion.1.own), channel_id=1, source_target_pairs={{0,2},{2,0},{4,6},{6,4},{1,3},{3,1},{5,7},{7,5},{8,10},{10,8},{12,... | collective-permute-start | bytes 270344 | tf_op jit(solution)/shard_map/ppermute | solution.py:29
  11.2 4.0 %collective-permute-start.6 = (bf16[1,88,256]{2,1,0:T(8,128)(2,1)S(1)}, bf16[1,88,256]{2,1,0:T(8,128)(2,1)S(1)}, u32[]{:S(2)}, u32[]{:S(2)}) collective-permute-start(bf16[1,88,256]{2,1,0:T(8,128)(2,1)S(1)} %collective-permute-done.4.refs_1_), channel_id=1, source_target_pairs={{0,1},{1,0},{2,3},{3,2},{4,5},{5,4},{6,7},{7,6},{8,9},{9,8},{10,11... | collective-permute-start | bytes 135176 | tf_op jit(solution)/shard_map/ppermute | solution.py:29
  15.9 4.1 %collective-permute-start.9 = (bf16[2,88,256]{2,1,0:T(8,128)(2,1)S(1)}, bf16[2,88,256]{2,1,0:T(8,128)(2,1)S(1)}, u32[]{:S(2)}, u32[]{:S(2)}) collective-permute-start(bf16[2,88,256]{2,1,0:T(8,128)(2,1)S(1)} %constant_dynamic-update-slice_fusion.mine), channel_id=1, source_target_pairs={{0,2},{2,0},{4,6},{6,4},{1,3},{3,1},{5,7},{7,5},{8,10},{10,8},{12,... | collective-permute-start | bytes 270344 | tf_op jit(solution)/shard_map/ppermute | solution.py:29
  16.0 3.5 %collective-permute-start.7 = (bf16[1,88,256]{2,1,0:T(8,128)(2,1)S(1)}, bf16[1,88,256]{2,1,0:T(8,128)(2,1)S(1)}, u32[]{:S(2)}, u32[]{:S(2)}) collective-permute-start(bf16[1,88,256]{2,1,0:T(8,128)(2,1)S(1)} %get-tuple-element.8), channel_id=1, source_target_pairs={{0,6},{2,4},{4,2},{6,0},{1,7},{3,5},{5,3},{7,1},{8,14},{10,12},{12... | collective-permute-start | bytes 135176 | tf_op jit(solution)/shard_map/ppermute | solution.py:29
  19.5 1.3 %collective-permute-start.8 = (bf16[1,88,256]{2,1,0:T(8,128)(2,1)S(1)}, bf16[1,88,256]{2,1,0:T(8,128)(2,1)S(1)}, u32[]{:S(2)}, u32[]{:S(2)}) collective-permute-start(bf16[1,88,256]{2,1,0:T(8,128)(2,1)S(1)} %collective-permute-done.7.across), channel_id=1, source_target_pairs={{0,2},{2,0},{4,6},{6,4},{1,3},{3,1},{5,7},{7,5},{8,10},{10,8},{12,... | collective-permute-start | bytes 135176 | tf_op jit(solution)/shard_map/ppermute | solution.py:29

commit v5 on v4

--- a/solution.py
+++ b/solution.py
@@ -100,9 +100,12 @@
     main, rem, lead = split(width)
     for k, value in enumerate(values):
         out_ref[0, lead:, k * main : (k + 1) * main] = value[:, :main].astype(out_ref.dtype)
-    if rem:
-        folded = fold(jnp.concatenate([value[:, main:] for value in values], axis=1))
-        out_ref[0, :lead, : folded.shape[1]] = folded.astype(out_ref.dtype)
+    rows, lanes = values[0].shape[0], rem * len(values)
+    for at in range(0, rows if rem else 0, FOLD):
+        deep, left = min(FOLD, rows - at), at // FOLD * lanes
+        for k, value in enumerate(values):
+            part = value[at : at + deep, main:].astype(out_ref.dtype)
+            out_ref[0, :deep, left + k * rem : left + (k + 1) * rem] = part
 
 
 def mains_and_rems(block, rows, rem, lead, total):
@@ -246,15 +249,19 @@
         square, cross = square + terms[0], cross + terms[1]
     high = cross.astype(jnp.bfloat16).astype(jnp.float32)
     pack(out_ref, (high, square), width)
+    lead = split(width)[2]
     low_ref[...] = jnp.zeros_like(low_ref)
-    pack(low_ref, (cross - high,), width)
+    low_ref[0, lead:, :width] = (cross - high).astype(low_ref.dtype)
 
 
 def panel_terms(col, block, low, rhs, width, rows):
-    high, square = natural(block, rows, width, 2)
-    total = times(high, rhs[col, 0]) + times(square, rhs[col, 1])
+    main, rem, lead = split(width)
+    total = times(block[lead : lead + rows, :main], rhs[col, 0, :main])
+    total += times(block[lead : lead + rows, main : 2 * main], rhs[col, 1, :main])
+    ends = jnp.concatenate([rhs[col, 0, main:], rhs[col, 1, main:]], axis=0)
+    total += times(unfold(block[:lead], rows, 2 * rem), ends)
     if low is not None:
-        total += times(natural(low, rows, width, 1)[0], rhs[col, 0])
+        total += times(low[lead:, :width], rhs[col, 0])
     return total
 
 
@@ -266,18 +273,18 @@
     )
 
 
-def far_lasts_kernel(width, across, rhs, early, out_ref):
+def far_lasts_kernel(width, across, rhs, early, own_ref, out_ref):
     rows = out_ref.shape[0]
     my_col = lax.axis_index("col")
-    out_ref[...] = early[...] + panel_terms(my_col ^ 3, across[0], None, rhs, width, rows)
-
-
-def late_lasts_kernel(width, across, rhs, early, own_ref, out_ref):
+    total = early[...] + panel_terms(my_col ^ 3, across[0], None, rhs, width, rows)
+    own = natural(own_ref[0], rows, width, 2)[1].astype(jnp.float32)
+    out_ref[...] = 1.5 * own - 0.5 * total
+
+
+def late_lasts_kernel(width, across, rhs, early, out_ref):
     rows = out_ref.shape[0]
     my_col = lax.axis_index("col")
-    total = early[...] + panel_terms(my_col ^ 2, across[0], None, rhs, width, rows)
-    own = natural(own_ref[0], rows, width, 2)[1].astype(jnp.float32)
-    out_ref[...] = 1.5 * own - 0.5 * total
+    out_ref[...] = early[...] - 0.5 * panel_terms(my_col ^ 2, across[0], None, rhs, width, rows)
 
 
 def call(kernel, name, out_shape, operands, scratch=(), **kwargs):
@@ -315,12 +322,12 @@
     mine = jnp.concatenate([firsts, low], axis=0)
     near = (mine, swap(mine, "col", 1))
     total = call(functools.partial(near_lasts_kernel, width), "near_lasts", out, (*near, rhs))
-    total = call(functools.partial(far_lasts_kernel, width), "far_lasts", out, (across, rhs, total))
+    total = call(functools.partial(far_lasts_kernel, width), "far_lasts", out, (across, rhs, total, block))
     return call(
         functools.partial(late_lasts_kernel, width),
         "late_lasts",
         out,
-        (swap(across, "col", 1), rhs, total, block),
+        (swap(across, "col", 1), rhs, total),
     )
 
 

time: 21.9 us -> 21.8 us (level)
  Pallas kernels: 3.03 us -> 2.76 us
  transfers between devices with their start and end apart: 10 -> 10, of which waited for: 6 -> 6; matrix products, arithmetic and copies ran while one was open for 0% -> 0% of each run, Pallas kernels for 3% -> 2%
where the time goes in v5:
time: 21.8 us; the launch traced here: 21.6 us
  starting transfers between devices  11.7 us (54%)
  waiting for transfers between devices  7.07 us (32%)
  Pallas kernels  2.76 us (13%)
    ppermute x3, starting transfers between devices, turn(): lax.ppermute(value, axis, [((i + offset) % size, i) for i in range(size)])  6.11 us
    ppermute x7, waiting for transfers between devices, swap(): return lax.ppermute(value, axis, [(i, i ^ offset) for i in range(size)])  5.67 us
    ppermute x7, starting transfers between devices, swap(): return lax.ppermute(value, axis, [(i, i ^ offset) for i in range(size)])  5.55 us
    pallas_call x4, Pallas kernels, call(): pl.pallas_call(kernel, out_shape=out_shape, in_specs=[VMEM] * len(operand...  1.85 us
    ppermute x3, waiting for transfers between devices, turn(): lax.ppermute(value, axis, [((i + offset) % size, i) for i in range(size)])  1.4 us
    pallas_call x1, Pallas kernels, body(): pl.pallas_call(pack_kernel, out_shape=jax.ShapeDtypeStruct((1, lead + row...  0.91 us
  transfers between devices with their start and end apart: 10, of which 6 were waited for; matrix products, arithmetic and copies ran while one was open for 0% of the time, Pallas kernels for 2%

profile of v5, /device:TPU:0, one launch (start us, length us, event | category | flops | bytes accessed | tf_op | source)
XLA Modules:
  0.0 21.6 jit_solution(4750541301584299342)
XLA Ops:
  0.0 0.9 %pack.1.own_ref = bf16[1,88,256]{2,1,0:T(8,128)(2,1)S(1)} custom-call(bf16[72,144]{1,0:T(8,128)(2,1)} %x_hbm.1, bf16[72,144]{1,0:T(8,128)(2,1)} %t_hbm.1, s32[5,5]{1,0:T(8,128)} %fill_x_hbm.1, s32[5,5]{1,0:T(8,128)} %fill_t_hbm.1), custom_call_target="tpu_custom_call" | custom-call | tf_op jit(solution)/shard_map/pack/pallas_call | solution.py:375
  0.9 3.1 %collective-permute-start.3 = (bf16[1,88,256]{2,1,0:T(8,128)(2,1)S(1)}, bf16[1,88,256]{2,1,0:T(8,128)(2,1)S(1)}, u32[]{:S(2)}, u32[]{:S(2)}) collective-permute-start(bf16[1,88,256]{2,1,0:T(8,128)(2,1)S(1)} %pack.1.own_ref), channel_id=1, source_target_pairs={{24,0},{0,8},{8,16},{16,24},{25,1},{1,9},{9,17},{17,25},{26,2},{2,... | collective-permute-start | bytes 135176 | tf_op jit(solution)/shard_map/ppermute | solution.py:34
  4.0 2.1 %collective-permute-start.2 = (bf16[1,88,256]{2,1,0:T(8,128)(2,1)S(1)}, bf16[1,88,256]{2,1,0:T(8,128)(2,1)S(1)}, u32[]{:S(2)}, u32[]{:S(2)}) collective-permute-start(bf16[1,88,256]{2,1,0:T(8,128)(2,1)S(1)} %pack.1.own_ref), channel_id=1, source_target_pairs={{8,0},{16,8},{24,16},{0,24},{9,1},{17,9},{25,17},{1,25},{10,2},{18... | collective-permute-start | bytes 135176 | tf_op jit(solution)/shard_map/ppermute | solution.py:34
  6.1 0.9 %collective-permute-start.4 = (bf16[1,88,256]{2,1,0:T(8,128)(2,1)S(1)}, bf16[1,88,256]{2,1,0:T(8,128)(2,1)S(1)}, u32[]{:S(2)}, u32[]{:S(2)}) collective-permute-start(bf16[1,88,256]{2,1,0:T(8,128)(2,1)S(1)} %pack.1.own_ref), channel_id=1, source_target_pairs={{16,0},{24,8},{0,16},{8,24},{17,1},{25,9},{1,17},{9,25},{18,2},{26... | collective-permute-start | bytes 135176 | tf_op jit(solution)/shard_map/ppermute | solution.py:34
  7.0 0.1 collective-permute-start
  7.1 1.0 %collective-permute-done.3 = bf16[1,88,256]{2,1,0:T(8,128)(2,1)S(1)} collective-permute-done((bf16[1,88,256]{2,1,0:T(8,128)(2,1)S(1)}, bf16[1,88,256]{2,1,0:T(8,128)(2,1)S(1)}, u32[]{:S(2)}, u32[]{:S(2)}) %collective-permute-start.3) | collective-permute-done | bytes 45088 | tf_op jit(solution)/shard_map/ppermute | solution.py:34
  8.1 0.4 %collective-permute-done.2 = bf16[1,88,256]{2,1,0:T(8,128)(2,1)S(1)} collective-permute-done((bf16[1,88,256]{2,1,0:T(8,128)(2,1)S(1)}, bf16[1,88,256]{2,1,0:T(8,128)(2,1)S(1)}, u32[]{:S(2)}, u32[]{:S(2)}) %collective-permute-start.2) | collective-permute-done | bytes 45088 | tf_op jit(solution)/shard_map/ppermute | solution.py:34
  8.5 1.6 %collective-permute-start.5 = (bf16[3,88,256]{2,1,0:T(8,128)(2,1)S(1)}, bf16[3,88,256]{2,1,0:T(8,128)(2,1)S(1)}, u32[]{:S(2)}, u32[]{:S(2)}) collective-permute-start(bf16[3,88,256]{2,1,0:T(8,128)(2,1)S(1)} %pad_maximum_fusion.refs_0_), channel_id=1, source_target_pairs={{0,1},{1,0},{2,3},{3,2},{4,5},{5,4},{6,7},{7,6},{8,9},{9,8},{10,11... | collective-permute-start | bytes 405512 | tf_op jit(solution)/shard_map/ppermute | solution.py:29
  10.1 0.8 %collective-permute-done = bf16[1,88,256]{2,1,0:T(8,128)(2,1)S(1)} collective-permute-done((bf16[1,88,256]{2,1,0:T(8,128)(2,1)S(1)}, bf16[1,88,256]{2,1,0:T(8,128)(2,1)S(1)}, u32[]{:S(2)}, u32[]{:S(2)}) %collective-permute-start) | collective-permute-done | bytes 45088 | tf_op jit(solution)/shard_map/ppermute | solution.py:29
  11.0 0.2 %collective-permute-start.1 = (bf16[2,88,256]{2,1,0:T(8,128)(2,1)S(1)}, bf16[2,88,256]{2,1,0:T(8,128)(2,1)S(1)}, u32[]{:S(2)}, u32[]{:S(2)}) collective-permute-start(bf16[2,88,256]{2,1,0:T(8,128)(2,1)S(1)} %pad_maximum_fusion.1.own), channel_id=1, source_target_pairs={{0,2},{2,0},{4,6},{6,4},{1,3},{3,1},{5,7},{7,5},{8,10},{10,8},{12,... | collective-permute-start | bytes 270344 | tf_op jit(solution)/shard_map/ppermute | solution.py:29
  11.2 0.0 collective-permute-done.4.refs_1_
  11.2 1.5 %collective-permute-start.6 = (bf16[1,88,256]{2,1,0:T(8,128)(2,1)S(1)}, bf16[1,88,256]{2,1,0:T(8,128)(2,1)S(1)}, u32[]{:S(2)}, u32[]{:S(2)}) collective-permute-start(bf16[1,88,256]{2,1,0:T(8,128)(2,1)S(1)} %collective-permute-done.4.refs_1_), channel_id=1, source_target_pairs={{0,1},{1,0},{2,3},{3,2},{4,5},{5,4},{6,7},{7,6},{8,9},{9,8},{10,11... | collective-permute-start | bytes 135176 | tf_op jit(solution)/shard_map/ppermute | solution.py:29
  12.7 2.5 %collective-permute-done.6.refs_3_ = bf16[1,88,256]{2,1,0:T(8,128)(2,1)S(1)} collective-permute-done((bf16[1,88,256]{2,1,0:T(8,128)(2,1)S(1)}, bf16[1,88,256]{2,1,0:T(8,128)(2,1)S(1)}, u32[]{:S(2)}, u32[]{:S(2)}) %collective-permute-start.6) | collective-permute-done | bytes 45088 | tf_op jit(solution)/shard_map/ppermute | solution.py:29
  15.2 0.0 collective-permute-done.1.beside
  15.2 0.0 collective-permute-done.5.refs_2_
  15.2 0.6 %firsts.1 = (bf16[1,88,256]{2,1,0:T(8,128)(2,1)S(1)}, bf16[1,88,256]{2,1,0:T(8,128)(2,1)S(1)}, bf16[4,2,144,144]{3,2,1,0:T(8,128)(2,1)S(1)}) custom-call(bf16[2,88,256]{2,1,0:T(8,128)(2,1)S(1)} %pad_maximum_fusion.1.own, bf16[2,88,256]{2,1,0:T(8,128)(2,1)S(1)} %collective-permute-done.1.beside, bf16[3,88,256]{2,1,0:T(8,128)(2,1)S(1)} %pad_maximum_fusion.refs_0_, ...), custom_call_target="tpu_custom_call" | custom-call | tf_op jit(solution)/shard_map/firsts/pallas_call | solution.py:291
  15.8 0.1 collective-permute-start.9
  15.9 1.6 %collective-permute-start.7 = (bf16[1,88,256]{2,1,0:T(8,128)(2,1)S(1)}, bf16[1,88,256]{2,1,0:T(8,128)(2,1)S(1)}, u32[]{:S(2)}, u32[]{:S(2)}) collective-permute-start(bf16[1,88,256]{2,1,0:T(8,128)(2,1)S(1)} %get-tuple-element.8), channel_id=1, source_target_pairs={{0,6},{2,4},{4,2},{6,0},{1,7},{3,5},{5,3},{7,1},{8,14},{10,12},{12... | collective-permute-start | bytes 135176 | tf_op jit(solution)/shard_map/ppermute | solution.py:29
  17.5 1.9 %collective-permute-done.7.across = bf16[1,88,256]{2,1,0:T(8,128)(2,1)S(1)} collective-permute-done((bf16[1,88,256]{2,1,0:T(8,128)(2,1)S(1)}, bf16[1,88,256]{2,1,0:T(8,128)(2,1)S(1)}, u32[]{:S(2)}, u32[]{:S(2)}) %collective-permute-start.7) | collective-permute-done | bytes 45088 | tf_op jit(solution)/shard_map/ppermute | solution.py:29
  19.4 0.4 %collective-permute-start.8 = (bf16[1,88,256]{2,1,0:T(8,128)(2,1)S(1)}, bf16[1,88,256]{2,1,0:T(8,128)(2,1)S(1)}, u32[]{:S(2)}, u32[]{:S(2)}) collective-permute-start(bf16[1,88,256]{2,1,0:T(8,128)(2,1)S(1)} %collective-permute-done.7.across), channel_id=1, source_target_pairs={{0,2},{2,0},{4,6},{6,4},{1,3},{3,1},{5,7},{7,5},{8,10},{10,8},{12,... | collective-permute-start | bytes 135176 | tf_op jit(solution)/shard_map/ppermute | solution.py:29
  19.9 0.3 %near_lasts.1.early = f32[72,144]{1,0:T(8,128)S(1)} custom-call(bf16[2,88,256]{2,1,0:T(8,128)(2,1)S(1)} %constant_dynamic-update-slice_fusion.mine, bf16[2,88,256]{2,1,0:T(8,128)(2,1)S(1)} %collective-permute-done.9.other, bf16[4,2,144,144]{3,2,1,0:T(8,128)(2,1)S(1)} %get-tuple-element.9.rhs), custom_call_target="tpu_custom_call" | custom-call | tf_op jit(solution)/shard_map/near_lasts/pallas_call | solution.py:291
  20.2 0.2 far_lasts.1.early
  20.4 0.4 %collective-permute-done.8.across = bf16[1,88,256]{2,1,0:T(8,128)(2,1)S(1)} collective-permute-done((bf16[1,88,256]{2,1,0:T(8,128)(2,1)S(1)}, bf16[1,88,256]{2,1,0:T(8,128)(2,1)S(1)}, u32[]{:S(2)}, u32[]{:S(2)}) %collective-permute-start.8) | collective-permute-done | bytes 45088 | tf_op jit(solution)/shard_map/ppermute | solution.py:29
  20.8 0.8 %late_lasts.1 = f32[72,144]{1,0:T(8,128)} custom-call(bf16[1,88,256]{2,1,0:T(8,128)(2,1)S(1)} %collective-permute-done.8.across, bf16[4,2,144,144]{3,2,1,0:T(8,128)(2,1)S(1)} %get-tuple-element.9.rhs, f32[72,144]{1,0:T(8,128)S(1)} %far_lasts.1.early), custom_call_target="tpu_custom_call" | custom-call | tf_op jit(solution)/shard_map/late_lasts/pallas_call | solution.py:291
  (5 shorter events, 0.0 us)
Async XLA Ops:
  0.9 7.2 %collective-permute-start.3 = (bf16[1,88,256]{2,1,0:T(8,128)(2,1)S(1)}, bf16[1,88,256]{2,1,0:T(8,128)(2,1)S(1)}, u32[]{:S(2)}, u32[]{:S(2)}) collective-permute-start(bf16[1,88,256]{2,1,0:T(8,128)(2,1)S(1)} %pack.1.own_ref), channel_id=1, source_target_pairs={{24,0},{0,8},{8,16},{16,24},{25,1},{1,9},{9,17},{17,25},{26,2},{2,... | collective-permute-start | bytes 135176 | tf_op jit(solution)/shard_map/ppermute | solution.py:34
  4.0 4.5 %collective-permute-start.2 = (bf16[1,88,256]{2,1,0:T(8,128)(2,1)S(1)}, bf16[1,88,256]{2,1,0:T(8,128)(2,1)S(1)}, u32[]{:S(2)}, u32[]{:S(2)}) collective-permute-start(bf16[1,88,256]{2,1,0:T(8,128)(2,1)S(1)} %pack.1.own_ref), channel_id=1, source_target_pairs={{8,0},{16,8},{24,16},{0,24},{9,1},{17,9},{25,17},{1,25},{10,2},{18... | collective-permute-start | bytes 135176 | tf_op jit(solution)/shard_map/ppermute | solution.py:34
  6.1 5.1 %collective-permute-start.4 = (bf16[1,88,256]{2,1,0:T(8,128)(2,1)S(1)}, bf16[1,88,256]{2,1,0:T(8,128)(2,1)S(1)}, u32[]{:S(2)}, u32[]{:S(2)}) collective-permute-start(bf16[1,88,256]{2,1,0:T(8,128)(2,1)S(1)} %pack.1.own_ref), channel_id=1, source_target_pairs={{16,0},{24,8},{0,16},{8,24},{17,1},{25,9},{1,17},{9,25},{18,2},{26... | collective-permute-start | bytes 135176 | tf_op jit(solution)/shard_map/ppermute | solution.py:34
  7.0 3.9 %collective-permute-start = (bf16[1,88,256]{2,1,0:T(8,128)(2,1)S(1)}, bf16[1,88,256]{2,1,0:T(8,128)(2,1)S(1)}, u32[]{:S(2)}, u32[]{:S(2)}) collective-permute-start(bf16[1,88,256]{2,1,0:T(8,128)(2,1)S(1)} %pack.1.own_ref), channel_id=1, source_target_pairs={{0,6},{2,4},{4,2},{6,0},{1,7},{3,5},{5,3},{7,1},{8,14},{10,12},{12... | collective-permute-start | bytes 135176 | tf_op jit(solution)/shard_map/ppermute | solution.py:29
  8.5 6.7 %collective-permute-start.5 = (bf16[3,88,256]{2,1,0:T(8,128)(2,1)S(1)}, bf16[3,88,256]{2,1,0:T(8,128)(2,1)S(1)}, u32[]{:S(2)}, u32[]{:S(2)}) collective-permute-start(bf16[3,88,256]{2,1,0:T(8,128)(2,1)S(1)} %pad_maximum_fusion.refs_0_), channel_id=1, source_target_pairs={{0,1},{1,0},{2,3},{3,2},{4,5},{5,4},{6,7},{7,6},{8,9},{9,8},{10,11... | collective-permute-start | bytes 405512 | tf_op jit(solution)/shard_map/ppermute | solution.py:29
  11.0 4.3 %collective-permute-start.1 = (bf16[2,88,256]{2,1,0:T(8,128)(2,1)S(1)}, bf16[2,88,256]{2,1,0:T(8,128)(2,1)S(1)}, u32[]{:S(2)}, u32[]{:S(2)}) collective-permute-start(bf16[2,88,256]{2,1,0:T(8,128)(2,1)S(1)} %pad_maximum_fusion.1.own), channel_id=1, source_target_pairs={{0,2},{2,0},{4,6},{6,4},{1,3},{3,1},{5,7},{7,5},{8,10},{10,8},{12,... | collective-permute-start | bytes 270344 | tf_op jit(solution)/shard_map/ppermute | solution.py:29
  11.2 4.0 %collective-permute-start.6 = (bf16[1,88,256]{2,1,0:T(8,128)(2,1)S(1)}, bf16[1,88,256]{2,1,0:T(8,128)(2,1)S(1)}, u32[]{:S(2)}, u32[]{:S(2)}) collective-permute-start(bf16[1,88,256]{2,1,0:T(8,128)(2,1)S(1)} %collective-permute-done.4.refs_1_), channel_id=1, source_target_pairs={{0,1},{1,0},{2,3},{3,2},{4,5},{5,4},{6,7},{7,6},{8,9},{9,8},{10,11... | collective-permute-start | bytes 135176 | tf_op jit(solution)/shard_map/ppermute | solution.py:29
  15.8 4.1 %collective-permute-start.9 = (bf16[2,88,256]{2,1,0:T(8,128)(2,1)S(1)}, bf16[2,88,256]{2,1,0:T(8,128)(2,1)S(1)}, u32[]{:S(2)}, u32[]{:S(2)}) collective-permute-start(bf16[2,88,256]{2,1,0:T(8,128)(2,1)S(1)} %constant_dynamic-update-slice_fusion.mine), channel_id=1, source_target_pairs={{0,2},{2,0},{4,6},{6,4},{1,3},{3,1},{5,7},{7,5},{8,10},{10,8},{12,... | collective-permute-start | bytes 270344 | tf_op jit(solution)/shard_map/ppermute | solution.py:29
  15.9 3.5 %collective-permute-start.7 = (bf16[1,88,256]{2,1,0:T(8,128)(2,1)S(1)}, bf16[1,88,256]{2,1,0:T(8,128)(2,1)S(1)}, u32[]{:S(2)}, u32[]{:S(2)}) collective-permute-start(bf16[1,88,256]{2,1,0:T(8,128)(2,1)S(1)} %get-tuple-element.8), channel_id=1, source_target_pairs={{0,6},{2,4},{4,2},{6,0},{1,7},{3,5},{5,3},{7,1},{8,14},{10,12},{12... | collective-permute-start | bytes 135176 | tf_op jit(solution)/shard_map/ppermute | solution.py:29
  19.4 1.3 %collective-permute-start.8 = (bf16[1,88,256]{2,1,0:T(8,128)(2,1)S(1)}, bf16[1,88,256]{2,1,0:T(8,128)(2,1)S(1)}, u32[]{:S(2)}, u32[]{:S(2)}) collective-permute-start(bf16[1,88,256]{2,1,0:T(8,128)(2,1)S(1)} %collective-permute-done.7.across), channel_id=1, source_target_pairs={{0,2},{2,0},{4,6},{6,4},{1,3},{3,1},{5,7},{7,5},{8,10},{10,8},{12,... | collective-permute-start | bytes 135176 | tf_op jit(solution)/shard_map/ppermute | solution.py:29

commit v6 on v5

--- a/solution.py
+++ b/solution.py
@@ -265,26 +265,25 @@
     return total
 
 
-def near_lasts_kernel(width, mine, other, rhs, out_ref):
+def far_lasts_kernel(offset, width, panel, rhs, own_ref, out_ref):
+    rows = out_ref.shape[0]
+    terms = panel_terms(lax.axis_index("col") ^ offset, panel[0], None, rhs, width, rows)
+    own = natural(own_ref[0], rows, width, 2)[1].astype(jnp.float32)
+    out_ref[...] = 1.5 * own - 0.5 * terms
+
+
+def near_lasts_kernel(width, mine, other, rhs, early, out_ref):
     rows = out_ref.shape[0]
     my_col = lax.axis_index("col")
-    out_ref[...] = panel_terms(my_col, mine[0], mine[1], rhs, width, rows) + panel_terms(
-        my_col ^ 1, other[0], other[1], rhs, width, rows
-    )
-
-
-def far_lasts_kernel(width, across, rhs, early, own_ref, out_ref):
+    terms = panel_terms(my_col, mine[0], mine[1], rhs, width, rows)
+    terms += panel_terms(my_col ^ 1, other[0], other[1], rhs, width, rows)
+    out_ref[...] = early[...] - 0.5 * terms
+
+
+def late_lasts_kernel(offset, width, panel, rhs, early, out_ref):
     rows = out_ref.shape[0]
-    my_col = lax.axis_index("col")
-    total = early[...] + panel_terms(my_col ^ 3, across[0], None, rhs, width, rows)
-    own = natural(own_ref[0], rows, width, 2)[1].astype(jnp.float32)
-    out_ref[...] = 1.5 * own - 0.5 * total
-
-
-def late_lasts_kernel(width, across, rhs, early, out_ref):
-    rows = out_ref.shape[0]
-    my_col = lax.axis_index("col")
-    out_ref[...] = early[...] - 0.5 * panel_terms(my_col ^ 2, across[0], None, rhs, width, rows)
+    terms = panel_terms(lax.axis_index("col") ^ offset, panel[0], None, rhs, width, rows)
+    out_ref[...] = early[...] - 0.5 * terms
 
 
 def call(kernel, name, out_shape, operands, scratch=(), **kwargs):
@@ -317,17 +316,15 @@
         (held, beside, line, opposite, side_line, side_opposite),
         [pltpu.VMEM((grid, 2 * top, width), jnp.bfloat16)],
     )
-    across = swap(firsts, "col", 3)
     out = shape((rows, width), jnp.float32)
+    straight = swap(firsts, "col", 3)
+    crossed = swap(firsts, "col", 2)
     mine = jnp.concatenate([firsts, low], axis=0)
     near = (mine, swap(mine, "col", 1))
-    total = call(functools.partial(near_lasts_kernel, width), "near_lasts", out, (*near, rhs))
-    total = call(functools.partial(far_lasts_kernel, width), "far_lasts", out, (across, rhs, total, block))
+    far = call(functools.partial(far_lasts_kernel, 3, width), "far_lasts", out, (straight, rhs, block), cost_estimate=pl.CostEstimate(flops=1000000000, bytes_accessed=0, transcendentals=0),)
+    total = call(functools.partial(near_lasts_kernel, width), "near_lasts", out, (*near, rhs, far), )
     return call(
-        functools.partial(late_lasts_kernel, width),
-        "late_lasts",
-        out,
-        (swap(across, "col", 1), rhs, total),
+        functools.partial(late_lasts_kernel, 2, width), "late_lasts", out, (crossed, rhs, total)
     )
 
 

time: 21.8 us -> 21.5 us (0.986)
  no operation moved by 1% of the time
where the time goes in v6:
time: 21.5 us; the launch traced here: 21.3 us
  starting transfers between devices  11.5 us (53%)
  waiting for transfers between devices  6.96 us (32%)
  Pallas kernels  2.76 us (13%)
    ppermute x3, starting transfers between devices, turn(): lax.ppermute(value, axis, [((i + offset) % size, i) for i in range(size)])  6.11 us
    ppermute x7, waiting for transfers between devices, swap(): return lax.ppermute(value, axis, [(i, i ^ offset) for i in range(size)])  5.56 us
    ppermute x7, starting transfers between devices, swap(): return lax.ppermute(value, axis, [(i, i ^ offset) for i in range(size)])  5.4 us
    pallas_call x4, Pallas kernels, call(): pl.pallas_call(kernel, out_shape=out_shape, in_specs=[VMEM] * len(operand...  1.86 us
    ppermute x3, waiting for transfers between devices, turn(): lax.ppermute(value, axis, [((i + offset) % size, i) for i in range(size)])  1.4 us
    pallas_call x1, Pallas kernels, body(): pl.pallas_call(pack_kernel, out_shape=jax.ShapeDtypeStruct((1, lead + row...  0.91 us
  transfers between devices with their start and end apart: 10, of which 6 were waited for; matrix products, arithmetic and copies ran while one was open for 0% of the time, Pallas kernels for 2%

profile of v6, /device:TPU:0, one launch (start us, length us, event | category | flops | bytes accessed | tf_op | source)
XLA Modules:
  0.0 21.3 jit_solution(17303269323412641610)
XLA Ops:
  0.0 0.9 %pack.1.own_ref = bf16[1,88,256]{2,1,0:T(8,128)(2,1)S(1)} custom-call(bf16[72,144]{1,0:T(8,128)(2,1)} %x_hbm.1, bf16[72,144]{1,0:T(8,128)(2,1)} %t_hbm.1, s32[5,5]{1,0:T(8,128)} %fill_x_hbm.1, s32[5,5]{1,0:T(8,128)} %fill_t_hbm.1), custom_call_target="tpu_custom_call" | custom-call | tf_op jit(solution)/shard_map/pack/pallas_call | solution.py:372
  0.9 3.1 %collective-permute-start.3 = (bf16[1,88,256]{2,1,0:T(8,128)(2,1)S(1)}, bf16[1,88,256]{2,1,0:T(8,128)(2,1)S(1)}, u32[]{:S(2)}, u32[]{:S(2)}) collective-permute-start(bf16[1,88,256]{2,1,0:T(8,128)(2,1)S(1)} %pack.1.own_ref), channel_id=1, source_target_pairs={{24,0},{0,8},{8,16},{16,24},{25,1},{1,9},{9,17},{17,25},{26,2},{2,... | collective-permute-start | bytes 135176 | tf_op jit(solution)/shard_map/ppermute | solution.py:34
  4.0 2.1 %collective-permute-start.2 = (bf16[1,88,256]{2,1,0:T(8,128)(2,1)S(1)}, bf16[1,88,256]{2,1,0:T(8,128)(2,1)S(1)}, u32[]{:S(2)}, u32[]{:S(2)}) collective-permute-start(bf16[1,88,256]{2,1,0:T(8,128)(2,1)S(1)} %pack.1.own_ref), channel_id=1, source_target_pairs={{8,0},{16,8},{24,16},{0,24},{9,1},{17,9},{25,17},{1,25},{10,2},{18... | collective-permute-start | bytes 135176 | tf_op jit(solution)/shard_map/ppermute | solution.py:34
  6.1 0.9 %collective-permute-start.4 = (bf16[1,88,256]{2,1,0:T(8,128)(2,1)S(1)}, bf16[1,88,256]{2,1,0:T(8,128)(2,1)S(1)}, u32[]{:S(2)}, u32[]{:S(2)}) collective-permute-start(bf16[1,88,256]{2,1,0:T(8,128)(2,1)S(1)} %pack.1.own_ref), channel_id=1, source_target_pairs={{16,0},{24,8},{0,16},{8,24},{17,1},{25,9},{1,17},{9,25},{18,2},{26... | collective-permute-start | bytes 135176 | tf_op jit(solution)/shard_map/ppermute | solution.py:34
  7.0 0.1 collective-permute-start
  7.1 1.0 %collective-permute-done.3 = bf16[1,88,256]{2,1,0:T(8,128)(2,1)S(1)} collective-permute-done((bf16[1,88,256]{2,1,0:T(8,128)(2,1)S(1)}, bf16[1,88,256]{2,1,0:T(8,128)(2,1)S(1)}, u32[]{:S(2)}, u32[]{:S(2)}) %collective-permute-start.3) | collective-permute-done | bytes 45088 | tf_op jit(solution)/shard_map/ppermute | solution.py:34
  8.1 0.4 %collective-permute-done.2 = bf16[1,88,256]{2,1,0:T(8,128)(2,1)S(1)} collective-permute-done((bf16[1,88,256]{2,1,0:T(8,128)(2,1)S(1)}, bf16[1,88,256]{2,1,0:T(8,128)(2,1)S(1)}, u32[]{:S(2)}, u32[]{:S(2)}) %collective-permute-start.2) | collective-permute-done | bytes 45088 | tf_op jit(solution)/shard_map/ppermute | solution.py:34
  8.5 1.6 %collective-permute-start.5 = (bf16[3,88,256]{2,1,0:T(8,128)(2,1)S(1)}, bf16[3,88,256]{2,1,0:T(8,128)(2,1)S(1)}, u32[]{:S(2)}, u32[]{:S(2)}) collective-permute-start(bf16[3,88,256]{2,1,0:T(8,128)(2,1)S(1)} %pad_maximum_fusion.refs_0_), channel_id=1, source_target_pairs={{0,1},{1,0},{2,3},{3,2},{4,5},{5,4},{6,7},{7,6},{8,9},{9,8},{10,11... | collective-permute-start | bytes 405512 | tf_op jit(solution)/shard_map/ppermute | solution.py:29
  10.1 0.8 %collective-permute-done = bf16[1,88,256]{2,1,0:T(8,128)(2,1)S(1)} collective-permute-done((bf16[1,88,256]{2,1,0:T(8,128)(2,1)S(1)}, bf16[1,88,256]{2,1,0:T(8,128)(2,1)S(1)}, u32[]{:S(2)}, u32[]{:S(2)}) %collective-permute-start) | collective-permute-done | bytes 45088 | tf_op jit(solution)/shard_map/ppermute | solution.py:29
  11.0 0.2 %collective-permute-start.1 = (bf16[2,88,256]{2,1,0:T(8,128)(2,1)S(1)}, bf16[2,88,256]{2,1,0:T(8,128)(2,1)S(1)}, u32[]{:S(2)}, u32[]{:S(2)}) collective-permute-start(bf16[2,88,256]{2,1,0:T(8,128)(2,1)S(1)} %pad_maximum_fusion.1.own), channel_id=1, source_target_pairs={{0,2},{2,0},{4,6},{6,4},{1,3},{3,1},{5,7},{7,5},{8,10},{10,8},{12,... | collective-permute-start | bytes 270344 | tf_op jit(solution)/shard_map/ppermute | solution.py:29
  11.2 1.5 %collective-permute-start.6 = (bf16[1,88,256]{2,1,0:T(8,128)(2,1)S(1)}, bf16[1,88,256]{2,1,0:T(8,128)(2,1)S(1)}, u32[]{:S(2)}, u32[]{:S(2)}) collective-permute-start(bf16[1,88,256]{2,1,0:T(8,128)(2,1)S(1)} %collective-permute-done.4.refs_1_), channel_id=1, source_target_pairs={{0,1},{1,0},{2,3},{3,2},{4,5},{5,4},{6,7},{7,6},{8,9},{9,8},{10,11... | collective-permute-start | bytes 135176 | tf_op jit(solution)/shard_map/ppermute | solution.py:29
  12.7 2.5 %collective-permute-done.6.refs_3_ = bf16[1,88,256]{2,1,0:T(8,128)(2,1)S(1)} collective-permute-done((bf16[1,88,256]{2,1,0:T(8,128)(2,1)S(1)}, bf16[1,88,256]{2,1,0:T(8,128)(2,1)S(1)}, u32[]{:S(2)}, u32[]{:S(2)}) %collective-permute-start.6) | collective-permute-done | bytes 45088 | tf_op jit(solution)/shard_map/ppermute | solution.py:29
  15.2 0.0 collective-permute-done.1.beside
  15.2 0.0 collective-permute-done.5.refs_2_
  15.2 0.6 %firsts.1 = (bf16[1,88,256]{2,1,0:T(8,128)(2,1)S(1)}, bf16[1,88,256]{2,1,0:T(8,128)(2,1)S(1)}, bf16[4,2,144,144]{3,2,1,0:T(8,128)(2,1)S(1)}) custom-call(bf16[2,88,256]{2,1,0:T(8,128)(2,1)S(1)} %pad_maximum_fusion.1.own, bf16[2,88,256]{2,1,0:T(8,128)(2,1)S(1)} %collective-permute-done.1.beside, bf16[3,88,256]{2,1,0:T(8,128)(2,1)S(1)} %pad_maximum_fusion.refs_0_, ...), custom_call_target="tpu_custom_call" | custom-call | tf_op jit(solution)/shard_map/firsts/pallas_call | solution.py:290
  15.8 0.1 collective-permute-start.9
  15.9 1.6 %collective-permute-start.7 = (bf16[1,88,256]{2,1,0:T(8,128)(2,1)S(1)}, bf16[1,88,256]{2,1,0:T(8,128)(2,1)S(1)}, u32[]{:S(2)}, u32[]{:S(2)}) collective-permute-start(bf16[1,88,256]{2,1,0:T(8,128)(2,1)S(1)} %get-tuple-element.8), channel_id=1, source_target_pairs={{0,4},{2,6},{4,0},{6,2},{1,5},{3,7},{5,1},{7,3},{8,12},{10,14},{12... | collective-permute-start | bytes 135176 | tf_op jit(solution)/shard_map/ppermute | solution.py:29
  17.4 0.4 %collective-permute-start.8 = (bf16[2,88,256]{2,1,0:T(8,128)(2,1)S(1)}, bf16[2,88,256]{2,1,0:T(8,128)(2,1)S(1)}, u32[]{:S(2)}, u32[]{:S(2)}) collective-permute-start(bf16[2,88,256]{2,1,0:T(8,128)(2,1)S(1)} %constant_dynamic-update-slice_fusion.mine), channel_id=1, source_target_pairs={{0,2},{2,0},{4,6},{6,4},{1,3},{3,1},{5,7},{7,5},{8,10},{10,8},{12,... | collective-permute-start | bytes 270344 | tf_op jit(solution)/shard_map/ppermute | solution.py:29
  17.8 2.0 %collective-permute-done.9.panel = bf16[1,88,256]{2,1,0:T(8,128)(2,1)S(1)} collective-permute-done((bf16[1,88,256]{2,1,0:T(8,128)(2,1)S(1)}, bf16[1,88,256]{2,1,0:T(8,128)(2,1)S(1)}, u32[]{:S(2)}, u32[]{:S(2)}) %collective-permute-start.9) | collective-permute-done | bytes 45088 | tf_op jit(solution)/shard_map/ppermute | solution.py:29
  19.8 0.2 far_lasts.1.early
  20.0 0.0 collective-permute-done.8.other
  20.0 0.3 %near_lasts.1.early = f32[72,144]{1,0:T(8,128)S(1)} custom-call(bf16[2,88,256]{2,1,0:T(8,128)(2,1)S(1)} %constant_dynamic-update-slice_fusion.mine, bf16[2,88,256]{2,1,0:T(8,128)(2,1)S(1)} %collective-permute-done.8.other, bf16[4,2,144,144]{3,2,1,0:T(8,128)(2,1)S(1)} %get-tuple-element.9.rhs, f32[72,144]{1,0:T(8,128)S(1)} %far_lasts.1.early), custom_call_target="tpu_custom_call" | custom-call | tf_op jit(solution)/shard_map/near_lasts/pallas_call | solution.py:290
  20.3 0.2 %collective-permute-done.7.panel = bf16[1,88,256]{2,1,0:T(8,128)(2,1)S(1)} collective-permute-done((bf16[1,88,256]{2,1,0:T(8,128)(2,1)S(1)}, bf16[1,88,256]{2,1,0:T(8,128)(2,1)S(1)}, u32[]{:S(2)}, u32[]{:S(2)}) %collective-permute-start.7) | collective-permute-done | bytes 45088 | tf_op jit(solution)/shard_map/ppermute | solution.py:29
  20.5 0.8 %late_lasts.1 = f32[72,144]{1,0:T(8,128)} custom-call(bf16[1,88,256]{2,1,0:T(8,128)(2,1)S(1)} %collective-permute-done.7.panel, bf16[4,2,144,144]{3,2,1,0:T(8,128)(2,1)S(1)} %get-tuple-element.9.rhs, f32[72,144]{1,0:T(8,128)S(1)} %near_lasts.1.early), custom_call_target="tpu_custom_call" | custom-call | tf_op jit(solution)/shard_map/late_lasts/pallas_call | solution.py:290
  (5 shorter events, 0.0 us)
Async XLA Ops:
  0.9 7.2 %collective-permute-start.3 = (bf16[1,88,256]{2,1,0:T(8,128)(2,1)S(1)}, bf16[1,88,256]{2,1,0:T(8,128)(2,1)S(1)}, u32[]{:S(2)}, u32[]{:S(2)}) collective-permute-start(bf16[1,88,256]{2,1,0:T(8,128)(2,1)S(1)} %pack.1.own_ref), channel_id=1, source_target_pairs={{24,0},{0,8},{8,16},{16,24},{25,1},{1,9},{9,17},{17,25},{26,2},{2,... | collective-permute-start | bytes 135176 | tf_op jit(solution)/shard_map/ppermute | solution.py:34
  4.0 4.5 %collective-permute-start.2 = (bf16[1,88,256]{2,1,0:T(8,128)(2,1)S(1)}, bf16[1,88,256]{2,1,0:T(8,128)(2,1)S(1)}, u32[]{:S(2)}, u32[]{:S(2)}) collective-permute-start(bf16[1,88,256]{2,1,0:T(8,128)(2,1)S(1)} %pack.1.own_ref), channel_id=1, source_target_pairs={{8,0},{16,8},{24,16},{0,24},{9,1},{17,9},{25,17},{1,25},{10,2},{18... | collective-permute-start | bytes 135176 | tf_op jit(solution)/shard_map/ppermute | solution.py:34
  6.1 5.1 %collective-permute-start.4 = (bf16[1,88,256]{2,1,0:T(8,128)(2,1)S(1)}, bf16[1,88,256]{2,1,0:T(8,128)(2,1)S(1)}, u32[]{:S(2)}, u32[]{:S(2)}) collective-permute-start(bf16[1,88,256]{2,1,0:T(8,128)(2,1)S(1)} %pack.1.own_ref), channel_id=1, source_target_pairs={{16,0},{24,8},{0,16},{8,24},{17,1},{25,9},{1,17},{9,25},{18,2},{26... | collective-permute-start | bytes 135176 | tf_op jit(solution)/shard_map/ppermute | solution.py:34
  7.0 3.9 %collective-permute-start = (bf16[1,88,256]{2,1,0:T(8,128)(2,1)S(1)}, bf16[1,88,256]{2,1,0:T(8,128)(2,1)S(1)}, u32[]{:S(2)}, u32[]{:S(2)}) collective-permute-start(bf16[1,88,256]{2,1,0:T(8,128)(2,1)S(1)} %pack.1.own_ref), channel_id=1, source_target_pairs={{0,6},{2,4},{4,2},{6,0},{1,7},{3,5},{5,3},{7,1},{8,14},{10,12},{12... | collective-permute-start | bytes 135176 | tf_op jit(solution)/shard_map/ppermute | solution.py:29
  8.5 6.7 %collective-permute-start.5 = (bf16[3,88,256]{2,1,0:T(8,128)(2,1)S(1)}, bf16[3,88,256]{2,1,0:T(8,128)(2,1)S(1)}, u32[]{:S(2)}, u32[]{:S(2)}) collective-permute-start(bf16[3,88,256]{2,1,0:T(8,128)(2,1)S(1)} %pad_maximum_fusion.refs_0_), channel_id=1, source_target_pairs={{0,1},{1,0},{2,3},{3,2},{4,5},{5,4},{6,7},{7,6},{8,9},{9,8},{10,11... | collective-permute-start | bytes 405512 | tf_op jit(solution)/shard_map/ppermute | solution.py:29
  11.0 4.3 %collective-permute-start.1 = (bf16[2,88,256]{2,1,0:T(8,128)(2,1)S(1)}, bf16[2,88,256]{2,1,0:T(8,128)(2,1)S(1)}, u32[]{:S(2)}, u32[]{:S(2)}) collective-permute-start(bf16[2,88,256]{2,1,0:T(8,128)(2,1)S(1)} %pad_maximum_fusion.1.own), channel_id=1, source_target_pairs={{0,2},{2,0},{4,6},{6,4},{1,3},{3,1},{5,7},{7,5},{8,10},{10,8},{12,... | collective-permute-start | bytes 270344 | tf_op jit(solution)/shard_map/ppermute | solution.py:29
  11.2 4.0 %collective-permute-start.6 = (bf16[1,88,256]{2,1,0:T(8,128)(2,1)S(1)}, bf16[1,88,256]{2,1,0:T(8,128)(2,1)S(1)}, u32[]{:S(2)}, u32[]{:S(2)}) collective-permute-start(bf16[1,88,256]{2,1,0:T(8,128)(2,1)S(1)} %collective-permute-done.4.refs_1_), channel_id=1, source_target_pairs={{0,1},{1,0},{2,3},{3,2},{4,5},{5,4},{6,7},{7,6},{8,9},{9,8},{10,11... | collective-permute-start | bytes 135176 | tf_op jit(solution)/shard_map/ppermute | solution.py:29
  15.8 4.0 %collective-permute-start.9 = (bf16[1,88,256]{2,1,0:T(8,128)(2,1)S(1)}, bf16[1,88,256]{2,1,0:T(8,128)(2,1)S(1)}, u32[]{:S(2)}, u32[]{:S(2)}) collective-permute-start(bf16[1,88,256]{2,1,0:T(8,128)(2,1)S(1)} %get-tuple-element.8), channel_id=1, source_target_pairs={{0,6},{2,4},{4,2},{6,0},{1,7},{3,5},{5,3},{7,1},{8,14},{10,12},{12... | collective-permute-start | bytes 135176 | tf_op jit(solution)/shard_map/ppermute | solution.py:29
  15.9 4.6 %collective-permute-start.7 = (bf16[1,88,256]{2,1,0:T(8,128)(2,1)S(1)}, bf16[1,88,256]{2,1,0:T(8,128)(2,1)S(1)}, u32[]{:S(2)}, u32[]{:S(2)}) collective-permute-start(bf16[1,88,256]{2,1,0:T(8,128)(2,1)S(1)} %get-tuple-element.8), channel_id=1, source_target_pairs={{0,4},{2,6},{4,0},{6,2},{1,5},{3,7},{5,1},{7,3},{8,12},{10,14},{12... | collective-permute-start | bytes 135176 | tf_op jit(solution)/shard_map/ppermute | solution.py:29
  17.4 2.5 %collective-permute-start.8 = (bf16[2,88,256]{2,1,0:T(8,128)(2,1)S(1)}, bf16[2,88,256]{2,1,0:T(8,128)(2,1)S(1)}, u32[]{:S(2)}, u32[]{:S(2)}) collective-permute-start(bf16[2,88,256]{2,1,0:T(8,128)(2,1)S(1)} %constant_dynamic-update-slice_fusion.mine), channel_id=1, source_target_pairs={{0,2},{2,0},{4,6},{6,4},{1,3},{3,1},{5,7},{7,5},{8,10},{10,8},{12,... | collective-permute-start | bytes 270344 | tf_op jit(solution)/shard_map/ppermute | solution.py:29

commit v7 on v6

--- a/solution.py
+++ b/solution.py
@@ -10,6 +10,7 @@
 BLOCK = 128
 LANES = 128
 FOLD = 16
+TALL_FOLD = 24
 HBM = pl.BlockSpec(memory_space=pltpu.HBM)
 VMEM = pl.BlockSpec(memory_space=pltpu.VMEM)
 PARAMS = pltpu.CompilerParams(vmem_limit_bytes=48 * 1024 * 1024)
@@ -60,13 +61,13 @@
     return jnp.concatenate([value[at : at + FOLD] for at in range(0, rows, FOLD)], axis=1)
 
 
-def unfold(value, rows, lanes):
-    groups = [value[:, k * lanes : (k + 1) * lanes] for k in range(-(-rows // FOLD))]
+def unfold(value, rows, lanes, deep=FOLD):
+    groups = [value[:, k * lanes : (k + 1) * lanes] for k in range(-(-rows // deep))]
     return jnp.concatenate(groups, axis=0)[:rows]
 
 
 def pack_kernel(
-    x_hbm, t_hbm, fill_x_hbm, fill_t_hbm, out_ref, x_ref, t_ref, fill_x_ref, fill_t_ref, sems
+    packer, x_hbm, t_hbm, fill_x_hbm, fill_t_hbm, out_ref, x_ref, t_ref, fill_x_ref, fill_t_ref, sems
 ):
     rows, width = x_ref.shape
     pairs = ((fill_x_hbm, fill_x_ref), (fill_t_hbm, fill_t_ref), (x_hbm, x_ref), (t_hbm, t_ref))
@@ -81,19 +82,29 @@
     copies[2].wait()
     copies[3].wait()
     masked = [x_ref[...].astype(jnp.float32) * masks[0], t_ref[...].astype(jnp.float32) * masks[1]]
-    pack(out_ref, masked, width)
+    packer(out_ref, masked, width)
 
 
 def natural(block, rows, width, total):
-    main, rem, lead = split(width)
-    parts = [block[lead : lead + rows, k * main : (k + 1) * main] for k in range(total)]
-    if rem:
-        rems = unfold(block[:lead], rows, total * rem)
-        parts = [
-            jnp.concatenate([part, rems[:, k * rem : (k + 1) * rem]], axis=1)
-            for k, part in enumerate(parts)
-        ]
-    return parts
+    _, rem, _ = split(width)
+    rems = unfold(block[:TALL_FOLD], rows, total * rem, TALL_FOLD)
+    mains = [block[TALL_FOLD + k * rows : TALL_FOLD + (k + 1) * rows] for k in range(total)]
+    return [
+        jnp.concatenate([main, rems[:, k * rem : (k + 1) * rem]], axis=1)
+        for k, main in enumerate(mains)
+    ]
+
+
+def tall_pack(out_ref, values, width):
+    main, rem, _ = split(width)
+    rows, lanes = values[0].shape[0], rem * len(values)
+    for k, value in enumerate(values):
+        top = TALL_FOLD + k * rows
+        out_ref[0, top : top + rows, :] = value[:, :main].astype(out_ref.dtype)
+        for at in range(0, rows, TALL_FOLD):
+            deep, left = min(TALL_FOLD, rows - at), at // TALL_FOLD * lanes + k * rem
+            part = value[at : at + deep, main:].astype(out_ref.dtype)
+            out_ref[0, :deep, left : left + rem] = part
 
 
 def pack(out_ref, values, width):
@@ -235,7 +246,7 @@
 def firsts_kernel(offsets, width, own, beside, *refs):
     mine, others = refs[: len(offsets)], refs[len(offsets) : 2 * len(offsets)]
     out_ref, low_ref, rhs, lhs = refs[2 * len(offsets) :]
-    rows = own.shape[1] - split(width)[2]
+    rows = (own.shape[1] - TALL_FOLD) // 2
     top = aligned(rows)
     my_col = lax.axis_index("col")
     for ref, across in ((own, 0), (beside, 1)):
@@ -248,20 +259,23 @@
         terms = add_panels(row_offsets, left, right, lhs, rhs, width, rows)
         square, cross = square + terms[0], cross + terms[1]
     high = cross.astype(jnp.bfloat16).astype(jnp.float32)
-    pack(out_ref, (high, square), width)
-    lead = split(width)[2]
+    tall_pack(out_ref, (high, square), width)
+    low = (cross - high).astype(low_ref.dtype)
     low_ref[...] = jnp.zeros_like(low_ref)
-    low_ref[0, lead:, :width] = (cross - high).astype(low_ref.dtype)
+    low_ref[0, TALL_FOLD : TALL_FOLD + rows, :] = low[:, :LANES]
+    low_ref[0, TALL_FOLD + rows :, : width - LANES] = low[:, LANES:]
 
 
 def panel_terms(col, block, low, rhs, width, rows):
-    main, rem, lead = split(width)
-    total = times(block[lead : lead + rows, :main], rhs[col, 0, :main])
-    total += times(block[lead : lead + rows, main : 2 * main], rhs[col, 1, :main])
+    main, rem, _ = split(width)
+    first, second = TALL_FOLD, TALL_FOLD + rows
+    total = times(block[first:second], rhs[col, 0, :main])
+    total += times(block[second:], rhs[col, 1, :main])
     ends = jnp.concatenate([rhs[col, 0, main:], rhs[col, 1, main:]], axis=0)
-    total += times(unfold(block[:lead], rows, 2 * rem), ends)
+    total += times(unfold(block[:first], rows, 2 * rem, TALL_FOLD), ends)
     if low is not None:
-        total += times(low[lead:, :width], rhs[col, 0])
+        total += times(low[first:second], rhs[col, 0, :main])
+        total += times(low[second:, :rem], rhs[col, 0, main:])
     return total
 
 
@@ -368,10 +382,14 @@
 
 def body(x_matrix, tangent, fill_x, fill_t):
     rows, width = x_matrix.shape
-    main, _, lead = split(width)
+    sizes = tuple(lax.axis_size(a) for a in ("row", "col", "depth"))
+    main, rem, lead = split(width)
+    fast = sizes == (4, 4, 2) and main == LANES and rem > 0 and rows % TALL_FOLD == 0
+    fast = fast and 2 * rem * (rows // TALL_FOLD) <= LANES
+    packed = (TALL_FOLD + 2 * rows, LANES) if fast else (lead + rows, 2 * main)
     block = pl.pallas_call(
-        pack_kernel,
-        out_shape=jax.ShapeDtypeStruct((1, lead + rows, 2 * main), jnp.bfloat16),
+        functools.partial(pack_kernel, tall_pack if fast else pack),
+        out_shape=jax.ShapeDtypeStruct((1, *packed), jnp.bfloat16),
         in_specs=[HBM] * 4,
         out_specs=VMEM,
         scratch_shapes=[
@@ -384,8 +402,7 @@
         compiler_params=PARAMS,
         name="pack",
     )(*(pltpu.with_memory_space_constraint(a, pltpu.HBM) for a in (x_matrix, tangent, fill_x, fill_t)))
-    sizes = tuple(lax.axis_size(a) for a in ("row", "col", "depth"))
-    return (fast_body if sizes == (4, 4, 2) else general_body)(block, rows, width)
+    return (fast_body if fast else general_body)(block, rows, width)
 
 
 def solution(mesh):

time: 21.5 us -> 21.3 us (level)
  no operation moved by 1% of the time
where the time goes in v7:
time: 21.3 us; the launch traced here: 21.1 us
  starting transfers between devices  11.5 us (54%)
  waiting for transfers between devices  6.75 us (32%)
  Pallas kernels  2.76 us (13%)
    ppermute x3, starting transfers between devices, turn(): lax.ppermute(value, axis, [((i + offset) % size, i) for i in range(size)])  6.11 us
    ppermute x7, starting transfers between devices, swap(): return lax.ppermute(value, axis, [(i, i ^ offset) for i in range(size)])  5.43 us
    ppermute x7, waiting for transfers between devices, swap(): return lax.ppermute(value, axis, [(i, i ^ offset) for i in range(size)])  5.39 us
    pallas_call x4, Pallas kernels, call(): pl.pallas_call(kernel, out_shape=out_shape, in_specs=[VMEM] * len(operand...  1.85 us
    ppermute x3, waiting for transfers between devices, turn(): lax.ppermute(value, axis, [((i + offset) % size, i) for i in range(size)])  1.36 us
    pallas_call x1, Pallas kernels, body(): pl.pallas_call(functools.partial(pack_kernel, tall_pack if fast else pack...  0.91 us
  transfers between devices with their start and end apart: 10, of which 6 were waited for; matrix products, arithmetic and copies ran while one was open for 0% of the time, Pallas kernels for 2%

profile of v7, /device:TPU:0, one launch (start us, length us, event | category | flops | bytes accessed | tf_op | source)
XLA Modules:
  0.0 21.1 jit_solution(14554752256151388868)
XLA Ops:
  0.0 0.9 %pack.1.own_ref = bf16[1,168,128]{2,1,0:T(8,128)(2,1)S(1)} custom-call(bf16[72,144]{1,0:T(8,128)(2,1)} %x_hbm.1, bf16[72,144]{1,0:T(8,128)(2,1)} %t_hbm.1, s32[5,5]{1,0:T(8,128)} %fill_x_hbm.1, s32[5,5]{1,0:T(8,128)} %fill_t_hbm.1), custom_call_target="tpu_custom_call" | custom-call | tf_op jit(solution)/shard_map/pack/pallas_call | solution.py:390
  0.9 3.1 %collective-permute-start.3 = (bf16[1,168,128]{2,1,0:T(8,128)(2,1)S(1)}, bf16[1,168,128]{2,1,0:T(8,128)(2,1)S(1)}, u32[]{:S(2)}, u32[]{:S(2)}) collective-permute-start(bf16[1,168,128]{2,1,0:T(8,128)(2,1)S(1)} %pack.1.own_ref), channel_id=1, source_target_pairs={{24,0},{0,8},{8,16},{16,24},{25,1},{1,9},{9,17},{17,25},{26,2},{2,... | collective-permute-start | bytes 129032 | tf_op jit(solution)/shard_map/ppermute | solution.py:35
  4.0 2.1 %collective-permute-start.2 = (bf16[1,168,128]{2,1,0:T(8,128)(2,1)S(1)}, bf16[1,168,128]{2,1,0:T(8,128)(2,1)S(1)}, u32[]{:S(2)}, u32[]{:S(2)}) collective-permute-start(bf16[1,168,128]{2,1,0:T(8,128)(2,1)S(1)} %pack.1.own_ref), channel_id=1, source_target_pairs={{8,0},{16,8},{24,16},{0,24},{9,1},{17,9},{25,17},{1,25},{10,2},{18... | collective-permute-start | bytes 129032 | tf_op jit(solution)/shard_map/ppermute | solution.py:35
  6.1 0.9 %collective-permute-start.4 = (bf16[1,168,128]{2,1,0:T(8,128)(2,1)S(1)}, bf16[1,168,128]{2,1,0:T(8,128)(2,1)S(1)}, u32[]{:S(2)}, u32[]{:S(2)}) collective-permute-start(bf16[1,168,128]{2,1,0:T(8,128)(2,1)S(1)} %pack.1.own_ref), channel_id=1, source_target_pairs={{16,0},{24,8},{0,16},{8,24},{17,1},{25,9},{1,17},{9,25},{18,2},{26... | collective-permute-start | bytes 129032 | tf_op jit(solution)/shard_map/ppermute | solution.py:35
  7.0 0.1 collective-permute-start
  7.1 1.0 %collective-permute-done.3 = bf16[1,168,128]{2,1,0:T(8,128)(2,1)S(1)} collective-permute-done((bf16[1,168,128]{2,1,0:T(8,128)(2,1)S(1)}, bf16[1,168,128]{2,1,0:T(8,128)(2,1)S(1)}, u32[]{:S(2)}, u32[]{:S(2)}) %collective-permute-start.3) | collective-permute-done | bytes 43040 | tf_op jit(solution)/shard_map/ppermute | solution.py:35
  8.1 0.4 %collective-permute-done.2 = bf16[1,168,128]{2,1,0:T(8,128)(2,1)S(1)} collective-permute-done((bf16[1,168,128]{2,1,0:T(8,128)(2,1)S(1)}, bf16[1,168,128]{2,1,0:T(8,128)(2,1)S(1)}, u32[]{:S(2)}, u32[]{:S(2)}) %collective-permute-start.2) | collective-permute-done | bytes 43040 | tf_op jit(solution)/shard_map/ppermute | solution.py:35
  8.5 1.6 %collective-permute-start.5 = (bf16[3,168,128]{2,1,0:T(8,128)(2,1)S(1)}, bf16[3,168,128]{2,1,0:T(8,128)(2,1)S(1)}, u32[]{:S(2)}, u32[]{:S(2)}) collective-permute-start(bf16[3,168,128]{2,1,0:T(8,128)(2,1)S(1)} %pad_maximum_fusion.refs_0_), channel_id=1, source_target_pairs={{0,1},{1,0},{2,3},{3,2},{4,5},{5,4},{6,7},{7,6},{8,9},{9,8},{10,11... | collective-permute-start | bytes 387080 | tf_op jit(solution)/shard_map/ppermute | solution.py:30
  10.1 0.8 %collective-permute-done = bf16[1,168,128]{2,1,0:T(8,128)(2,1)S(1)} collective-permute-done((bf16[1,168,128]{2,1,0:T(8,128)(2,1)S(1)}, bf16[1,168,128]{2,1,0:T(8,128)(2,1)S(1)}, u32[]{:S(2)}, u32[]{:S(2)}) %collective-permute-start) | collective-permute-done | bytes 43040 | tf_op jit(solution)/shard_map/ppermute | solution.py:30
  10.9 0.2 %collective-permute-start.1 = (bf16[2,168,128]{2,1,0:T(8,128)(2,1)S(1)}, bf16[2,168,128]{2,1,0:T(8,128)(2,1)S(1)}, u32[]{:S(2)}, u32[]{:S(2)}) collective-permute-start(bf16[2,168,128]{2,1,0:T(8,128)(2,1)S(1)} %pad_maximum_fusion.1.own), channel_id=1, source_target_pairs={{0,2},{2,0},{4,6},{6,4},{1,3},{3,1},{5,7},{7,5},{8,10},{10,8},{12,... | collective-permute-start | bytes 258056 | tf_op jit(solution)/shard_map/ppermute | solution.py:30
  11.1 0.0 collective-permute-done.4.refs_1_
  11.1 1.5 %collective-permute-start.6 = (bf16[1,168,128]{2,1,0:T(8,128)(2,1)S(1)}, bf16[1,168,128]{2,1,0:T(8,128)(2,1)S(1)}, u32[]{:S(2)}, u32[]{:S(2)}) collective-permute-start(bf16[1,168,128]{2,1,0:T(8,128)(2,1)S(1)} %collective-permute-done.4.refs_1_), channel_id=1, source_target_pairs={{0,1},{1,0},{2,3},{3,2},{4,5},{5,4},{6,7},{7,6},{8,9},{9,8},{10,11... | collective-permute-start | bytes 129032 | tf_op jit(solution)/shard_map/ppermute | solution.py:30
  12.7 2.5 %collective-permute-done.6.refs_3_ = bf16[1,168,128]{2,1,0:T(8,128)(2,1)S(1)} collective-permute-done((bf16[1,168,128]{2,1,0:T(8,128)(2,1)S(1)}, bf16[1,168,128]{2,1,0:T(8,128)(2,1)S(1)}, u32[]{:S(2)}, u32[]{:S(2)}) %collective-permute-start.6) | collective-permute-done | bytes 43040 | tf_op jit(solution)/shard_map/ppermute | solution.py:30
  15.2 0.0 collective-permute-done.1.beside
  15.2 0.0 collective-permute-done.5.refs_2_
  15.2 0.6 %firsts.1 = (bf16[1,168,128]{2,1,0:T(8,128)(2,1)S(1)}, bf16[1,168,128]{2,1,0:T(8,128)(2,1)S(1)}, bf16[4,2,144,144]{3,2,1,0:T(8,128)(2,1)S(1)}) custom-call(bf16[2,168,128]{2,1,0:T(8,128)(2,1)S(1)} %pad_maximum_fusion.1.own, bf16[2,168,128]{2,1,0:T(8,128)(2,1)S(1)} %collective-permute-done.1.beside, bf16[3,168,128]{2,1,0:T(8,128)(2,1)S(1)} %pad_maximum_fusion.refs_0_, ...), custom_call_target="tpu_custom_call" | custom-call | tf_op jit(solution)/shard_map/firsts/pallas_call | solution.py:304
  15.8 0.1 collective-permute-start.9
  15.8 1.6 %collective-permute-start.7 = (bf16[1,168,128]{2,1,0:T(8,128)(2,1)S(1)}, bf16[1,168,128]{2,1,0:T(8,128)(2,1)S(1)}, u32[]{:S(2)}, u32[]{:S(2)}) collective-permute-start(bf16[1,168,128]{2,1,0:T(8,128)(2,1)S(1)} %get-tuple-element.8), channel_id=1, source_target_pairs={{0,4},{2,6},{4,0},{6,2},{1,5},{3,7},{5,1},{7,3},{8,12},{10,14},{12... | collective-permute-start | bytes 129032 | tf_op jit(solution)/shard_map/ppermute | solution.py:30
  17.4 0.3 %collective-permute-start.8 = (bf16[2,168,128]{2,1,0:T(8,128)(2,1)S(1)}, bf16[2,168,128]{2,1,0:T(8,128)(2,1)S(1)}, u32[]{:S(2)}, u32[]{:S(2)}) collective-permute-start(bf16[2,168,128]{2,1,0:T(8,128)(2,1)S(1)} %constant_dynamic-update-slice_fusion.mine), channel_id=1, source_target_pairs={{0,2},{2,0},{4,6},{6,4},{1,3},{3,1},{5,7},{7,5},{8,10},{10,8},{12,... | collective-permute-start | bytes 258056 | tf_op jit(solution)/shard_map/ppermute | solution.py:30
  17.8 1.9 %collective-permute-done.9.panel = bf16[1,168,128]{2,1,0:T(8,128)(2,1)S(1)} collective-permute-done((bf16[1,168,128]{2,1,0:T(8,128)(2,1)S(1)}, bf16[1,168,128]{2,1,0:T(8,128)(2,1)S(1)}, u32[]{:S(2)}, u32[]{:S(2)}) %collective-permute-start.9) | collective-permute-done | bytes 43040 | tf_op jit(solution)/shard_map/ppermute | solution.py:30
  19.7 0.2 far_lasts.1.early
  19.9 0.2 %near_lasts.1.early = f32[72,144]{1,0:T(8,128)S(1)} custom-call(bf16[2,168,128]{2,1,0:T(8,128)(2,1)S(1)} %constant_dynamic-update-slice_fusion.mine, bf16[2,168,128]{2,1,0:T(8,128)(2,1)S(1)} %collective-permute-done.8.other, bf16[4,2,144,144]{3,2,1,0:T(8,128)(2,1)S(1)} %get-tuple-element.9.rhs, f32[72,144]{1,0:T(8,128)S(1)} %far_lasts.1.early), custom_call_target="tpu_custom_call" | custom-call | tf_op jit(solution)/shard_map/near_lasts/pallas_call | solution.py:304
  20.1 0.2 collective-permute-done.7.panel
  20.3 0.8 %late_lasts.1 = f32[72,144]{1,0:T(8,128)} custom-call(bf16[1,168,128]{2,1,0:T(8,128)(2,1)S(1)} %collective-permute-done.7.panel, bf16[4,2,144,144]{3,2,1,0:T(8,128)(2,1)S(1)} %get-tuple-element.9.rhs, f32[72,144]{1,0:T(8,128)S(1)} %near_lasts.1.early), custom_call_target="tpu_custom_call" | custom-call | tf_op jit(solution)/shard_map/late_lasts/pallas_call | solution.py:304
  (5 shorter events, 0.0 us)
Async XLA Ops:
  0.9 7.2 %collective-permute-start.3 = (bf16[1,168,128]{2,1,0:T(8,128)(2,1)S(1)}, bf16[1,168,128]{2,1,0:T(8,128)(2,1)S(1)}, u32[]{:S(2)}, u32[]{:S(2)}) collective-permute-start(bf16[1,168,128]{2,1,0:T(8,128)(2,1)S(1)} %pack.1.own_ref), channel_id=1, source_target_pairs={{24,0},{0,8},{8,16},{16,24},{25,1},{1,9},{9,17},{17,25},{26,2},{2,... | collective-permute-start | bytes 129032 | tf_op jit(solution)/shard_map/ppermute | solution.py:35
  4.0 4.5 %collective-permute-start.2 = (bf16[1,168,128]{2,1,0:T(8,128)(2,1)S(1)}, bf16[1,168,128]{2,1,0:T(8,128)(2,1)S(1)}, u32[]{:S(2)}, u32[]{:S(2)}) collective-permute-start(bf16[1,168,128]{2,1,0:T(8,128)(2,1)S(1)} %pack.1.own_ref), channel_id=1, source_target_pairs={{8,0},{16,8},{24,16},{0,24},{9,1},{17,9},{25,17},{1,25},{10,2},{18... | collective-permute-start | bytes 129032 | tf_op jit(solution)/shard_map/ppermute | solution.py:35
  6.1 5.1 %collective-permute-start.4 = (bf16[1,168,128]{2,1,0:T(8,128)(2,1)S(1)}, bf16[1,168,128]{2,1,0:T(8,128)(2,1)S(1)}, u32[]{:S(2)}, u32[]{:S(2)}) collective-permute-start(bf16[1,168,128]{2,1,0:T(8,128)(2,1)S(1)} %pack.1.own_ref), channel_id=1, source_target_pairs={{16,0},{24,8},{0,16},{8,24},{17,1},{25,9},{1,17},{9,25},{18,2},{26... | collective-permute-start | bytes 129032 | tf_op jit(solution)/shard_map/ppermute | solution.py:35
  7.0 3.9 %collective-permute-start = (bf16[1,168,128]{2,1,0:T(8,128)(2,1)S(1)}, bf16[1,168,128]{2,1,0:T(8,128)(2,1)S(1)}, u32[]{:S(2)}, u32[]{:S(2)}) collective-permute-start(bf16[1,168,128]{2,1,0:T(8,128)(2,1)S(1)} %pack.1.own_ref), channel_id=1, source_target_pairs={{0,6},{2,4},{4,2},{6,0},{1,7},{3,5},{5,3},{7,1},{8,14},{10,12},{12... | collective-permute-start | bytes 129032 | tf_op jit(solution)/shard_map/ppermute | solution.py:30
  8.5 6.7 %collective-permute-start.5 = (bf16[3,168,128]{2,1,0:T(8,128)(2,1)S(1)}, bf16[3,168,128]{2,1,0:T(8,128)(2,1)S(1)}, u32[]{:S(2)}, u32[]{:S(2)}) collective-permute-start(bf16[3,168,128]{2,1,0:T(8,128)(2,1)S(1)} %pad_maximum_fusion.refs_0_), channel_id=1, source_target_pairs={{0,1},{1,0},{2,3},{3,2},{4,5},{5,4},{6,7},{7,6},{8,9},{9,8},{10,11... | collective-permute-start | bytes 387080 | tf_op jit(solution)/shard_map/ppermute | solution.py:30
  10.9 4.3 %collective-permute-start.1 = (bf16[2,168,128]{2,1,0:T(8,128)(2,1)S(1)}, bf16[2,168,128]{2,1,0:T(8,128)(2,1)S(1)}, u32[]{:S(2)}, u32[]{:S(2)}) collective-permute-start(bf16[2,168,128]{2,1,0:T(8,128)(2,1)S(1)} %pad_maximum_fusion.1.own), channel_id=1, source_target_pairs={{0,2},{2,0},{4,6},{6,4},{1,3},{3,1},{5,7},{7,5},{8,10},{10,8},{12,... | collective-permute-start | bytes 258056 | tf_op jit(solution)/shard_map/ppermute | solution.py:30
  11.1 4.0 %collective-permute-start.6 = (bf16[1,168,128]{2,1,0:T(8,128)(2,1)S(1)}, bf16[1,168,128]{2,1,0:T(8,128)(2,1)S(1)}, u32[]{:S(2)}, u32[]{:S(2)}) collective-permute-start(bf16[1,168,128]{2,1,0:T(8,128)(2,1)S(1)} %collective-permute-done.4.refs_1_), channel_id=1, source_target_pairs={{0,1},{1,0},{2,3},{3,2},{4,5},{5,4},{6,7},{7,6},{8,9},{9,8},{10,11... | collective-permute-start | bytes 129032 | tf_op jit(solution)/shard_map/ppermute | solution.py:30
  15.8 3.9 %collective-permute-start.9 = (bf16[1,168,128]{2,1,0:T(8,128)(2,1)S(1)}, bf16[1,168,128]{2,1,0:T(8,128)(2,1)S(1)}, u32[]{:S(2)}, u32[]{:S(2)}) collective-permute-start(bf16[1,168,128]{2,1,0:T(8,128)(2,1)S(1)} %get-tuple-element.8), channel_id=1, source_target_pairs={{0,6},{2,4},{4,2},{6,0},{1,7},{3,5},{5,3},{7,1},{8,14},{10,12},{12... | collective-permute-start | bytes 129032 | tf_op jit(solution)/shard_map/ppermute | solution.py:30
  15.8 4.5 %collective-permute-start.7 = (bf16[1,168,128]{2,1,0:T(8,128)(2,1)S(1)}, bf16[1,168,128]{2,1,0:T(8,128)(2,1)S(1)}, u32[]{:S(2)}, u32[]{:S(2)}) collective-permute-start(bf16[1,168,128]{2,1,0:T(8,128)(2,1)S(1)} %get-tuple-element.8), channel_id=1, source_target_pairs={{0,4},{2,6},{4,0},{6,2},{1,5},{3,7},{5,1},{7,3},{8,12},{10,14},{12... | collective-permute-start | bytes 129032 | tf_op jit(solution)/shard_map/ppermute | solution.py:30
  17.4 2.4 %collective-permute-start.8 = (bf16[2,168,128]{2,1,0:T(8,128)(2,1)S(1)}, bf16[2,168,128]{2,1,0:T(8,128)(2,1)S(1)}, u32[]{:S(2)}, u32[]{:S(2)}) collective-permute-start(bf16[2,168,128]{2,1,0:T(8,128)(2,1)S(1)} %constant_dynamic-update-slice_fusion.mine), channel_id=1, source_target_pairs={{0,2},{2,0},{4,6},{6,4},{1,3},{3,1},{5,7},{7,5},{8,10},{10,8},{12,... | collective-permute-start | bytes 258056 | tf_op jit(solution)/shard_map/ppermute | solution.py:30

commit v8 on v7

--- a/solution.py
+++ b/solution.py
@@ -286,18 +286,30 @@
     out_ref[...] = 1.5 * own - 0.5 * terms
 
 
-def near_lasts_kernel(width, mine, other, rhs, early, out_ref):
+def near_lasts_kernel(width, mine, other, rhs, early, out_ref, ends_ref):
     rows = out_ref.shape[0]
     my_col = lax.axis_index("col")
     terms = panel_terms(my_col, mine[0], mine[1], rhs, width, rows)
     terms += panel_terms(my_col ^ 1, other[0], other[1], rhs, width, rows)
     out_ref[...] = early[...] - 0.5 * terms
-
-
-def late_lasts_kernel(offset, width, panel, rhs, early, out_ref):
-    rows = out_ref.shape[0]
-    terms = panel_terms(lax.axis_index("col") ^ offset, panel[0], None, rhs, width, rows)
-    out_ref[...] = early[...] - 0.5 * terms
+    main, rem, _ = split(width)
+    col = my_col ^ 2
+    ends_ref[...] = jnp.zeros_like(ends_ref)
+    for group in range(ends_ref.shape[0]):
+        for which in range(2):
+            at = (2 * group + which) * rem
+            ends_ref[group, at : at + rem] = rhs[col, which, main:]
+
+
+def late_lasts_kernel(offset, width, panel, rhs, early, ends, out_ref):
+    rows, main = out_ref.shape[0], split(width)[0]
+    col = lax.axis_index("col") ^ offset
+    first, second = TALL_FOLD, TALL_FOLD + rows
+    terms = times(panel[0, first:second], rhs[col, 0, :main])
+    terms += times(panel[0, second:], rhs[col, 1, :main])
+    folded = panel[0, :first, : ends.shape[1]]
+    groups = [times(folded, ends[group]) for group in range(ends.shape[0])]
+    out_ref[...] = early[...] - 0.5 * (terms + jnp.concatenate(groups, axis=0))
 
 
 def call(kernel, name, out_shape, operands, scratch=(), **kwargs):
@@ -336,9 +348,13 @@
     mine = jnp.concatenate([firsts, low], axis=0)
     near = (mine, swap(mine, "col", 1))
     far = call(functools.partial(far_lasts_kernel, 3, width), "far_lasts", out, (straight, rhs, block), cost_estimate=pl.CostEstimate(flops=1000000000, bytes_accessed=0, transcendentals=0),)
-    total = call(functools.partial(near_lasts_kernel, width), "near_lasts", out, (*near, rhs, far), )
+    rem, groups = split(width)[1], rows // TALL_FOLD
+    ends = shape((groups, groups * 2 * rem, width), block.dtype)
+    total, ends = call(
+        functools.partial(near_lasts_kernel, width), "near_lasts", (out, ends), (*near, rhs, far)
+    )
     return call(
-        functools.partial(late_lasts_kernel, 2, width), "late_lasts", out, (crossed, rhs, total)
+        functools.partial(late_lasts_kernel, 2, width), "late_lasts", out, (crossed, rhs, total, ends)
     )
 
 

time: 21.3 us -> 21.3 us (level)
  no operation moved by 1% of the time
where the time goes in v8:
time: 21.3 us; the launch traced here: 21.1 us
  starting transfers between devices  11.5 us (54%)
  waiting for transfers between devices  6.75 us (32%)
  Pallas kernels  2.74 us (13%)
    ppermute x3, starting transfers between devices, turn(): lax.ppermute(value, axis, [((i + offset) % size, i) for i in range(size)])  6.11 us
    ppermute x7, starting transfers between devices, swap(): return lax.ppermute(value, axis, [(i, i ^ offset) for i in range(size)])  5.43 us
    ppermute x7, waiting for transfers between devices, swap(): return lax.ppermute(value, axis, [(i, i ^ offset) for i in range(size)])  5.39 us
    pallas_call x4, Pallas kernels, call(): pl.pallas_call(kernel, out_shape=out_shape, in_specs=[VMEM] * len(operand...  1.84 us
    ppermute x3, waiting for transfers between devices, turn(): lax.ppermute(value, axis, [((i + offset) % size, i) for i in range(size)])  1.36 us
    pallas_call x1, Pallas kernels, body(): pl.pallas_call(functools.partial(pack_kernel, tall_pack if fast else pack...  0.91 us
  transfers between devices with their start and end apart: 10, of which 6 were waited for; matrix products, arithmetic and copies ran while one was open for 0% of the time, Pallas kernels for 2%

profile of v8, /device:TPU:0, one launch (start us, length us, event | category | flops | bytes accessed | tf_op | source)
XLA Modules:
  0.0 21.1 jit_solution(9667637040877302097)
XLA Ops:
  0.0 0.9 %pack.1.own_ref = bf16[1,168,128]{2,1,0:T(8,128)(2,1)S(1)} custom-call(bf16[72,144]{1,0:T(8,128)(2,1)} %x_hbm.1, bf16[72,144]{1,0:T(8,128)(2,1)} %t_hbm.1, s32[5,5]{1,0:T(8,128)} %fill_x_hbm.1, s32[5,5]{1,0:T(8,128)} %fill_t_hbm.1), custom_call_target="tpu_custom_call" | custom-call | tf_op jit(solution)/shard_map/pack/pallas_call | solution.py:406
  0.9 3.1 %collective-permute-start.3 = (bf16[1,168,128]{2,1,0:T(8,128)(2,1)S(1)}, bf16[1,168,128]{2,1,0:T(8,128)(2,1)S(1)}, u32[]{:S(2)}, u32[]{:S(2)}) collective-permute-start(bf16[1,168,128]{2,1,0:T(8,128)(2,1)S(1)} %pack.1.own_ref), channel_id=1, source_target_pairs={{24,0},{0,8},{8,16},{16,24},{25,1},{1,9},{9,17},{17,25},{26,2},{2,... | collective-permute-start | bytes 129032 | tf_op jit(solution)/shard_map/ppermute | solution.py:35
  4.0 2.1 %collective-permute-start.2 = (bf16[1,168,128]{2,1,0:T(8,128)(2,1)S(1)}, bf16[1,168,128]{2,1,0:T(8,128)(2,1)S(1)}, u32[]{:S(2)}, u32[]{:S(2)}) collective-permute-start(bf16[1,168,128]{2,1,0:T(8,128)(2,1)S(1)} %pack.1.own_ref), channel_id=1, source_target_pairs={{8,0},{16,8},{24,16},{0,24},{9,1},{17,9},{25,17},{1,25},{10,2},{18... | collective-permute-start | bytes 129032 | tf_op jit(solution)/shard_map/ppermute | solution.py:35
  6.1 0.9 %collective-permute-start.4 = (bf16[1,168,128]{2,1,0:T(8,128)(2,1)S(1)}, bf16[1,168,128]{2,1,0:T(8,128)(2,1)S(1)}, u32[]{:S(2)}, u32[]{:S(2)}) collective-permute-start(bf16[1,168,128]{2,1,0:T(8,128)(2,1)S(1)} %pack.1.own_ref), channel_id=1, source_target_pairs={{16,0},{24,8},{0,16},{8,24},{17,1},{25,9},{1,17},{9,25},{18,2},{26... | collective-permute-start | bytes 129032 | tf_op jit(solution)/shard_map/ppermute | solution.py:35
  7.0 0.1 collective-permute-start
  7.1 1.0 %collective-permute-done.3 = bf16[1,168,128]{2,1,0:T(8,128)(2,1)S(1)} collective-permute-done((bf16[1,168,128]{2,1,0:T(8,128)(2,1)S(1)}, bf16[1,168,128]{2,1,0:T(8,128)(2,1)S(1)}, u32[]{:S(2)}, u32[]{:S(2)}) %collective-permute-start.3) | collective-permute-done | bytes 43040 | tf_op jit(solution)/shard_map/ppermute | solution.py:35
  8.1 0.4 %collective-permute-done.2 = bf16[1,168,128]{2,1,0:T(8,128)(2,1)S(1)} collective-permute-done((bf16[1,168,128]{2,1,0:T(8,128)(2,1)S(1)}, bf16[1,168,128]{2,1,0:T(8,128)(2,1)S(1)}, u32[]{:S(2)}, u32[]{:S(2)}) %collective-permute-start.2) | collective-permute-done | bytes 43040 | tf_op jit(solution)/shard_map/ppermute | solution.py:35
  8.5 1.6 %collective-permute-start.5 = (bf16[3,168,128]{2,1,0:T(8,128)(2,1)S(1)}, bf16[3,168,128]{2,1,0:T(8,128)(2,1)S(1)}, u32[]{:S(2)}, u32[]{:S(2)}) collective-permute-start(bf16[3,168,128]{2,1,0:T(8,128)(2,1)S(1)} %pad_maximum_fusion.refs_0_), channel_id=1, source_target_pairs={{0,1},{1,0},{2,3},{3,2},{4,5},{5,4},{6,7},{7,6},{8,9},{9,8},{10,11... | collective-permute-start | bytes 387080 | tf_op jit(solution)/shard_map/ppermute | solution.py:30
  10.1 0.8 %collective-permute-done = bf16[1,168,128]{2,1,0:T(8,128)(2,1)S(1)} collective-permute-done((bf16[1,168,128]{2,1,0:T(8,128)(2,1)S(1)}, bf16[1,168,128]{2,1,0:T(8,128)(2,1)S(1)}, u32[]{:S(2)}, u32[]{:S(2)}) %collective-permute-start) | collective-permute-done | bytes 43040 | tf_op jit(solution)/shard_map/ppermute | solution.py:30
  10.9 0.2 %collective-permute-start.1 = (bf16[2,168,128]{2,1,0:T(8,128)(2,1)S(1)}, bf16[2,168,128]{2,1,0:T(8,128)(2,1)S(1)}, u32[]{:S(2)}, u32[]{:S(2)}) collective-permute-start(bf16[2,168,128]{2,1,0:T(8,128)(2,1)S(1)} %pad_maximum_fusion.1.own), channel_id=1, source_target_pairs={{0,2},{2,0},{4,6},{6,4},{1,3},{3,1},{5,7},{7,5},{8,10},{10,8},{12,... | collective-permute-start | bytes 258056 | tf_op jit(solution)/shard_map/ppermute | solution.py:30
  11.1 0.0 collective-permute-done.4.refs_1_
  11.1 1.5 %collective-permute-start.6 = (bf16[1,168,128]{2,1,0:T(8,128)(2,1)S(1)}, bf16[1,168,128]{2,1,0:T(8,128)(2,1)S(1)}, u32[]{:S(2)}, u32[]{:S(2)}) collective-permute-start(bf16[1,168,128]{2,1,0:T(8,128)(2,1)S(1)} %collective-permute-done.4.refs_1_), channel_id=1, source_target_pairs={{0,1},{1,0},{2,3},{3,2},{4,5},{5,4},{6,7},{7,6},{8,9},{9,8},{10,11... | collective-permute-start | bytes 129032 | tf_op jit(solution)/shard_map/ppermute | solution.py:30
  12.7 2.5 %collective-permute-done.6.refs_3_ = bf16[1,168,128]{2,1,0:T(8,128)(2,1)S(1)} collective-permute-done((bf16[1,168,128]{2,1,0:T(8,128)(2,1)S(1)}, bf16[1,168,128]{2,1,0:T(8,128)(2,1)S(1)}, u32[]{:S(2)}, u32[]{:S(2)}) %collective-permute-start.6) | collective-permute-done | bytes 43040 | tf_op jit(solution)/shard_map/ppermute | solution.py:30
  15.2 0.0 collective-permute-done.1.beside
  15.2 0.0 collective-permute-done.5.refs_2_
  15.2 0.6 %firsts.1 = (bf16[1,168,128]{2,1,0:T(8,128)(2,1)S(1)}, bf16[1,168,128]{2,1,0:T(8,128)(2,1)S(1)}, bf16[4,2,144,144]{3,2,1,0:T(8,128)(2,1)S(1)}) custom-call(bf16[2,168,128]{2,1,0:T(8,128)(2,1)S(1)} %pad_maximum_fusion.1.own, bf16[2,168,128]{2,1,0:T(8,128)(2,1)S(1)} %collective-permute-done.1.beside, bf16[3,168,128]{2,1,0:T(8,128)(2,1)S(1)} %pad_maximum_fusion.refs_0_, ...), custom_call_target="tpu_custom_call" | custom-call | tf_op jit(solution)/shard_map/firsts/pallas_call | solution.py:316
  15.8 0.1 collective-permute-start.9
  15.8 1.6 %collective-permute-start.7 = (bf16[1,168,128]{2,1,0:T(8,128)(2,1)S(1)}, bf16[1,168,128]{2,1,0:T(8,128)(2,1)S(1)}, u32[]{:S(2)}, u32[]{:S(2)}) collective-permute-start(bf16[1,168,128]{2,1,0:T(8,128)(2,1)S(1)} %get-tuple-element.10), channel_id=1, source_target_pairs={{0,4},{2,6},{4,0},{6,2},{1,5},{3,7},{5,1},{7,3},{8,12},{10,14},{12... | collective-permute-start | bytes 129032 | tf_op jit(solution)/shard_map/ppermute | solution.py:30
  17.4 0.3 %collective-permute-start.8 = (bf16[2,168,128]{2,1,0:T(8,128)(2,1)S(1)}, bf16[2,168,128]{2,1,0:T(8,128)(2,1)S(1)}, u32[]{:S(2)}, u32[]{:S(2)}) collective-permute-start(bf16[2,168,128]{2,1,0:T(8,128)(2,1)S(1)} %constant_dynamic-update-slice_fusion.mine), channel_id=1, source_target_pairs={{0,2},{2,0},{4,6},{6,4},{1,3},{3,1},{5,7},{7,5},{8,10},{10,8},{12,... | collective-permute-start | bytes 258056 | tf_op jit(solution)/shard_map/ppermute | solution.py:30
  17.8 1.9 %collective-permute-done.9.panel = bf16[1,168,128]{2,1,0:T(8,128)(2,1)S(1)} collective-permute-done((bf16[1,168,128]{2,1,0:T(8,128)(2,1)S(1)}, bf16[1,168,128]{2,1,0:T(8,128)(2,1)S(1)}, u32[]{:S(2)}, u32[]{:S(2)}) %collective-permute-start.9) | collective-permute-done | bytes 43040 | tf_op jit(solution)/shard_map/ppermute | solution.py:30
  19.7 0.2 far_lasts.1.early
  19.9 0.2 %near_lasts.1 = (f32[72,144]{1,0:T(8,128)S(1)}, bf16[3,96,144]{2,1,0:T(8,128)(2,1)S(1)}) custom-call(bf16[2,168,128]{2,1,0:T(8,128)(2,1)S(1)} %constant_dynamic-update-slice_fusion.mine, bf16[2,168,128]{2,1,0:T(8,128)(2,1)S(1)} %collective-permute-done.8.other, bf16[4,2,144,144]{3,2,1,0:T(8,128)(2,1)S(1)} %get-tuple-element.11.rhs, f32[72,144]{1,0:T(8,128)S(1)} %far_lasts.1.early), custom_call_target="tpu_custom_call" | custom-call | tf_op jit(solution)/shard_map/near_lasts/pallas_call | solution.py:316
  20.1 0.2 collective-permute-done.7.panel
  20.3 0.8 %late_lasts.1 = f32[72,144]{1,0:T(8,128)} custom-call(bf16[1,168,128]{2,1,0:T(8,128)(2,1)S(1)} %collective-permute-done.7.panel, bf16[4,2,144,144]{3,2,1,0:T(8,128)(2,1)S(1)} %get-tuple-element.11.rhs, f32[72,144]{1,0:T(8,128)S(1)} %get-tuple-element.13.early, bf16[3,96,144]{2,1,0:T(8,128)(2,1)S(1)} %get-tuple-element.14.ends), custom_call_target="tpu_custom_call" | custom-call | tf_op jit(solution)/shard_map/late_lasts/pallas_call | solution.py:316
  (5 shorter events, 0.0 us)
Async XLA Ops:
  0.9 7.2 %collective-permute-start.3 = (bf16[1,168,128]{2,1,0:T(8,128)(2,1)S(1)}, bf16[1,168,128]{2,1,0:T(8,128)(2,1)S(1)}, u32[]{:S(2)}, u32[]{:S(2)}) collective-permute-start(bf16[1,168,128]{2,1,0:T(8,128)(2,1)S(1)} %pack.1.own_ref), channel_id=1, source_target_pairs={{24,0},{0,8},{8,16},{16,24},{25,1},{1,9},{9,17},{17,25},{26,2},{2,... | collective-permute-start | bytes 129032 | tf_op jit(solution)/shard_map/ppermute | solution.py:35
  4.0 4.5 %collective-permute-start.2 = (bf16[1,168,128]{2,1,0:T(8,128)(2,1)S(1)}, bf16[1,168,128]{2,1,0:T(8,128)(2,1)S(1)}, u32[]{:S(2)}, u32[]{:S(2)}) collective-permute-start(bf16[1,168,128]{2,1,0:T(8,128)(2,1)S(1)} %pack.1.own_ref), channel_id=1, source_target_pairs={{8,0},{16,8},{24,16},{0,24},{9,1},{17,9},{25,17},{1,25},{10,2},{18... | collective-permute-start | bytes 129032 | tf_op jit(solution)/shard_map/ppermute | solution.py:35
  6.1 5.1 %collective-permute-start.4 = (bf16[1,168,128]{2,1,0:T(8,128)(2,1)S(1)}, bf16[1,168,128]{2,1,0:T(8,128)(2,1)S(1)}, u32[]{:S(2)}, u32[]{:S(2)}) collective-permute-start(bf16[1,168,128]{2,1,0:T(8,128)(2,1)S(1)} %pack.1.own_ref), channel_id=1, source_target_pairs={{16,0},{24,8},{0,16},{8,24},{17,1},{25,9},{1,17},{9,25},{18,2},{26... | collective-permute-start | bytes 129032 | tf_op jit(solution)/shard_map/ppermute | solution.py:35
  7.0 3.9 %collective-permute-start = (bf16[1,168,128]{2,1,0:T(8,128)(2,1)S(1)}, bf16[1,168,128]{2,1,0:T(8,128)(2,1)S(1)}, u32[]{:S(2)}, u32[]{:S(2)}) collective-permute-start(bf16[1,168,128]{2,1,0:T(8,128)(2,1)S(1)} %pack.1.own_ref), channel_id=1, source_target_pairs={{0,6},{2,4},{4,2},{6,0},{1,7},{3,5},{5,3},{7,1},{8,14},{10,12},{12... | collective-permute-start | bytes 129032 | tf_op jit(solution)/shard_map/ppermute | solution.py:30
  8.5 6.7 %collective-permute-start.5 = (bf16[3,168,128]{2,1,0:T(8,128)(2,1)S(1)}, bf16[3,168,128]{2,1,0:T(8,128)(2,1)S(1)}, u32[]{:S(2)}, u32[]{:S(2)}) collective-permute-start(bf16[3,168,128]{2,1,0:T(8,128)(2,1)S(1)} %pad_maximum_fusion.refs_0_), channel_id=1, source_target_pairs={{0,1},{1,0},{2,3},{3,2},{4,5},{5,4},{6,7},{7,6},{8,9},{9,8},{10,11... | collective-permute-start | bytes 387080 | tf_op jit(solution)/shard_map/ppermute | solution.py:30
  10.9 4.3 %collective-permute-start.1 = (bf16[2,168,128]{2,1,0:T(8,128)(2,1)S(1)}, bf16[2,168,128]{2,1,0:T(8,128)(2,1)S(1)}, u32[]{:S(2)}, u32[]{:S(2)}) collective-permute-start(bf16[2,168,128]{2,1,0:T(8,128)(2,1)S(1)} %pad_maximum_fusion.1.own), channel_id=1, source_target_pairs={{0,2},{2,0},{4,6},{6,4},{1,3},{3,1},{5,7},{7,5},{8,10},{10,8},{12,... | collective-permute-start | bytes 258056 | tf_op jit(solution)/shard_map/ppermute | solution.py:30
  11.1 4.0 %collective-permute-start.6 = (bf16[1,168,128]{2,1,0:T(8,128)(2,1)S(1)}, bf16[1,168,128]{2,1,0:T(8,128)(2,1)S(1)}, u32[]{:S(2)}, u32[]{:S(2)}) collective-permute-start(bf16[1,168,128]{2,1,0:T(8,128)(2,1)S(1)} %collective-permute-done.4.refs_1_), channel_id=1, source_target_pairs={{0,1},{1,0},{2,3},{3,2},{4,5},{5,4},{6,7},{7,6},{8,9},{9,8},{10,11... | collective-permute-start | bytes 129032 | tf_op jit(solution)/shard_map/ppermute | solution.py:30
  15.8 3.9 %collective-permute-start.9 = (bf16[1,168,128]{2,1,0:T(8,128)(2,1)S(1)}, bf16[1,168,128]{2,1,0:T(8,128)(2,1)S(1)}, u32[]{:S(2)}, u32[]{:S(2)}) collective-permute-start(bf16[1,168,128]{2,1,0:T(8,128)(2,1)S(1)} %get-tuple-element.10), channel_id=1, source_target_pairs={{0,6},{2,4},{4,2},{6,0},{1,7},{3,5},{5,3},{7,1},{8,14},{10,12},{12... | collective-permute-start | bytes 129032 | tf_op jit(solution)/shard_map/ppermute | solution.py:30
  15.8 4.5 %collective-permute-start.7 = (bf16[1,168,128]{2,1,0:T(8,128)(2,1)S(1)}, bf16[1,168,128]{2,1,0:T(8,128)(2,1)S(1)}, u32[]{:S(2)}, u32[]{:S(2)}) collective-permute-start(bf16[1,168,128]{2,1,0:T(8,128)(2,1)S(1)} %get-tuple-element.10), channel_id=1, source_target_pairs={{0,4},{2,6},{4,0},{6,2},{1,5},{3,7},{5,1},{7,3},{8,12},{10,14},{12... | collective-permute-start | bytes 129032 | tf_op jit(solution)/shard_map/ppermute | solution.py:30
  17.4 2.4 %collective-permute-start.8 = (bf16[2,168,128]{2,1,0:T(8,128)(2,1)S(1)}, bf16[2,168,128]{2,1,0:T(8,128)(2,1)S(1)}, u32[]{:S(2)}, u32[]{:S(2)}) collective-permute-start(bf16[2,168,128]{2,1,0:T(8,128)(2,1)S(1)} %constant_dynamic-update-slice_fusion.mine), channel_id=1, source_target_pairs={{0,2},{2,0},{4,6},{6,4},{1,3},{3,1},{5,7},{7,5},{8,10},{10,8},{12,... | collective-permute-start | bytes 258056 | tf_op jit(solution)/shard_map/ppermute | solution.py:30

commit v9 on v8

--- a/solution.py
+++ b/solution.py
@@ -232,8 +232,8 @@
         for a, b in zip(
             natural(mine[k], rows, width, 2), natural(others[k], rows, width, 2), strict=True
         ):
-            a, b = a.astype(jnp.float32), b.astype(jnp.float32)
             halves = [jnp.where(my_depth == 0, a, b), jnp.where(my_depth == 0, b, a)]
+            halves = [half.astype(jnp.float32) for half in halves]
             panels.append(jnp.concatenate(halves, axis=0).astype(jnp.bfloat16))
         for which, panel in enumerate(panels):
             rhs[row, which] = panel

time: 21.3 us -> 21.3 us (level)
  no operation moved by 1% of the time
where the time goes in v9:
time: 21.3 us; the launch traced here: 21.1 us
  starting transfers between devices  11.5 us (54%)
  waiting for transfers between devices  6.75 us (32%)
  Pallas kernels  2.74 us (13%)
    ppermute x3, starting transfers between devices, turn(): lax.ppermute(value, axis, [((i + offset) % size, i) for i in range(size)])  6.11 us
    ppermute x7, starting transfers between devices, swap(): return lax.ppermute(value, axis, [(i, i ^ offset) for i in range(size)])  5.43 us
    ppermute x7, waiting for transfers between devices, swap(): return lax.ppermute(value, axis, [(i, i ^ offset) for i in range(size)])  5.39 us
    pallas_call x4, Pallas kernels, call(): pl.pallas_call(kernel, out_shape=out_shape, in_specs=[VMEM] * len(operand...  1.83 us
    ppermute x3, waiting for transfers between devices, turn(): lax.ppermute(value, axis, [((i + offset) % size, i) for i in range(size)])  1.36 us
    pallas_call x1, Pallas kernels, body(): pl.pallas_call(functools.partial(pack_kernel, tall_pack if fast else pack...  0.91 us
  transfers between devices with their start and end apart: 10, of which 6 were waited for; matrix products, arithmetic and copies ran while one was open for 0% of the time, Pallas kernels for 2%

profile of v9, /device:TPU:0, one launch (start us, length us, event | category | flops | bytes accessed | tf_op | source)
XLA Modules:
  0.0 21.1 jit_solution(4355876974752524130)
XLA Ops:
  0.0 0.9 %pack.1.own_ref = bf16[1,168,128]{2,1,0:T(8,128)(2,1)S(1)} custom-call(bf16[72,144]{1,0:T(8,128)(2,1)} %x_hbm.1, bf16[72,144]{1,0:T(8,128)(2,1)} %t_hbm.1, s32[5,5]{1,0:T(8,128)} %fill_x_hbm.1, s32[5,5]{1,0:T(8,128)} %fill_t_hbm.1), custom_call_target="tpu_custom_call" | custom-call | tf_op jit(solution)/shard_map/pack/pallas_call | solution.py:406
  0.9 3.1 %collective-permute-start.3 = (bf16[1,168,128]{2,1,0:T(8,128)(2,1)S(1)}, bf16[1,168,128]{2,1,0:T(8,128)(2,1)S(1)}, u32[]{:S(2)}, u32[]{:S(2)}) collective-permute-start(bf16[1,168,128]{2,1,0:T(8,128)(2,1)S(1)} %pack.1.own_ref), channel_id=1, source_target_pairs={{24,0},{0,8},{8,16},{16,24},{25,1},{1,9},{9,17},{17,25},{26,2},{2,... | collective-permute-start | bytes 129032 | tf_op jit(solution)/shard_map/ppermute | solution.py:35
  4.0 2.1 %collective-permute-start.2 = (bf16[1,168,128]{2,1,0:T(8,128)(2,1)S(1)}, bf16[1,168,128]{2,1,0:T(8,128)(2,1)S(1)}, u32[]{:S(2)}, u32[]{:S(2)}) collective-permute-start(bf16[1,168,128]{2,1,0:T(8,128)(2,1)S(1)} %pack.1.own_ref), channel_id=1, source_target_pairs={{8,0},{16,8},{24,16},{0,24},{9,1},{17,9},{25,17},{1,25},{10,2},{18... | collective-permute-start | bytes 129032 | tf_op jit(solution)/shard_map/ppermute | solution.py:35
  6.1 0.9 %collective-permute-start.4 = (bf16[1,168,128]{2,1,0:T(8,128)(2,1)S(1)}, bf16[1,168,128]{2,1,0:T(8,128)(2,1)S(1)}, u32[]{:S(2)}, u32[]{:S(2)}) collective-permute-start(bf16[1,168,128]{2,1,0:T(8,128)(2,1)S(1)} %pack.1.own_ref), channel_id=1, source_target_pairs={{16,0},{24,8},{0,16},{8,24},{17,1},{25,9},{1,17},{9,25},{18,2},{26... | collective-permute-start | bytes 129032 | tf_op jit(solution)/shard_map/ppermute | solution.py:35
  7.0 0.1 collective-permute-start
  7.1 1.0 %collective-permute-done.3 = bf16[1,168,128]{2,1,0:T(8,128)(2,1)S(1)} collective-permute-done((bf16[1,168,128]{2,1,0:T(8,128)(2,1)S(1)}, bf16[1,168,128]{2,1,0:T(8,128)(2,1)S(1)}, u32[]{:S(2)}, u32[]{:S(2)}) %collective-permute-start.3) | collective-permute-done | bytes 43040 | tf_op jit(solution)/shard_map/ppermute | solution.py:35
  8.1 0.4 %collective-permute-done.2 = bf16[1,168,128]{2,1,0:T(8,128)(2,1)S(1)} collective-permute-done((bf16[1,168,128]{2,1,0:T(8,128)(2,1)S(1)}, bf16[1,168,128]{2,1,0:T(8,128)(2,1)S(1)}, u32[]{:S(2)}, u32[]{:S(2)}) %collective-permute-start.2) | collective-permute-done | bytes 43040 | tf_op jit(solution)/shard_map/ppermute | solution.py:35
  8.5 1.6 %collective-permute-start.5 = (bf16[3,168,128]{2,1,0:T(8,128)(2,1)S(1)}, bf16[3,168,128]{2,1,0:T(8,128)(2,1)S(1)}, u32[]{:S(2)}, u32[]{:S(2)}) collective-permute-start(bf16[3,168,128]{2,1,0:T(8,128)(2,1)S(1)} %pad_maximum_fusion.refs_0_), channel_id=1, source_target_pairs={{0,1},{1,0},{2,3},{3,2},{4,5},{5,4},{6,7},{7,6},{8,9},{9,8},{10,11... | collective-permute-start | bytes 387080 | tf_op jit(solution)/shard_map/ppermute | solution.py:30
  10.1 0.8 %collective-permute-done = bf16[1,168,128]{2,1,0:T(8,128)(2,1)S(1)} collective-permute-done((bf16[1,168,128]{2,1,0:T(8,128)(2,1)S(1)}, bf16[1,168,128]{2,1,0:T(8,128)(2,1)S(1)}, u32[]{:S(2)}, u32[]{:S(2)}) %collective-permute-start) | collective-permute-done | bytes 43040 | tf_op jit(solution)/shard_map/ppermute | solution.py:30
  10.9 0.2 %collective-permute-start.1 = (bf16[2,168,128]{2,1,0:T(8,128)(2,1)S(1)}, bf16[2,168,128]{2,1,0:T(8,128)(2,1)S(1)}, u32[]{:S(2)}, u32[]{:S(2)}) collective-permute-start(bf16[2,168,128]{2,1,0:T(8,128)(2,1)S(1)} %pad_maximum_fusion.1.own), channel_id=1, source_target_pairs={{0,2},{2,0},{4,6},{6,4},{1,3},{3,1},{5,7},{7,5},{8,10},{10,8},{12,... | collective-permute-start | bytes 258056 | tf_op jit(solution)/shard_map/ppermute | solution.py:30
  11.1 0.0 collective-permute-done.4.refs_1_
  11.1 1.5 %collective-permute-start.6 = (bf16[1,168,128]{2,1,0:T(8,128)(2,1)S(1)}, bf16[1,168,128]{2,1,0:T(8,128)(2,1)S(1)}, u32[]{:S(2)}, u32[]{:S(2)}) collective-permute-start(bf16[1,168,128]{2,1,0:T(8,128)(2,1)S(1)} %collective-permute-done.4.refs_1_), channel_id=1, source_target_pairs={{0,1},{1,0},{2,3},{3,2},{4,5},{5,4},{6,7},{7,6},{8,9},{9,8},{10,11... | collective-permute-start | bytes 129032 | tf_op jit(solution)/shard_map/ppermute | solution.py:30
  12.7 2.5 %collective-permute-done.6.refs_3_ = bf16[1,168,128]{2,1,0:T(8,128)(2,1)S(1)} collective-permute-done((bf16[1,168,128]{2,1,0:T(8,128)(2,1)S(1)}, bf16[1,168,128]{2,1,0:T(8,128)(2,1)S(1)}, u32[]{:S(2)}, u32[]{:S(2)}) %collective-permute-start.6) | collective-permute-done | bytes 43040 | tf_op jit(solution)/shard_map/ppermute | solution.py:30
  15.2 0.0 collective-permute-done.1.beside
  15.2 0.0 collective-permute-done.5.refs_2_
  15.2 0.6 %firsts.1 = (bf16[1,168,128]{2,1,0:T(8,128)(2,1)S(1)}, bf16[1,168,128]{2,1,0:T(8,128)(2,1)S(1)}, bf16[4,2,144,144]{3,2,1,0:T(8,128)(2,1)S(1)}) custom-call(bf16[2,168,128]{2,1,0:T(8,128)(2,1)S(1)} %pad_maximum_fusion.1.own, bf16[2,168,128]{2,1,0:T(8,128)(2,1)S(1)} %collective-permute-done.1.beside, bf16[3,168,128]{2,1,0:T(8,128)(2,1)S(1)} %pad_maximum_fusion.refs_0_, ...), custom_call_target="tpu_custom_call" | custom-call | tf_op jit(solution)/shard_map/firsts/pallas_call | solution.py:316
  15.7 0.1 collective-permute-start.9
  15.8 1.6 %collective-permute-start.7 = (bf16[1,168,128]{2,1,0:T(8,128)(2,1)S(1)}, bf16[1,168,128]{2,1,0:T(8,128)(2,1)S(1)}, u32[]{:S(2)}, u32[]{:S(2)}) collective-permute-start(bf16[1,168,128]{2,1,0:T(8,128)(2,1)S(1)} %get-tuple-element.10), channel_id=1, source_target_pairs={{0,4},{2,6},{4,0},{6,2},{1,5},{3,7},{5,1},{7,3},{8,12},{10,14},{12... | collective-permute-start | bytes 129032 | tf_op jit(solution)/shard_map/ppermute | solution.py:30
  17.4 0.3 %collective-permute-start.8 = (bf16[2,168,128]{2,1,0:T(8,128)(2,1)S(1)}, bf16[2,168,128]{2,1,0:T(8,128)(2,1)S(1)}, u32[]{:S(2)}, u32[]{:S(2)}) collective-permute-start(bf16[2,168,128]{2,1,0:T(8,128)(2,1)S(1)} %constant_dynamic-update-slice_fusion.mine), channel_id=1, source_target_pairs={{0,2},{2,0},{4,6},{6,4},{1,3},{3,1},{5,7},{7,5},{8,10},{10,8},{12,... | collective-permute-start | bytes 258056 | tf_op jit(solution)/shard_map/ppermute | solution.py:30
  17.8 1.9 %collective-permute-done.9.panel = bf16[1,168,128]{2,1,0:T(8,128)(2,1)S(1)} collective-permute-done((bf16[1,168,128]{2,1,0:T(8,128)(2,1)S(1)}, bf16[1,168,128]{2,1,0:T(8,128)(2,1)S(1)}, u32[]{:S(2)}, u32[]{:S(2)}) %collective-permute-start.9) | collective-permute-done | bytes 43040 | tf_op jit(solution)/shard_map/ppermute | solution.py:30
  19.6 0.2 far_lasts.1.early
  19.9 0.2 %near_lasts.1 = (f32[72,144]{1,0:T(8,128)S(1)}, bf16[3,96,144]{2,1,0:T(8,128)(2,1)S(1)}) custom-call(bf16[2,168,128]{2,1,0:T(8,128)(2,1)S(1)} %constant_dynamic-update-slice_fusion.mine, bf16[2,168,128]{2,1,0:T(8,128)(2,1)S(1)} %collective-permute-done.8.other, bf16[4,2,144,144]{3,2,1,0:T(8,128)(2,1)S(1)} %get-tuple-element.11.rhs, f32[72,144]{1,0:T(8,128)S(1)} %far_lasts.1.early), custom_call_target="tpu_custom_call" | custom-call | tf_op jit(solution)/shard_map/near_lasts/pallas_call | solution.py:316
  20.1 0.2 collective-permute-done.7.panel
  20.3 0.8 %late_lasts.1 = f32[72,144]{1,0:T(8,128)} custom-call(bf16[1,168,128]{2,1,0:T(8,128)(2,1)S(1)} %collective-permute-done.7.panel, bf16[4,2,144,144]{3,2,1,0:T(8,128)(2,1)S(1)} %get-tuple-element.11.rhs, f32[72,144]{1,0:T(8,128)S(1)} %get-tuple-element.13.early, bf16[3,96,144]{2,1,0:T(8,128)(2,1)S(1)} %get-tuple-element.14.ends), custom_call_target="tpu_custom_call" | custom-call | tf_op jit(solution)/shard_map/late_lasts/pallas_call | solution.py:316
  (5 shorter events, 0.0 us)
Async XLA Ops:
  0.9 7.2 %collective-permute-start.3 = (bf16[1,168,128]{2,1,0:T(8,128)(2,1)S(1)}, bf16[1,168,128]{2,1,0:T(8,128)(2,1)S(1)}, u32[]{:S(2)}, u32[]{:S(2)}) collective-permute-start(bf16[1,168,128]{2,1,0:T(8,128)(2,1)S(1)} %pack.1.own_ref), channel_id=1, source_target_pairs={{24,0},{0,8},{8,16},{16,24},{25,1},{1,9},{9,17},{17,25},{26,2},{2,... | collective-permute-start | bytes 129032 | tf_op jit(solution)/shard_map/ppermute | solution.py:35
  4.0 4.5 %collective-permute-start.2 = (bf16[1,168,128]{2,1,0:T(8,128)(2,1)S(1)}, bf16[1,168,128]{2,1,0:T(8,128)(2,1)S(1)}, u32[]{:S(2)}, u32[]{:S(2)}) collective-permute-start(bf16[1,168,128]{2,1,0:T(8,128)(2,1)S(1)} %pack.1.own_ref), channel_id=1, source_target_pairs={{8,0},{16,8},{24,16},{0,24},{9,1},{17,9},{25,17},{1,25},{10,2},{18... | collective-permute-start | bytes 129032 | tf_op jit(solution)/shard_map/ppermute | solution.py:35
  6.1 5.1 %collective-permute-start.4 = (bf16[1,168,128]{2,1,0:T(8,128)(2,1)S(1)}, bf16[1,168,128]{2,1,0:T(8,128)(2,1)S(1)}, u32[]{:S(2)}, u32[]{:S(2)}) collective-permute-start(bf16[1,168,128]{2,1,0:T(8,128)(2,1)S(1)} %pack.1.own_ref), channel_id=1, source_target_pairs={{16,0},{24,8},{0,16},{8,24},{17,1},{25,9},{1,17},{9,25},{18,2},{26... | collective-permute-start | bytes 129032 | tf_op jit(solution)/shard_map/ppermute | solution.py:35
  7.0 3.9 %collective-permute-start = (bf16[1,168,128]{2,1,0:T(8,128)(2,1)S(1)}, bf16[1,168,128]{2,1,0:T(8,128)(2,1)S(1)}, u32[]{:S(2)}, u32[]{:S(2)}) collective-permute-start(bf16[1,168,128]{2,1,0:T(8,128)(2,1)S(1)} %pack.1.own_ref), channel_id=1, source_target_pairs={{0,6},{2,4},{4,2},{6,0},{1,7},{3,5},{5,3},{7,1},{8,14},{10,12},{12... | collective-permute-start | bytes 129032 | tf_op jit(solution)/shard_map/ppermute | solution.py:30
  8.5 6.7 %collective-permute-start.5 = (bf16[3,168,128]{2,1,0:T(8,128)(2,1)S(1)}, bf16[3,168,128]{2,1,0:T(8,128)(2,1)S(1)}, u32[]{:S(2)}, u32[]{:S(2)}) collective-permute-start(bf16[3,168,128]{2,1,0:T(8,128)(2,1)S(1)} %pad_maximum_fusion.refs_0_), channel_id=1, source_target_pairs={{0,1},{1,0},{2,3},{3,2},{4,5},{5,4},{6,7},{7,6},{8,9},{9,8},{10,11... | collective-permute-start | bytes 387080 | tf_op jit(solution)/shard_map/ppermute | solution.py:30
  10.9 4.3 %collective-permute-start.1 = (bf16[2,168,128]{2,1,0:T(8,128)(2,1)S(1)}, bf16[2,168,128]{2,1,0:T(8,128)(2,1)S(1)}, u32[]{:S(2)}, u32[]{:S(2)}) collective-permute-start(bf16[2,168,128]{2,1,0:T(8,128)(2,1)S(1)} %pad_maximum_fusion.1.own), channel_id=1, source_target_pairs={{0,2},{2,0},{4,6},{6,4},{1,3},{3,1},{5,7},{7,5},{8,10},{10,8},{12,... | collective-permute-start | bytes 258056 | tf_op jit(solution)/shard_map/ppermute | solution.py:30
  11.1 4.0 %collective-permute-start.6 = (bf16[1,168,128]{2,1,0:T(8,128)(2,1)S(1)}, bf16[1,168,128]{2,1,0:T(8,128)(2,1)S(1)}, u32[]{:S(2)}, u32[]{:S(2)}) collective-permute-start(bf16[1,168,128]{2,1,0:T(8,128)(2,1)S(1)} %collective-permute-done.4.refs_1_), channel_id=1, source_target_pairs={{0,1},{1,0},{2,3},{3,2},{4,5},{5,4},{6,7},{7,6},{8,9},{9,8},{10,11... | collective-permute-start | bytes 129032 | tf_op jit(solution)/shard_map/ppermute | solution.py:30
  15.7 3.9 %collective-permute-start.9 = (bf16[1,168,128]{2,1,0:T(8,128)(2,1)S(1)}, bf16[1,168,128]{2,1,0:T(8,128)(2,1)S(1)}, u32[]{:S(2)}, u32[]{:S(2)}) collective-permute-start(bf16[1,168,128]{2,1,0:T(8,128)(2,1)S(1)} %get-tuple-element.10), channel_id=1, source_target_pairs={{0,6},{2,4},{4,2},{6,0},{1,7},{3,5},{5,3},{7,1},{8,14},{10,12},{12... | collective-permute-start | bytes 129032 | tf_op jit(solution)/shard_map/ppermute | solution.py:30
  15.8 4.5 %collective-permute-start.7 = (bf16[1,168,128]{2,1,0:T(8,128)(2,1)S(1)}, bf16[1,168,128]{2,1,0:T(8,128)(2,1)S(1)}, u32[]{:S(2)}, u32[]{:S(2)}) collective-permute-start(bf16[1,168,128]{2,1,0:T(8,128)(2,1)S(1)} %get-tuple-element.10), channel_id=1, source_target_pairs={{0,4},{2,6},{4,0},{6,2},{1,5},{3,7},{5,1},{7,3},{8,12},{10,14},{12... | collective-permute-start | bytes 129032 | tf_op jit(solution)/shard_map/ppermute | solution.py:30
  17.4 2.4 %collective-permute-start.8 = (bf16[2,168,128]{2,1,0:T(8,128)(2,1)S(1)}, bf16[2,168,128]{2,1,0:T(8,128)(2,1)S(1)}, u32[]{:S(2)}, u32[]{:S(2)}) collective-permute-start(bf16[2,168,128]{2,1,0:T(8,128)(2,1)S(1)} %constant_dynamic-update-slice_fusion.mine), channel_id=1, source_target_pairs={{0,2},{2,0},{4,6},{6,4},{1,3},{3,1},{5,7},{7,5},{8,10},{10,8},{12,... | collective-permute-start | bytes 258056 | tf_op jit(solution)/shard_map/ppermute | solution.py:30

commit v10 on v9

--- a/solution.py
+++ b/solution.py
@@ -233,8 +233,7 @@
             natural(mine[k], rows, width, 2), natural(others[k], rows, width, 2), strict=True
         ):
             halves = [jnp.where(my_depth == 0, a, b), jnp.where(my_depth == 0, b, a)]
-            halves = [half.astype(jnp.float32) for half in halves]
-            panels.append(jnp.concatenate(halves, axis=0).astype(jnp.bfloat16))
+            panels.append(jnp.concatenate(halves, axis=0))
         for which, panel in enumerate(panels):
             rhs[row, which] = panel
         both = times(lhs[row], panels[0])

time: 21.3 us -> 21.3 us (level)
  no operation moved by 1% of the time
where the time goes in v10:
time: 21.3 us; the launch traced here: 21.1 us
  starting transfers between devices  11.5 us (54%)
  waiting for transfers between devices  6.75 us (32%)
  Pallas kernels  2.74 us (13%)
    ppermute x3, starting transfers between devices, turn(): lax.ppermute(value, axis, [((i + offset) % size, i) for i in range(size)])  6.11 us
    ppermute x7, starting transfers between devices, swap(): return lax.ppermute(value, axis, [(i, i ^ offset) for i in range(size)])  5.43 us
    ppermute x7, waiting for transfers between devices, swap(): return lax.ppermute(value, axis, [(i, i ^ offset) for i in range(size)])  5.39 us
    pallas_call x4, Pallas kernels, call(): pl.pallas_call(kernel, out_shape=out_shape, in_specs=[VMEM] * len(operand...  1.83 us
    ppermute x3, waiting for transfers between devices, turn(): lax.ppermute(value, axis, [((i + offset) % size, i) for i in range(size)])  1.36 us
    pallas_call x1, Pallas kernels, body(): pl.pallas_call(functools.partial(pack_kernel, tall_pack if fast else pack...  0.91 us
  transfers between devices with their start and end apart: 10, of which 6 were waited for; matrix products, arithmetic and copies ran while one was open for 0% of the time, Pallas kernels for 2%

profile of v10, /device:TPU:0, one launch (start us, length us, event | category | flops | bytes accessed | tf_op | source)
XLA Modules:
  0.0 21.1 jit_solution(938907270344866597)
XLA Ops:
  0.0 0.9 %pack.1.own_ref = bf16[1,168,128]{2,1,0:T(8,128)(2,1)S(1)} custom-call(bf16[72,144]{1,0:T(8,128)(2,1)} %x_hbm.1, bf16[72,144]{1,0:T(8,128)(2,1)} %t_hbm.1, s32[5,5]{1,0:T(8,128)} %fill_x_hbm.1, s32[5,5]{1,0:T(8,128)} %fill_t_hbm.1), custom_call_target="tpu_custom_call" | custom-call | tf_op jit(solution)/shard_map/pack/pallas_call | solution.py:405
  0.9 3.1 %collective-permute-start.3 = (bf16[1,168,128]{2,1,0:T(8,128)(2,1)S(1)}, bf16[1,168,128]{2,1,0:T(8,128)(2,1)S(1)}, u32[]{:S(2)}, u32[]{:S(2)}) collective-permute-start(bf16[1,168,128]{2,1,0:T(8,128)(2,1)S(1)} %pack.1.own_ref), channel_id=1, source_target_pairs={{24,0},{0,8},{8,16},{16,24},{25,1},{1,9},{9,17},{17,25},{26,2},{2,... | collective-permute-start | bytes 129032 | tf_op jit(solution)/shard_map/ppermute | solution.py:35
  4.0 2.1 %collective-permute-start.2 = (bf16[1,168,128]{2,1,0:T(8,128)(2,1)S(1)}, bf16[1,168,128]{2,1,0:T(8,128)(2,1)S(1)}, u32[]{:S(2)}, u32[]{:S(2)}) collective-permute-start(bf16[1,168,128]{2,1,0:T(8,128)(2,1)S(1)} %pack.1.own_ref), channel_id=1, source_target_pairs={{8,0},{16,8},{24,16},{0,24},{9,1},{17,9},{25,17},{1,25},{10,2},{18... | collective-permute-start | bytes 129032 | tf_op jit(solution)/shard_map/ppermute | solution.py:35
  6.1 0.9 %collective-permute-start.4 = (bf16[1,168,128]{2,1,0:T(8,128)(2,1)S(1)}, bf16[1,168,128]{2,1,0:T(8,128)(2,1)S(1)}, u32[]{:S(2)}, u32[]{:S(2)}) collective-permute-start(bf16[1,168,128]{2,1,0:T(8,128)(2,1)S(1)} %pack.1.own_ref), channel_id=1, source_target_pairs={{16,0},{24,8},{0,16},{8,24},{17,1},{25,9},{1,17},{9,25},{18,2},{26... | collective-permute-start | bytes 129032 | tf_op jit(solution)/shard_map/ppermute | solution.py:35
  7.0 0.1 collective-permute-start
  7.1 1.0 %collective-permute-done.3 = bf16[1,168,128]{2,1,0:T(8,128)(2,1)S(1)} collective-permute-done((bf16[1,168,128]{2,1,0:T(8,128)(2,1)S(1)}, bf16[1,168,128]{2,1,0:T(8,128)(2,1)S(1)}, u32[]{:S(2)}, u32[]{:S(2)}) %collective-permute-start.3) | collective-permute-done | bytes 43040 | tf_op jit(solution)/shard_map/ppermute | solution.py:35
  8.1 0.4 %collective-permute-done.2 = bf16[1,168,128]{2,1,0:T(8,128)(2,1)S(1)} collective-permute-done((bf16[1,168,128]{2,1,0:T(8,128)(2,1)S(1)}, bf16[1,168,128]{2,1,0:T(8,128)(2,1)S(1)}, u32[]{:S(2)}, u32[]{:S(2)}) %collective-permute-start.2) | collective-permute-done | bytes 43040 | tf_op jit(solution)/shard_map/ppermute | solution.py:35
  8.5 1.6 %collective-permute-start.5 = (bf16[3,168,128]{2,1,0:T(8,128)(2,1)S(1)}, bf16[3,168,128]{2,1,0:T(8,128)(2,1)S(1)}, u32[]{:S(2)}, u32[]{:S(2)}) collective-permute-start(bf16[3,168,128]{2,1,0:T(8,128)(2,1)S(1)} %pad_maximum_fusion.refs_0_), channel_id=1, source_target_pairs={{0,1},{1,0},{2,3},{3,2},{4,5},{5,4},{6,7},{7,6},{8,9},{9,8},{10,11... | collective-permute-start | bytes 387080 | tf_op jit(solution)/shard_map/ppermute | solution.py:30
  10.1 0.8 %collective-permute-done = bf16[1,168,128]{2,1,0:T(8,128)(2,1)S(1)} collective-permute-done((bf16[1,168,128]{2,1,0:T(8,128)(2,1)S(1)}, bf16[1,168,128]{2,1,0:T(8,128)(2,1)S(1)}, u32[]{:S(2)}, u32[]{:S(2)}) %collective-permute-start) | collective-permute-done | bytes 43040 | tf_op jit(solution)/shard_map/ppermute | solution.py:30
  10.9 0.2 %collective-permute-start.1 = (bf16[2,168,128]{2,1,0:T(8,128)(2,1)S(1)}, bf16[2,168,128]{2,1,0:T(8,128)(2,1)S(1)}, u32[]{:S(2)}, u32[]{:S(2)}) collective-permute-start(bf16[2,168,128]{2,1,0:T(8,128)(2,1)S(1)} %pad_maximum_fusion.1.own), channel_id=1, source_target_pairs={{0,2},{2,0},{4,6},{6,4},{1,3},{3,1},{5,7},{7,5},{8,10},{10,8},{12,... | collective-permute-start | bytes 258056 | tf_op jit(solution)/shard_map/ppermute | solution.py:30
  11.1 0.0 collective-permute-done.4.refs_1_
  11.1 1.5 %collective-permute-start.6 = (bf16[1,168,128]{2,1,0:T(8,128)(2,1)S(1)}, bf16[1,168,128]{2,1,0:T(8,128)(2,1)S(1)}, u32[]{:S(2)}, u32[]{:S(2)}) collective-permute-start(bf16[1,168,128]{2,1,0:T(8,128)(2,1)S(1)} %collective-permute-done.4.refs_1_), channel_id=1, source_target_pairs={{0,1},{1,0},{2,3},{3,2},{4,5},{5,4},{6,7},{7,6},{8,9},{9,8},{10,11... | collective-permute-start | bytes 129032 | tf_op jit(solution)/shard_map/ppermute | solution.py:30
  12.7 2.5 %collective-permute-done.6.refs_3_ = bf16[1,168,128]{2,1,0:T(8,128)(2,1)S(1)} collective-permute-done((bf16[1,168,128]{2,1,0:T(8,128)(2,1)S(1)}, bf16[1,168,128]{2,1,0:T(8,128)(2,1)S(1)}, u32[]{:S(2)}, u32[]{:S(2)}) %collective-permute-start.6) | collective-permute-done | bytes 43040 | tf_op jit(solution)/shard_map/ppermute | solution.py:30
  15.2 0.0 collective-permute-done.1.beside
  15.2 0.0 collective-permute-done.5.refs_2_
  15.2 0.6 %firsts.1 = (bf16[1,168,128]{2,1,0:T(8,128)(2,1)S(1)}, bf16[1,168,128]{2,1,0:T(8,128)(2,1)S(1)}, bf16[4,2,144,144]{3,2,1,0:T(8,128)(2,1)S(1)}) custom-call(bf16[2,168,128]{2,1,0:T(8,128)(2,1)S(1)} %pad_maximum_fusion.1.own, bf16[2,168,128]{2,1,0:T(8,128)(2,1)S(1)} %collective-permute-done.1.beside, bf16[3,168,128]{2,1,0:T(8,128)(2,1)S(1)} %pad_maximum_fusion.refs_0_, ...), custom_call_target="tpu_custom_call" | custom-call | tf_op jit(solution)/shard_map/firsts/pallas_call | solution.py:315
  15.7 0.1 collective-permute-start.9
  15.8 1.6 %collective-permute-start.7 = (bf16[1,168,128]{2,1,0:T(8,128)(2,1)S(1)}, bf16[1,168,128]{2,1,0:T(8,128)(2,1)S(1)}, u32[]{:S(2)}, u32[]{:S(2)}) collective-permute-start(bf16[1,168,128]{2,1,0:T(8,128)(2,1)S(1)} %get-tuple-element.10), channel_id=1, source_target_pairs={{0,4},{2,6},{4,0},{6,2},{1,5},{3,7},{5,1},{7,3},{8,12},{10,14},{12... | collective-permute-start | bytes 129032 | tf_op jit(solution)/shard_map/ppermute | solution.py:30
  17.4 0.3 %collective-permute-start.8 = (bf16[2,168,128]{2,1,0:T(8,128)(2,1)S(1)}, bf16[2,168,128]{2,1,0:T(8,128)(2,1)S(1)}, u32[]{:S(2)}, u32[]{:S(2)}) collective-permute-start(bf16[2,168,128]{2,1,0:T(8,128)(2,1)S(1)} %constant_dynamic-update-slice_fusion.mine), channel_id=1, source_target_pairs={{0,2},{2,0},{4,6},{6,4},{1,3},{3,1},{5,7},{7,5},{8,10},{10,8},{12,... | collective-permute-start | bytes 258056 | tf_op jit(solution)/shard_map/ppermute | solution.py:30
  17.8 1.9 %collective-permute-done.9.panel = bf16[1,168,128]{2,1,0:T(8,128)(2,1)S(1)} collective-permute-done((bf16[1,168,128]{2,1,0:T(8,128)(2,1)S(1)}, bf16[1,168,128]{2,1,0:T(8,128)(2,1)S(1)}, u32[]{:S(2)}, u32[]{:S(2)}) %collective-permute-start.9) | collective-permute-done | bytes 43040 | tf_op jit(solution)/shard_map/ppermute | solution.py:30
  19.7 0.2 far_lasts.1.early
  19.9 0.2 %near_lasts.1 = (f32[72,144]{1,0:T(8,128)S(1)}, bf16[3,96,144]{2,1,0:T(8,128)(2,1)S(1)}) custom-call(bf16[2,168,128]{2,1,0:T(8,128)(2,1)S(1)} %constant_dynamic-update-slice_fusion.mine, bf16[2,168,128]{2,1,0:T(8,128)(2,1)S(1)} %collective-permute-done.8.other, bf16[4,2,144,144]{3,2,1,0:T(8,128)(2,1)S(1)} %get-tuple-element.11.rhs, f32[72,144]{1,0:T(8,128)S(1)} %far_lasts.1.early), custom_call_target="tpu_custom_call" | custom-call | tf_op jit(solution)/shard_map/near_lasts/pallas_call | solution.py:315
  20.1 0.2 collective-permute-done.7.panel
  20.3 0.8 %late_lasts.1 = f32[72,144]{1,0:T(8,128)} custom-call(bf16[1,168,128]{2,1,0:T(8,128)(2,1)S(1)} %collective-permute-done.7.panel, bf16[4,2,144,144]{3,2,1,0:T(8,128)(2,1)S(1)} %get-tuple-element.11.rhs, f32[72,144]{1,0:T(8,128)S(1)} %get-tuple-element.13.early, bf16[3,96,144]{2,1,0:T(8,128)(2,1)S(1)} %get-tuple-element.14.ends), custom_call_target="tpu_custom_call" | custom-call | tf_op jit(solution)/shard_map/late_lasts/pallas_call | solution.py:315
  (5 shorter events, 0.0 us)
Async XLA Ops:
  0.9 7.2 %collective-permute-start.3 = (bf16[1,168,128]{2,1,0:T(8,128)(2,1)S(1)}, bf16[1,168,128]{2,1,0:T(8,128)(2,1)S(1)}, u32[]{:S(2)}, u32[]{:S(2)}) collective-permute-start(bf16[1,168,128]{2,1,0:T(8,128)(2,1)S(1)} %pack.1.own_ref), channel_id=1, source_target_pairs={{24,0},{0,8},{8,16},{16,24},{25,1},{1,9},{9,17},{17,25},{26,2},{2,... | collective-permute-start | bytes 129032 | tf_op jit(solution)/shard_map/ppermute | solution.py:35
  4.0 4.5 %collective-permute-start.2 = (bf16[1,168,128]{2,1,0:T(8,128)(2,1)S(1)}, bf16[1,168,128]{2,1,0:T(8,128)(2,1)S(1)}, u32[]{:S(2)}, u32[]{:S(2)}) collective-permute-start(bf16[1,168,128]{2,1,0:T(8,128)(2,1)S(1)} %pack.1.own_ref), channel_id=1, source_target_pairs={{8,0},{16,8},{24,16},{0,24},{9,1},{17,9},{25,17},{1,25},{10,2},{18... | collective-permute-start | bytes 129032 | tf_op jit(solution)/shard_map/ppermute | solution.py:35
  6.1 5.1 %collective-permute-start.4 = (bf16[1,168,128]{2,1,0:T(8,128)(2,1)S(1)}, bf16[1,168,128]{2,1,0:T(8,128)(2,1)S(1)}, u32[]{:S(2)}, u32[]{:S(2)}) collective-permute-start(bf16[1,168,128]{2,1,0:T(8,128)(2,1)S(1)} %pack.1.own_ref), channel_id=1, source_target_pairs={{16,0},{24,8},{0,16},{8,24},{17,1},{25,9},{1,17},{9,25},{18,2},{26... | collective-permute-start | bytes 129032 | tf_op jit(solution)/shard_map/ppermute | solution.py:35
  7.0 3.9 %collective-permute-start = (bf16[1,168,128]{2,1,0:T(8,128)(2,1)S(1)}, bf16[1,168,128]{2,1,0:T(8,128)(2,1)S(1)}, u32[]{:S(2)}, u32[]{:S(2)}) collective-permute-start(bf16[1,168,128]{2,1,0:T(8,128)(2,1)S(1)} %pack.1.own_ref), channel_id=1, source_target_pairs={{0,6},{2,4},{4,2},{6,0},{1,7},{3,5},{5,3},{7,1},{8,14},{10,12},{12... | collective-permute-start | bytes 129032 | tf_op jit(solution)/shard_map/ppermute | solution.py:30
  8.5 6.7 %collective-permute-start.5 = (bf16[3,168,128]{2,1,0:T(8,128)(2,1)S(1)}, bf16[3,168,128]{2,1,0:T(8,128)(2,1)S(1)}, u32[]{:S(2)}, u32[]{:S(2)}) collective-permute-start(bf16[3,168,128]{2,1,0:T(8,128)(2,1)S(1)} %pad_maximum_fusion.refs_0_), channel_id=1, source_target_pairs={{0,1},{1,0},{2,3},{3,2},{4,5},{5,4},{6,7},{7,6},{8,9},{9,8},{10,11... | collective-permute-start | bytes 387080 | tf_op jit(solution)/shard_map/ppermute | solution.py:30
  10.9 4.3 %collective-permute-start.1 = (bf16[2,168,128]{2,1,0:T(8,128)(2,1)S(1)}, bf16[2,168,128]{2,1,0:T(8,128)(2,1)S(1)}, u32[]{:S(2)}, u32[]{:S(2)}) collective-permute-start(bf16[2,168,128]{2,1,0:T(8,128)(2,1)S(1)} %pad_maximum_fusion.1.own), channel_id=1, source_target_pairs={{0,2},{2,0},{4,6},{6,4},{1,3},{3,1},{5,7},{7,5},{8,10},{10,8},{12,... | collective-permute-start | bytes 258056 | tf_op jit(solution)/shard_map/ppermute | solution.py:30
  11.1 4.0 %collective-permute-start.6 = (bf16[1,168,128]{2,1,0:T(8,128)(2,1)S(1)}, bf16[1,168,128]{2,1,0:T(8,128)(2,1)S(1)}, u32[]{:S(2)}, u32[]{:S(2)}) collective-permute-start(bf16[1,168,128]{2,1,0:T(8,128)(2,1)S(1)} %collective-permute-done.4.refs_1_), channel_id=1, source_target_pairs={{0,1},{1,0},{2,3},{3,2},{4,5},{5,4},{6,7},{7,6},{8,9},{9,8},{10,11... | collective-permute-start | bytes 129032 | tf_op jit(solution)/shard_map/ppermute | solution.py:30
  15.7 3.9 %collective-permute-start.9 = (bf16[1,168,128]{2,1,0:T(8,128)(2,1)S(1)}, bf16[1,168,128]{2,1,0:T(8,128)(2,1)S(1)}, u32[]{:S(2)}, u32[]{:S(2)}) collective-permute-start(bf16[1,168,128]{2,1,0:T(8,128)(2,1)S(1)} %get-tuple-element.10), channel_id=1, source_target_pairs={{0,6},{2,4},{4,2},{6,0},{1,7},{3,5},{5,3},{7,1},{8,14},{10,12},{12... | collective-permute-start | bytes 129032 | tf_op jit(solution)/shard_map/ppermute | solution.py:30
  15.8 4.5 %collective-permute-start.7 = (bf16[1,168,128]{2,1,0:T(8,128)(2,1)S(1)}, bf16[1,168,128]{2,1,0:T(8,128)(2,1)S(1)}, u32[]{:S(2)}, u32[]{:S(2)}) collective-permute-start(bf16[1,168,128]{2,1,0:T(8,128)(2,1)S(1)} %get-tuple-element.10), channel_id=1, source_target_pairs={{0,4},{2,6},{4,0},{6,2},{1,5},{3,7},{5,1},{7,3},{8,12},{10,14},{12... | collective-permute-start | bytes 129032 | tf_op jit(solution)/shard_map/ppermute | solution.py:30
  17.4 2.4 %collective-permute-start.8 = (bf16[2,168,128]{2,1,0:T(8,128)(2,1)S(1)}, bf16[2,168,128]{2,1,0:T(8,128)(2,1)S(1)}, u32[]{:S(2)}, u32[]{:S(2)}) collective-permute-start(bf16[2,168,128]{2,1,0:T(8,128)(2,1)S(1)} %constant_dynamic-update-slice_fusion.mine), channel_id=1, source_target_pairs={{0,2},{2,0},{4,6},{6,4},{1,3},{3,1},{5,7},{7,5},{8,10},{10,8},{12,... | collective-permute-start | bytes 258056 | tf_op jit(solution)/shard_map/ppermute | solution.py:30
